TPU v7x, 32 devices: a whole 2x2x4 slice. The times are simulated.
32 devices in a mesh: section: 2 (over x), dp: 16 (over z, y, core).
Axes of the slice: x: 2, y: 2, z: 4, core: 2. Of those that a mesh axis runs over, the one named last changes fastest.
Arguments:
- inputs: bfloat16 [2, 2048, 768], P(None, 'dp'), may hold values from -6 to 6
- segments: int32 [2, 2048], P(None, 'dp'), may hold values from 0 to 47, never falling along the last dimension, each value on 1 to 64 neighbouring positions
- cotangent: bfloat16 [2, 2048, 768], P(None, 'dp'), may hold values from -6 to 6
- norm_gain: bfloat16 [2, 768], P('section', 'dp'), may hold values from 0.099609375 to 1.8984375
- w_main: bfloat16 [2, 768, 3328], P('section', 'dp'), may hold values from -0.21875 to 0.21875
- w_dt: bfloat16 [2, 768, 24], P('section', 'dp'), may hold values from -0.21875 to 0.21875
- conv_weight: bfloat16 [2, 4, 1792], P('section', None, 'dp'), may hold values from -3 to 3
- conv_bias: bfloat16 [2, 1792], P('section', 'dp'), may hold values from -3 to 3
- dt_bias: float32 [2, 24], P('section'), may hold values from -4 to -1
- a_log: float32 [2, 24], P('section'), may hold values from -3 to 0
- skip_d: float32 [2, 24], P('section'), may hold values from 0.5 to 2
- gate_gain: bfloat16 [2, 1536], P('section', 'dp'), may hold values from 0.099609375 to 1.8984375
- w_out: bfloat16 [2, 1536, 768], P('section', 'dp'), may hold values from -0.15625 to 0.15625
Outputs:
- hidden: bfloat16 [2, 2, 2048, 768], P('section', None, 'dp')
- grad_inputs: float32 [2, 2, 2048, 768], P('section', None, 'dp')
- grad_norm_gain: float32 [2, 768], P('section', 'dp')
- grad_w_main: float32 [2, 768, 3328], P('section', 'dp')
- grad_w_dt: float32 [2, 768, 24], P('section', 'dp')
- grad_conv_weight: float32 [2, 4, 1792], P('section', None, 'dp')
- grad_conv_bias: float32 [2, 1792], P('section', 'dp')
- grad_dt_bias: float32 [2, 24], P('section')
- grad_a_log: float32 [2, 24], P('section')
- grad_skip_d: float32 [2, 24], P('section')
- grad_gate_gain: float32 [2, 1536], P('section', 'dp')
- grad_w_out: float32 [2, 1536, 768], P('section', 'dp')
Inputs may be any that keep to these rules, and one draw needn't show every extreme that they name: `segments`: segment numbers never fall along a micro-batch's tokens; each segment spans 1 to 64 tokens, and one spans exactly that many.
All inputs are finite; a program needn't handle non-finite values.
Results may differ from a plain program's by a relative error of at most 0.011.
Values may be sent and summed in bfloat16 or wider, within the bound.
No kernel may reach another device: no remote copies, remote signals or barrier semaphores. Data moves between devices by JAX's collectives and lax.ppermute only.
A program may use at most 128 MiB of HBM per device.

v0:
```python
import functools

import jax
import jax.numpy as jnp
from jax import lax
from jax.experimental import pallas as pl
from jax.experimental.pallas import tpu as pltpu
from jax.sharding import PartitionSpec as P

norm_eps = 1e-05
F32 = jnp.float32
BF16 = jnp.bfloat16
LANES = 128
TAPS = 4
VMEM_BYTES = 28 * 1024 * 1024


def dot_nn(a, b):
    return lax.dot_general(a, b, (((1,), (0,)), ((), ())), preferred_element_type=F32)


def dot_nt(a, b):
    return lax.dot_general(a, b, (((1,), (1,)), ((), ())), preferred_element_type=F32)


def dot_tn(a, b):
    return lax.dot_general(a, b, (((0,), (0,)), ((), ())), preferred_element_type=F32)


def split(a):
    high = a.astype(BF16)
    return high, (a - high.astype(F32)).astype(BF16)


def exact(dot, a, b):
    ah, al = split(a)
    bh, bl = split(b)
    return dot(ah, bh) + (dot(ah, bl) + dot(al, bh))


def near(dot, a, b):
    return exact(dot, a, b)


def triangle(lower):
    rows = lax.broadcasted_iota(jnp.int32, (LANES, LANES), 0)
    cols = lax.broadcasted_iota(jnp.int32, (LANES, LANES), 1)
    return jnp.where(rows >= cols if lower else rows <= cols, 1.0, 0.0).astype(BF16)


def running(tri, a):
    high = a.astype(BF16)
    rest = a - high.astype(F32)
    mid = rest.astype(BF16)
    low = (rest - mid.astype(F32)).astype(BF16)
    return dot_nn(tri, high) + (dot_nn(tri, mid) + dot_nn(tri, low))


def sigmoid(a):
    return 0.5 * jnp.tanh(0.5 * a) + 0.5


def softplus(a):
    return jnp.maximum(a, 0.0) + jnp.log1p(jnp.exp(-jnp.abs(a)))


def cols(j, width=LANES):
    return slice(j * width, (j + 1) * width)


def token_masks(ids):
    length = ids.shape[1]
    across = jnp.broadcast_to(ids, (length, length))
    wide = across.T
    rows = lax.broadcasted_iota(jnp.int32, (length, length), 0)
    lane = lax.broadcasted_iota(jnp.int32, (length, length), 1)
    linked = jnp.where((rows >= lane) & (wide == across), 1.0, 0.0)
    sees = [None]
    for k in range(1, TAPS):
        sees.append(jnp.where((rows >= k) & (pltpu.roll(wide, k, 0) == wide), 1.0, 0.0))
    return linked, sees


def take(which_ref, choices, into, sems):
    def start(choice):
        for i, ((ref, index), target) in enumerate(zip(choice, into)):
            pltpu.make_async_copy(ref if index is None else ref.at[index], target, sems.at[i]).start()

    if len(choices) == 1:
        start(choices[0])
        return
    for number, choice in enumerate(choices):
        pl.when(which_ref[0] == number)(functools.partial(start, choice))


def taken(into, sems, *numbers):
    for i in numbers:
        pltpu.make_async_copy(into[i], into[i], sems.at[i]).wait()


def conv_taps(v, sees):
    return [v] + [sees[k] * pltpu.roll(v, k, 0) for k in range(1, TAPS)]


def conv_sum(taps, cw_ref, cb_ref, at):
    total = cb_ref[:, at] + cw_ref[TAPS - 1 : TAPS, at] * taps[0]
    for k in range(1, TAPS):
        total = total + cw_ref[TAPS - 1 - k : TAPS - k, at] * taps[k]
    return total


def pair_of(values, j):
    lane = lax.broadcasted_iota(jnp.int32, (values.shape[0], LANES), 1)
    first = jnp.broadcast_to(values[:, 2 * j : 2 * j + 1], lane.shape)
    second = jnp.broadcast_to(values[:, 2 * j + 1 : 2 * j + 2], lane.shape)
    return jnp.where(lane < LANES // 2, first, second)


def halves(values):
    lane = lax.broadcasted_iota(jnp.int32, values.shape, 1)
    low = jnp.where(lane < LANES // 2, values, 0.0)
    return jnp.concatenate([low, values - low], axis=0)


def decay(cum, cum_t, linked, h):
    spread = cum[:, h : h + 1] - cum_t[h : h + 1, :]
    return linked * jnp.exp(jnp.minimum(spread, 0.0))


def micro_of(which_ref, mode):
    return (0, 1, which_ref[0], 1 - which_ref[0])[mode]


def held(which_ref, options, indices):
    refs = [ref if index is None else ref.at[index] for ref, index in zip(options, indices)]

    def read(at=slice(None)):
        values = [ref[:, at] for ref in refs]
        return values[0] if len(values) == 1 else jnp.where(which_ref[0] == 0, values[0], values[1])

    return read


KEPT = 8


def fwd_kernel(plan, mode, which_ref, ids_ref, wm_ref, wo_ref, gin_ref, cw_ref, cb_ref, gg_ref, hp_ref, sk_ref, *refs):
    sources, refs = refs[: len(plan)], refs[len(plan) :]
    v_ref, n_ref, p_ref, dtr_ref, y_ref, mix_ref, total_ref, g_ref, r2_ref = refs
    inner, width = gg_ref.shape[1], p_ref.shape[1]
    pairs = inner // LANES
    linked, sees = token_masks(ids_ref[micro_of(which_ref, mode)])
    u = held(which_ref, sources, plan)().astype(F32)
    r = lax.rsqrt(jnp.mean(u * u, axis=-1, keepdims=True) + norm_eps)
    n = (u * r * gin_ref[...]).astype(BF16)
    n_ref[...] = n
    for c in range(width // 256):
        p_ref[:, cols(c, 256)] = dot_nn(n, wm_ref[:, cols(c, 256)])
    dtr = dot_nn(n, wm_ref[:, width:])
    dtr_ref[...] = dtr

    def conv(j):
        total = conv_sum(conv_taps(p_ref[:, inner + j * LANES : inner + (j + 1) * LANES], sees), cw_ref, cb_ref, cols(j))
        total_ref[:, cols(j)] = total
        return total * sigmoid(total)

    b_state = conv(pairs)
    c_state = conv(pairs + 1)
    cross = exact(dot_nt, c_state, b_state)
    dt = softplus(dtr + hp_ref[0:1, :])
    cum = running(triangle(True), -dt * jnp.exp(hp_ref[1:2, :]))
    cum_t = cum.T
    squares = jnp.zeros((u.shape[0], LANES), F32)
    for j in range(pairs):
        at = cols(j)
        x = conv(j)
        m = jnp.concatenate([cross * decay(cum, cum_t, linked, 2 * j), cross * decay(cum, cum_t, linked, 2 * j + 1)], axis=1)
        y = near(dot_nn, m, halves(x * pair_of(dt, j))) + sk_ref[:, at] * x
        y_ref[:, at] = y
        z = p_ref[:, at]
        g = y * (z * sigmoid(z))
        g_ref[:, at] = g
        squares = squares + g * g
    r2 = lax.rsqrt(jnp.sum(squares, axis=-1, keepdims=True) / inner + norm_eps)
    for j in range(pairs):
        at = cols(j)
        mix_ref[:, at] = (g_ref[:, at] * r2 * gg_ref[:, at]).astype(BF16)
    r2_ref[...] = jnp.broadcast_to(r2, r2_ref.shape)
    mixed = mix_ref[...]
    for c in range(u.shape[1] // 256):
        at = cols(c, 256)
        v_ref[:, at] = (u[:, at] + dot_nn(mixed, wo_ref[:, at])).astype(BF16)


def bwd_kernel(plan, mode, which_ref, ids_ref, wm_ref, wo_ref, gin_ref, cw_ref, cb_ref, gg_ref, hp_ref, sk_ref, *refs):
    count = KEPT * len(plan)
    sources, refs = refs[:count], refs[count:]
    gi_ref, gl_ref, gp_ref, gdt_ref, dch_ref, din_ref, dgin_ref, dhp_ref, gm_scr = refs
    gv, u_low, p, dtr, y_kept, totals, g_kept, r2_kept = [
        held(which_ref, [sources[KEPT * k + i] for k in range(len(plan))], [indices[i] for indices in plan]) for i in range(KEPT)
    ]
    dch_ref[...] = jnp.zeros(dch_ref.shape, F32)
    din_ref[...] = jnp.zeros(din_ref.shape, F32)
    inner = gg_ref.shape[1]
    pairs = inner // LANES
    length = gm_scr.shape[0]
    linked, sees = token_masks(ids_ref[micro_of(which_ref, mode)])
    gb = gv()
    inners = jnp.zeros((length, 256), F32)
    for c in range(inner // 256):
        at = cols(c, 256)
        gm = dot_nt(gb, wo_ref[at, :])
        gm_scr[:, at] = gm
        inners = inners + gm * gg_ref[:, at] * g_kept(at)
    r2 = r2_kept()[:, 0:1]
    pull = r2 * r2 * r2 * (jnp.sum(inners, axis=-1, keepdims=True) / inner)

    def conv(j):
        total = totals(cols(j))
        return total, sigmoid(total)

    def conv_back(j, total, sig, grad):
        at = cols(j)
        v = p(slice(inner + j * LANES, inner + (j + 1) * LANES))
        ds = grad * (sig * (1.0 + total * (1.0 - sig)))
        dch_ref[TAPS : TAPS + 1, at] = jnp.sum(ds, axis=0, keepdims=True)
        dch_ref[TAPS - 1 : TAPS, at] = jnp.sum(ds * v, axis=0, keepdims=True)
        dv = cw_ref[TAPS - 1 : TAPS, at] * ds
        for k in range(1, TAPS):
            row = slice(TAPS - 1 - k, TAPS - k)
            moved = pltpu.roll(sees[k] * ds, length - k, 0)
            dch_ref[row, at] = jnp.sum(moved * v, axis=0, keepdims=True)
            dv = dv + cw_ref[row, at] * moved
        gp_ref[:, inner + j * LANES : inner + (j + 1) * LANES] = dv.astype(BF16)

    sb, gb_sig = conv(pairs)
    b_state = sb * gb_sig
    sc, gc_sig = conv(pairs + 1)
    c_state = sc * gc_sig
    cross = exact(dot_nt, c_state, b_state)
    dt_arg = dtr() + hp_ref[0:1, :]
    dt = softplus(dt_arg)
    rate = jnp.exp(hp_ref[1:2, :])
    cum = running(triangle(True), -dt * rate)
    cum_t = cum.T
    dcross = jnp.zeros((length, length), F32)
    dcum = jnp.zeros((length, LANES), F32)
    ddt = jnp.zeros((length, LANES), F32)
    dskip = jnp.zeros((8, LANES), F32)
    lane = lax.broadcasted_iota(jnp.int32, (2 * LANES, LANES), 1)
    row = lax.broadcasted_iota(jnp.int32, (2 * LANES, LANES), 0)
    half = jnp.where((row % LANES) < LANES // 2, 0, 1)
    for j in range(pairs):
        at = cols(j)
        pick = jnp.where(lane == 2 * j + half, 1.0, 0.0).astype(BF16)
        gm = gm_scr[:, at]
        g = g_kept(at)
        din_ref[0:1, at] = jnp.sum(gm * (g * r2), axis=0, keepdims=True)
        dg = gm * gg_ref[:, at] * r2 - g * pull
        z = p(at)
        sig = sigmoid(z)
        y = y_kept(at)
        dy = dg * (z * sig)
        gp_ref[:, at] = (dg * y * (sig * (1.0 + z * (1.0 - sig)))).astype(BF16)
        total, tsig = conv(j)
        x = total * tsig
        dtp = pair_of(dt, j)
        xw = x * dtp
        dy_st = halves(dy)
        l1 = decay(cum, cum_t, linked, 2 * j)
        l2 = decay(cum, cum_t, linked, 2 * j + 1)
        dm = near(dot_nt, dy_st, xw)
        dcross = dcross + dm[:length] * l1 + dm[length:] * l2
        m = jnp.concatenate([cross * l1, cross * l2], axis=0)
        dxw = near(dot_tn, m, dy_st)
        skip = sk_ref[:, at]
        lanes = jnp.broadcast_to(jnp.sum(dy * x, axis=0, keepdims=True), (8, LANES))
        dskip = dskip + dot_nn(jnp.concatenate(split(lanes), axis=1), pick)
        q = dy * (y - skip * x) - dxw * xw
        dcum = dcum + dot_nn(jnp.concatenate(split(q), axis=1), pick)
        ddt = ddt + dot_nn(jnp.concatenate(split(dxw * x), axis=1), pick)
        conv_back(j, total, tsig, skip * dy + dxw * dtp)
    conv_back(pairs, sb, gb_sig, exact(dot_tn, dcross, c_state))
    conv_back(pairs + 1, sc, gc_sig, exact(dot_nn, dcross, b_state))
    dlog = running(triangle(False), dcum)
    draw = (ddt - rate * dlog) * sigmoid(dt_arg)
    gdt = draw.astype(BF16)
    gdt_ref[...] = gdt
    dhp_ref[0:1, :] = jnp.sum(draw, axis=0, keepdims=True)
    dhp_ref[1:2, :] = jnp.sum(dlog * (-dt * rate), axis=0, keepdims=True)
    dhp_ref[2:3, :] = dskip[0:1]
    dhp_ref[3:8, :] = jnp.zeros((5, LANES), F32)
    u = u_low().astype(F32)
    gin = gin_ref[...]
    r = lax.rsqrt(jnp.mean(u * u, axis=-1, keepdims=True) + norm_eps)
    gp = gp_ref[...]
    width = gp.shape[1]
    gn = jnp.concatenate(
        [dot_nt(gp, wm_ref[cols(c, 256), :width]) + dot_nt(gdt, wm_ref[cols(c, 256), width:]) for c in range(u.shape[1] // 256)], axis=1
    )
    dgin_ref[...] = jnp.broadcast_to(jnp.sum(gn * (u * r), axis=0, keepdims=True), dgin_ref.shape)
    gng = gn * gin
    back = r * r * r * jnp.mean(gng * u, axis=-1, keepdims=True)
    grad = gb.astype(F32) + (gng * r - u * back)
    gi_ref[...] = grad
    gl_ref[...] = grad.astype(BF16)


def shape_of(shape, dtype=F32):
    return jax.ShapeDtypeStruct(shape, dtype)


VMEM_SPEC = pl.BlockSpec(memory_space=pltpu.VMEM)
HBM_SPEC = pl.BlockSpec(memory_space=pltpu.HBM)
SMEM_SPEC = pl.BlockSpec(memory_space=pltpu.SMEM)
PARAMS = pltpu.CompilerParams(vmem_limit_bytes=VMEM_BYTES)


def layer_sizes(weights):
    return weights[0].shape[0], weights[1].shape[0], weights[0].shape[1] - LANES


def forward_layer(mode, which, ids, weights, choices):
    tok = ids.shape[2]
    feat, inner, width = layer_sizes(weights)
    return pl.pallas_call(
        functools.partial(fwd_kernel, tuple(index for _, index in choices), mode),
        in_specs=[SMEM_SPEC] + [VMEM_SPEC] * (9 + len(choices)),
        out_specs=[VMEM_SPEC] * 9,
        out_shape=(
            shape_of((tok, feat), BF16),
            shape_of((tok, feat), BF16),
            shape_of((tok, width)),
            shape_of((tok, LANES)),
            shape_of((tok, inner)),
            shape_of((tok, inner), BF16),
            shape_of((tok, width - inner)),
            shape_of((tok, inner)),
            shape_of((tok, LANES)),
        ),
        compiler_params=PARAMS,
        name="layer_forward",
    )(which, ids, *weights, *[source for source, _ in choices])


def backward_layer(mode, which, ids, weights, choices):
    tok = ids.shape[2]
    feat, inner, width = layer_sizes(weights)
    return pl.pallas_call(
        functools.partial(bwd_kernel, tuple(tuple(index for _, index in choice) for choice in choices), mode),
        in_specs=[SMEM_SPEC] + [VMEM_SPEC] * (9 + KEPT * len(choices)),
        out_specs=[VMEM_SPEC] * 8,
        out_shape=(
            shape_of((tok, feat)),
            shape_of((tok, feat), BF16),
            shape_of((tok, width), BF16),
            shape_of((tok, LANES), BF16),
            shape_of((8, width - inner)),
            shape_of((8, inner)),
            shape_of((8, feat)),
            shape_of((8, LANES)),
        ),
        scratch_shapes=[pltpu.VMEM((tok, inner), F32)],
        compiler_params=PARAMS,
        name="layer_backward",
    )(which, ids, *weights, *[source for choice in choices for source, _ in choice])


def lay(blocks, size, chunks):
    lane = lax.broadcasted_iota(jnp.int32, (8, LANES), 1)
    out = [jnp.zeros((8, LANES), F32) for _ in range(chunks)]
    for i, block in enumerate(blocks):
        chunk, shift = (i * size) // LANES, (i * size) % LANES
        turned = pltpu.roll(block, shift, 1) if shift else block
        out[chunk] = jnp.where((lane >= shift) & (lane < shift + size), turned, out[chunk])
        if shift + size > LANES:
            out[chunk + 1] = jnp.where(lane < shift + size - LANES, turned, out[chunk + 1])
    return out


def cut(chunks, size, i):
    lane = lax.broadcasted_iota(jnp.int32, (8, LANES), 1)
    chunk, shift = (i * size) // LANES, (i * size) % LANES
    turn = (LANES - shift) % LANES
    block = pltpu.roll(chunks[chunk], turn, 1) if turn else chunks[chunk]
    if shift + size > LANES:
        block = jnp.where(lane < LANES - shift, block, pltpu.roll(chunks[chunk + 1], turn, 1))
    return jnp.where(lane < size, block, 0.0)


def pack_kernel(wm_ref, wo_ref, wdt_ref, cw_ref, cb_ref, gg_ref, ng_ref, out_ref, line, square):
    rows, width = wm_ref.shape
    feat = wo_ref.shape[1]
    blocks = wo_ref.shape[0] // rows
    out_ref[:, :width] = wm_ref[...]
    for b in range(blocks):
        out_ref[:, width + b * feat : width + (b + 1) * feat] = wo_ref[b * rows : (b + 1) * rows, :]
    last = width + blocks * feat
    out_ref[:, last + LANES :] = jnp.zeros((rows, LANES), BF16)
    square[...] = jnp.zeros(square.shape, F32)
    square[: wdt_ref.shape[0], :rows] = wdt_ref[...].astype(F32)
    out_ref[:, last : last + LANES] = square[...].T[:rows].astype(BF16)
    line[...] = jnp.zeros(line.shape, F32)
    line[0:TAPS, : cw_ref.shape[1]] = cw_ref[...].astype(F32)
    for k, ref in enumerate((cb_ref, gg_ref, ng_ref)):
        line[TAPS + k : TAPS + k + 1, : ref.shape[1]] = ref[...].astype(F32)
    out_ref[0:16, last + LANES :] = line[...].astype(BF16)


def pack_shard(wm, wo, wdt, cw, cb, gg, ng):
    rows, width = wm.shape
    full = width + wo.shape[0] // rows * wo.shape[1] + 2 * LANES
    return pl.pallas_call(
        pack_kernel,
        out_shape=shape_of((rows, full), BF16),
        scratch_shapes=[pltpu.VMEM((16, LANES), F32), pltpu.VMEM((LANES, LANES), F32)],
        compiler_params=pltpu.CompilerParams(vmem_limit_bytes=2 * VMEM_BYTES),
        name="pack_shard",
    )(wm, wo, wdt, cw, cb, gg, ng)


Z_CHIPS = 4


def spot(z, y, c):
    return (z * 2 + y) * 2 + c


def routed(value, move):
    pairs = []
    for z in range(Z_CHIPS):
        for y in range(2):
            for c in range(2):
                target = move(z, y, c)
                if target is not None:
                    pairs.append((spot(z, y, c), spot(*target)))
    return lax.ppermute(value, "dp", pairs)


def to_core(z, y, c):
    return z, y, 1 - c


def to_y(z, y, c):
    return z, 1 - y, c


def to_near(z, y, c):
    return z ^ 1, y, c


def to_middle(z, y, c):
    return (3 - z, y, c) if z in (1, 2) else None


def to_ends(z, y, c):
    return (z ^ 1, y, c) if z in (1, 2) else None


def from_ends(z, y, c):
    return (z ^ 1, y, c) if z in (0, 3) else None


def slot_places(z):
    return (z, z + 1 - 2 * lax.rem(z, 2), jnp.where(z < 2, 2, 1), jnp.where(z < 2, 3, 0))


def behind(value, other):
    return lax.optimization_barrier((value, other))[0]


def gather_slots(own):
    def pair(block, across):
        return jnp.concatenate([across, block], axis=0)

    near, second, own_y = lax.optimization_barrier((routed(own, to_near), routed(own, to_middle), routed(own, to_y)))
    own_pair = pair(own, own_y)
    last, ends, near_y = lax.optimization_barrier((routed(near, to_middle), routed(second, to_ends), routed(near, to_y)))
    second = second + ends
    near_pair = pair(near, near_y)
    own_core = routed(behind(own_pair, ends), to_core)
    ends, second_y = lax.optimization_barrier((routed(last, to_ends), routed(second, to_y)))
    last = last + ends
    second_pair = pair(second, second_y)
    near_core = routed(behind(near_pair, ends), to_core)
    second_core = routed(second_pair, to_core)
    last_pair = pair(last, routed(last, to_y))
    return [own_pair, near_pair, second_pair, last_pair, own_core, near_core, second_core, routed(last_pair, to_core)]


def scatter_slots(first_pair, rest, vectors):
    rows = first_pair[0].shape[0] // 2

    def met(kept, value):
        total = kept.astype(F32) + value.astype(F32)
        return total[:rows].astype(BF16), total[rows:]

    def low(value):
        return value.astype(BF16)

    def summed(step):
        return vectors + lax.ppermute(vectors, "dp", [(i, i ^ step) for i in range(4 * Z_CHIPS)])

    far, last = met(first_pair[0], routed(first_pair[1], to_core))
    kept, sent = rest(far)
    vectors = behind(vectors, far)
    vectors = summed(1)
    came = routed(far, to_y)
    over = [routed(block, to_core) for block in sent]
    far, second = met(kept[2], over[2])
    came, vectors = lax.optimization_barrier((came, vectors))
    came, last = routed(behind(far, came), to_y), last + came.astype(F32)
    line = routed(low(last), from_ends)
    vectors = summed(2)
    far, near = met(kept[1], over[1])
    came, line, vectors = lax.optimization_barrier((came, line, vectors))
    last, second = last + line.astype(F32), second + came.astype(F32)
    came, line, ends = routed(behind(far, came), to_y), routed(low(last), to_middle), routed(low(second), from_ends)
    vectors = summed(4)
    far, own = met(kept[0], over[0])
    came, line, ends, vectors = lax.optimization_barrier((came, line, ends, vectors))
    near, second = near + came.astype(F32) + line.astype(F32), second + ends.astype(F32)
    started = came
    came = routed(behind(far, came), to_y)
    near, second = routed(low(near), to_near), routed(low(second), to_middle)
    vectors = summed(8)
    return (own + came.astype(F32), second, near), vectors, started


def owners_of(where_ref):
    z, y, c = where_ref[1], where_ref[2], where_ref[3]
    return [(spot(at, 1 - y, core), spot(at, y, core)) for core in (c, 1 - c) for at in slot_places(z)]


def settle_kernel(chans, where_ref, *refs):
    pairs, (wm_ref, wo_ref, cw_ref, cb_ref, gg_ref, gin_ref, line_ref, sem) = refs[:8], refs[8:]
    rows = pairs[0].shape[0] // 2
    feat = wo_ref.shape[1]
    width = wm_ref.shape[1] - LANES
    inner = wo_ref.shape[0]
    last = width + inner
    copies = []
    for pair, owners in zip(pairs, owners_of(where_ref)):
        for half, owner in enumerate(owners):
            mine = pl.ds(half * rows, rows)
            to = pl.ds(pl.multiple_of(owner * rows, 16), rows)
            copies.append((pair.at[pl.ds(half * rows, 16), pl.ds(last + LANES, LANES)], line_ref.at[owner]))
            copies.append((pair.at[mine, pl.ds(0, width)], wm_ref.at[to, pl.ds(0, width)]))
            copies.append((pair.at[mine, pl.ds(last, LANES)], wm_ref.at[to, pl.ds(width, LANES)]))
            for b in range(inner // wm_ref.shape[0]):
                into = pl.ds(pl.multiple_of((owner * (inner // wm_ref.shape[0]) + b) * rows, 16), rows)
                copies.append((pair.at[mine, pl.ds(width + b * feat, feat)], wo_ref.at[into]))
    for source, target in copies:
        pltpu.make_async_copy(source, target, sem).start()
    for whole in (wm_ref, wo_ref, line_ref):
        pltpu.make_async_copy(whole, whole, sem).wait()
    lines = [line_ref[i].astype(F32)[0:8] for i in range(line_ref.shape[0])]
    for c, chunk in enumerate(lay(lines, chans, cw_ref.shape[1] // LANES)):
        cw_ref[:, cols(c)] = chunk[0:TAPS]
        cb_ref[:, cols(c)] = chunk[TAPS : TAPS + 1]
    for c, chunk in enumerate(lay(lines, inner // len(lines), gg_ref.shape[1] // LANES)):
        gg_ref[:, cols(c)] = chunk[TAPS + 1 : TAPS + 2]
    for c, chunk in enumerate(lay(lines, rows, gin_ref.shape[1] // LANES)):
        gin_ref[:, cols(c)] = chunk[TAPS + 2 : TAPS + 3]


def settle(where, pairs, width, chans, feat):
    rows, full = pairs[0].shape[0] // 2, pairs[0].shape[1]
    owners, inner = feat // rows, full - width - 2 * LANES
    return pl.pallas_call(
        functools.partial(settle_kernel, chans),
        in_specs=[SMEM_SPEC] + [HBM_SPEC] * 8,
        out_specs=[VMEM_SPEC] * 6,
        out_shape=(
            shape_of((feat, width + LANES), BF16),
            shape_of((inner, feat), BF16),
            shape_of((TAPS, owners * chans)),
            shape_of((1, owners * chans)),
            shape_of((1, inner)),
            shape_of((1, feat)),
        ),
        scratch_shapes=[pltpu.VMEM((owners, 16, LANES), BF16), pltpu.SemaphoreType.DMA],
        compiler_params=PARAMS,
        name="settle_weights",
    )(where, *pairs)


def slot_blocks(where_ref):
    owners = owners_of(where_ref)
    return [owner for slot in range(4) for pair in (owners[slot], owners[4 + slot]) for owner in pair]


def write_slot(slot, turned, mixed, gp_ref, gb_ref, gdt_ref, line_ref, kept_ref, sent_ref, where_ref):
    rows, width, feat = kept_ref.shape[0] // 2, gp_ref.shape[1], gb_ref.shape[1]
    blocks = mixed.shape[0] // turned.shape[0]
    last = width + blocks * feat
    mine = turned[4 * slot * rows : 4 * (slot + 1) * rows, :]

    def put(at, term):
        kept_ref[:, at] = term[: 2 * rows].astype(BF16)
        sent_ref[:, at] = term[2 * rows :].astype(BF16)

    for c in range(width // 256):
        put(cols(c, 256), dot_nn(mine, gp_ref[:, cols(c, 256)]))
    put(slice(last, last + LANES), dot_nn(mine, gdt_ref[...]))
    owners = slot_blocks(where_ref)[4 * slot : 4 * slot + 4]
    for part, owner in enumerate(owners):
        ref, to = (kept_ref, sent_ref)[part // 2], part % 2 * rows
        for b in range(blocks):
            start = ((4 * slot + part) * blocks + b) * rows
            at = slice(width + b * feat, width + (b + 1) * feat)
            ref[to : to + rows, at] = dot_nn(mixed[start : start + rows, :], gb_ref[...]).astype(BF16)
        line = line_ref[owner]
        ref[to : to + 16, last + LANES :] = jnp.concatenate([line, jnp.zeros_like(line)], axis=0).astype(BF16)
        ref[to + 16 : to + rows, last + LANES :] = jnp.zeros((rows - 16, LANES), BF16)


def first_weight_kernel(rows, chans, where_ref, *refs):
    sources, smalls, outs, scratch = refs[:20], refs[20:32], refs[32:41], refs[41:]
    kept_ref, sent_ref, vec_ref, turned_ref, mixed_ref, gp_ref, gb_ref, gdt_ref, line_ref = outs
    n_ref, mix_ref, flat_ref, wide_ref, sems = scratch
    tok, feat, inner = sources[0].shape[0], n_ref.shape[1], mix_ref.shape[1]
    blocks = inner // feat
    into = [ref.at[part * tok : (part + 1) * tok] for part in range(2) for ref in (n_ref, mix_ref, gp_ref, gb_ref, gdt_ref)]
    take(where_ref, [[(source, None) for source in sources[10 * i : 10 * i + 10]] for i in range(2)], into, sems)
    early = jnp.where(where_ref[0] == 0, 0.0, 1.0)
    sums = [one[...] + early * zero[...] + (1.0 - early) * two[...] for zero, one, two in zip(smalls[0::3], smalls[1::3], smalls[2::3])]
    vec_ref[...] = sums[3]
    pieces = [[total[:, cols(c)] for c in range(total.shape[1] // LANES)] for total in sums]
    row = lax.broadcasted_iota(jnp.int32, (8, LANES), 0)
    for i in range(feat // rows):
        block = cut(pieces[0], chans, i)
        block = jnp.where(row == TAPS + 1, jnp.broadcast_to(cut(pieces[1], blocks * rows, i)[0:1], block.shape), block)
        line_ref[i] = jnp.where(row == TAPS + 2, jnp.broadcast_to(cut(pieces[2], rows, i)[0:1], block.shape), block)
    owners = slot_blocks(where_ref)
    taken(into, sems, 0, 5)
    flat_ref[...] = n_ref[...].T
    for i, owner in enumerate(owners):
        turned_ref[i * rows : (i + 1) * rows, :] = flat_ref[pl.ds(pl.multiple_of(owner * rows, 16), rows), :]
    taken(into, sems, 1, 6)
    wide_ref[...] = mix_ref[...].T
    many = blocks * rows
    for i, owner in enumerate(owners):
        mixed_ref[i * many : (i + 1) * many, :] = wide_ref[pl.ds(pl.multiple_of(owner * many, 16), many), :]
    taken(into, sems, 2, 7, 3, 8, 4, 9)
    write_slot(3, turned_ref, mixed_ref, gp_ref, gb_ref, gdt_ref, line_ref, kept_ref, sent_ref, where_ref)


def rest_weight_kernel(where_ref, turned_ref, mixed_ref, gp_ref, gb_ref, gdt_ref, line_ref, *outs):
    for slot in (2, 1, 0):
        write_slot(slot, turned_ref, mixed_ref, gp_ref, gb_ref, gdt_ref, line_ref, outs[slot], outs[3 + slot], where_ref)


def weight_terms(where, one, other, smalls, rows, chans):
    tok, feat = one[0].shape
    inner, width = one[1].shape[1], one[2].shape[1]
    pair = shape_of((2 * rows, width + inner + 2 * LANES), BF16)
    shared = (
        shape_of((feat, 2 * tok), BF16),
        shape_of((inner, 2 * tok), BF16),
        shape_of((2 * tok, width), BF16),
        shape_of((2 * tok, feat), BF16),
        shape_of((2 * tok, LANES), BF16),
        shape_of((feat // rows, 8, LANES)),
    )
    kept, sent, vectors, *common = pl.pallas_call(
        functools.partial(first_weight_kernel, rows, chans),
        in_specs=[SMEM_SPEC] + [HBM_SPEC] * 20 + [VMEM_SPEC] * 12,
        out_specs=[VMEM_SPEC] * 9,
        out_shape=(pair, pair, shape_of((8, LANES))) + shared,
        scratch_shapes=[
            pltpu.VMEM((2 * tok, feat), BF16),
            pltpu.VMEM((2 * tok, inner), BF16),
            pltpu.VMEM((feat, 2 * tok), BF16),
            pltpu.VMEM((inner, 2 * tok), BF16),
            pltpu.SemaphoreType.DMA((10,)),
        ],
        compiler_params=PARAMS,
        name="weight_gradients_first",
    )(where, *one, *other, *smalls)

    def rest(after):
        outs = pl.pallas_call(
            rest_weight_kernel,
            in_specs=[SMEM_SPEC] + [VMEM_SPEC] * 6,
            out_specs=[VMEM_SPEC] * 6,
            out_shape=(pair,) * 6,
            compiler_params=PARAMS,
            name="weight_gradients_rest",
        )(where, behind(common[0], after), *common[1:])
        return outs[:3], outs[3:]

    return (kept, sent), vectors, rest


def unpack_kernel(own_ref, second_ref, near_ref, wm_ref, wo_ref, wdt_ref, cw_ref, cb_ref, gg_ref, ng_ref, square):
    rows, width = wm_ref.shape
    feat = wo_ref.shape[1]
    blocks = wo_ref.shape[0] // rows
    last = width + blocks * feat

    def total(at, count):
        some = slice(0, count)
        return own_ref[some, at] + (second_ref[some, at].astype(F32) + near_ref[some, at].astype(F32))

    for c in range(width // 256):
        wm_ref[:, cols(c, 256)] = total(cols(c, 256), rows)
    for b in range(blocks):
        wo_ref[b * rows : (b + 1) * rows, :] = total(slice(width + b * feat, width + (b + 1) * feat), rows)
    square[...] = jnp.zeros(square.shape, F32)
    square[:rows, :] = total(slice(last, last + LANES), rows)
    wdt_ref[...] = square[...].T[: wdt_ref.shape[0], :rows]
    line = total(slice(last + LANES, last + 2 * LANES), 16)
    cw_ref[...] = line[0:TAPS, : cw_ref.shape[1]]
    for k, ref in enumerate((cb_ref, gg_ref, ng_ref)):
        ref[...] = line[TAPS + k : TAPS + k + 1, : ref.shape[1]]


def unpack_sums(terms, wm, wo, wdt, cw, cb, gg, ng):
    return pl.pallas_call(
        unpack_kernel,
        out_shape=tuple(shape_of(part.shape) for part in (wm, wo, wdt, cw, cb, gg, ng)),
        scratch_shapes=[pltpu.VMEM((LANES, LANES), F32)],
        compiler_params=PARAMS,
        name="unpack_sums",
    )(*terms)


def small_rows(vectors, rows):
    flat = jnp.concatenate([vector.reshape(-1) for vector in vectors])
    lines = -(-flat.shape[0] // LANES)
    wide = -(-lines // rows)
    flat = jnp.pad(flat, (0, lines * LANES - flat.shape[0])).reshape(lines, LANES)
    flat = jnp.pad(flat, ((0, rows * wide - lines), (0, 0)))
    return flat.reshape(wide, rows, LANES).transpose(1, 0, 2).reshape(rows, wide * LANES)


def small_flat(block, owners):
    rows, wide = block.shape[0] // owners, block.shape[1] // LANES
    return block.reshape(owners, rows, wide, LANES).transpose(0, 2, 1, 3).reshape(owners, wide * rows * LANES)


def total_over(value, axis):
    count = lax.axis_size(axis)
    step = 1
    while step < count:
        value = value + lax.ppermute(value, axis, [(i, i ^ step) for i in range(count)])
        step = step * 2
    return value


def shards(inputs, segments, cotangent, norm_gain, w_main, w_dt, conv_weight, conv_bias, dt_bias, a_log, skip_d, gate_gain, w_out):
    first = lax.axis_index("section") == 0
    dp = lax.axis_size("dp")
    feat = inputs.shape[2]
    rows, width = w_main.shape[1:]
    heads = w_dt.shape[2]
    chans, own_inner = conv_weight.shape[2], gate_gain.shape[1]
    inner = own_inner * dp
    blocks = own_inner // rows

    owned = (w_main[0], w_out[0], jnp.swapaxes(w_dt[0], 0, 1), conv_weight[0], conv_bias, gate_gain, norm_gain)
    aligned = rows % 16 == 0 and dp == 4 * Z_CHIPS
    side = lax.axis_index("section")
    place = lax.axis_index("dp")
    where = jnp.stack([side, place // 4, place // 2 % 2, place % 2]).astype(jnp.int32)
    if aligned:
        wm, wo, cw, cb, gg, gin = settle(where, gather_slots(pack_shard(*owned)), width, chans, feat)
    else:
        small = small_rows((conv_weight[0], conv_bias[0], gate_gain[0], norm_gain[0]), rows)
        out_block = w_out[0].reshape(blocks, rows, feat).transpose(1, 0, 2).reshape(rows, inner)
        packed = jnp.concatenate([w_main[0], out_block, jnp.pad(w_dt[0], ((0, 0), (0, LANES - heads))), small], axis=1)
        whole = lax.all_gather(packed, "dp", axis=0, tiled=True)
    marks = [TAPS * chans, (TAPS + 1) * chans, (TAPS + 1) * chans + own_inner, (TAPS + 1) * chans + own_inner + rows]
    if not aligned:
        wm = jnp.concatenate([whole[:, :width], whole[:, width + inner : width + inner + LANES]], axis=1)
        wo = whole[:, width : width + inner].reshape(dp, rows, blocks, feat).transpose(0, 2, 1, 3).reshape(inner, feat)
        flat = small_flat(whole[:, width + inner + LANES :], dp).astype(F32)
        cw = flat[:, : marks[0]].reshape(dp, TAPS, chans).transpose(1, 0, 2).reshape(TAPS, dp * chans)
        cb = flat[:, marks[0] : marks[1]].reshape(1, dp * chans)
        gg = flat[:, marks[1] : marks[2]].reshape(1, inner)
        gin = flat[:, marks[2] : marks[3]].reshape(1, feat)
    hp = jnp.pad(jnp.concatenate([dt_bias, a_log], axis=0), ((0, 6), (0, LANES - heads)))
    sk = jnp.repeat(skip_d, inner // heads, axis=1)
    weights = (wm, wo, gin, cw, cb, gg, hp, sk)

    def choose(one, other):
        return jnp.where(first, one, other)

    up = down = [(0, 1), (1, 0)]
    ids = segments.astype(F32)[:, None, :]
    f0 = forward_layer(0, where, ids, weights, [(inputs, 0)])
    r0 = lax.ppermute(f0[0], "section", up)
    f1 = forward_layer(3, where, ids, weights, [(inputs, 1), (r0, None)])
    r1 = lax.ppermute(f1[0], "section", up)
    f2 = forward_layer(1, where, ids, weights, [(inputs, 1), (r1, None)])

    def stored(tick):
        return [(tick[i], None) for i in (2, 3, 4, 6, 7, 8)]

    kept = stored(f1)
    now = [[(cotangent, 0), (inputs, 1)] + kept, [(cotangent, 0), (r0, None)] + kept]
    b0 = backward_layer(0, where, ids, weights, now)
    d0 = lax.ppermute(b0[1], "section", down)
    now = [
        [(d0, None), (inputs, 0)] + stored(f0),
        [(cotangent, 1), (r1, None)] + stored(f2),
    ]
    b1 = backward_layer(2, where, ids, weights, now)
    d1 = lax.ppermute(b1[1], "section", down)
    b2 = backward_layer(1, where, ids, weights, [[(d1, None), (inputs, 1)] + kept])
    dch, din, dgin, dhp = tuple(choose(two, zero) + one for zero, one, two in zip(b0[4:], b1[4:], b2[4:]))
    on_first = (f0[1], f0[5], b1[2], d0, b1[3]), (f1[1], f1[5], b2[2], d1, b2[3])
    on_last = (f2[1], f2[5], b1[2], cotangent[1], b1[3]), (f1[1], f1[5], b0[2], cotangent[0], b0[3])
    if aligned:
        smalls = [part[i] for i in (4, 5, 6, 7) for part in (b0, b1, b2)]
        first_pair, vectors, rest = weight_terms(where, on_first[0] + on_first[1], on_last[0] + on_last[1], smalls, rows, chans)
    else:
        n, mix, gp, gb, gdt = tuple(
            jnp.concatenate([choose(on_first[0][i], on_last[0][i]), choose(on_first[1][i], on_last[1][i])], axis=0) for i in range(5)
        )
        own = [
            small_rows(
                (
                    dch[:TAPS, i * chans : (i + 1) * chans],
                    dch[TAPS, i * chans : (i + 1) * chans],
                    din[0, i * own_inner : (i + 1) * own_inner],
                    dgin[0, i * rows : (i + 1) * rows],
                ),
                rows,
            )
            for i in range(dp)
        ]
        wide = dot_tn(mix, gb).reshape(dp, blocks, rows, feat).transpose(0, 2, 1, 3).reshape(feat, inner)
        parts = [dot_tn(n, gp), wide, dot_tn(n, gdt), jnp.concatenate(own, axis=0)]
        packed_grad = jnp.concatenate([part.astype(BF16) for part in parts], axis=1)
    if aligned:
        terms, vectors, started = scatter_slots(first_pair, rest, vectors)
        heads_sum = vectors[:, :heads]
    else:
        summed = lax.psum_scatter(packed_grad, "dp", scatter_dimension=0, tiled=True)
        heads_sum = total_over(dhp[:3, :heads], "dp")
        started = summed
    if aligned:
        g_main, g_out, g_dt, g_cw, g_cb, g_gg, g_ng = unpack_sums(terms, *owned)
        g_dt = jnp.swapaxes(g_dt, 0, 1)
    else:
        summed = summed.astype(F32)
        got = small_flat(summed[:, width + inner + LANES :], 1)[0]
        g_main = summed[:, :width]
        g_out = summed[:, width : width + inner].reshape(rows, blocks, feat).transpose(1, 0, 2).reshape(own_inner, feat)
        g_dt = summed[:, width + inner : width + inner + heads]
        g_cw = got[: marks[0]].reshape(TAPS, chans)
        g_cb, g_gg, g_ng = (got[None, marks[i] : marks[i + 1]] for i in range(3))
    outs = [part[0] for part in (f0, f1, f2, b0, b1, b2)]
    outs = lax.optimization_barrier((*outs, started))
    hidden = jnp.stack([choose(outs[0], outs[1]), choose(outs[1], outs[2])])[None]
    grad_inputs = jnp.stack([choose(outs[4], outs[3]), choose(outs[5], outs[4])])[None]
    return (
        hidden,
        grad_inputs,
        g_ng,
        g_main[None],
        g_dt[None],
        g_cw[None],
        g_cb,
        heads_sum[0:1],
        heads_sum[1:2],
        heads_sum[2:3],
        g_gg,
        g_out[None],
    )


def solution(mesh):
    placed = (
        P(None, "dp", None),
        P(None, "dp"),
        P(None, "dp", None),
        P("section", "dp"),
        P("section", "dp", None),
        P("section", "dp", None),
        P("section", None, "dp"),
        P("section", "dp"),
        P("section", None),
        P("section", None),
        P("section", None),
        P("section", "dp"),
        P("section", "dp", None),
    )
    return jax.shard_map(
        shards,
        mesh=mesh,
        in_specs=placed,
        out_specs=(
            P("section", None, "dp", None),
            P("section", None, "dp", None),
            P("section", "dp"),
            P("section", "dp", None),
            P("section", "dp", None),
            P("section", None, "dp"),
            P("section", "dp"),
            P("section", None),
            P("section", None),
            P("section", None),
            P("section", "dp"),
            P("section", "dp", None),
        ),
        check_vma=False,
    )
```

profile of v0, /device:TPU:8, one launch (start us, length us, event | category | flops | bytes accessed | tf_op | source)
XLA Modules:
  0.0 192.8 jit_solution(8296606279255504683)
XLA Ops:
  0.6 2.0 %pack_shard.1 = bf16[48,5120]{1,0:T(8,128)(2,1)} custom-call(bf16[48,3328]{1,0:T(8,128)(2,1)} %bitcast.40, bf16[96,768]{1,0:T(8,128)(2,1)} %bitcast.41, bf16[24,48]{1,0:T(8,128)(2,1)} %bitcast.42, bf16[4,112]{1,0:T(4,128)(2,1)} %bitcast.43, bf16[1,112]{1,0:T(2,128)(2,1)} %cb_ref.1, bf16[1,96]{1,0:T(2,128)(2,1)} %gg_ref.1, bf16[1,48]{1,0:T(2,128)(2,1)} %ng_ref.1), custom_call_target="tpu_custom_call" | custom-call | tf_op jit(solution)/shard_map/pack_shard/pallas_call | solution.py:413
  2.6 5.0 %collective-permute-start.1 = (bf16[48,5120]{1,0:T(8,128)(2,1)}, bf16[48,5120]{1,0:T(8,128)(2,1)S(1)}, u32[]{:S(2)}, u32[]{:S(2)}) collective-permute-start(bf16[48,5120]{1,0:T(8,128)(2,1)} %pack_shard.1), channel_id=1, source_target_pairs={{4,8},{5,9},{6,10},{7,11},{8,4},{9,5},{10,6},{11,7},{20,24},{21,25... | collective-permute-start | bytes 1474568 | tf_op jit(solution)/shard_map/ppermute | solution.py:437
  7.7 1.6 collective-permute-start.2
  9.2 6.5 %collective-permute-done = bf16[48,5120]{1,0:T(8,128)(2,1)S(1)} collective-permute-done((bf16[48,5120]{1,0:T(8,128)(2,1)}, bf16[48,5120]{1,0:T(8,128)(2,1)S(1)}, u32[]{:S(2)}, u32[]{:S(2)}) %collective-permute-start) | collective-permute-done | bytes 491552 | tf_op jit(solution)/shard_map/ppermute | solution.py:437
  15.8 3.0 %collective-permute-done.1 = bf16[48,5120]{1,0:T(8,128)(2,1)S(1)} collective-permute-done((bf16[48,5120]{1,0:T(8,128)(2,1)}, bf16[48,5120]{1,0:T(8,128)(2,1)S(1)}, u32[]{:S(2)}, u32[]{:S(2)}) %collective-permute-start.1) | collective-permute-done | bytes 491552 | tf_op jit(solution)/shard_map/ppermute | solution.py:437
  18.8 1.5 collective-permute-done.2
  20.3 2.2 %collective-permute-start.3 = (bf16[48,5120]{1,0:T(8,128)(2,1)S(1)}, bf16[48,5120]{1,0:T(8,128)(2,1)S(1)}, u32[]{:S(2)}, u32[]{:S(2)}) collective-permute-start(bf16[48,5120]{1,0:T(8,128)(2,1)S(1)} %collective-permute-done), channel_id=1, source_target_pairs={{4,8},{5,9},{6,10},{7,11},{8,4},{9,5},{10,6},{11,7},{20,24},{21,25... | collective-permute-start | bytes 1474568 | tf_op jit(solution)/shard_map/ppermute | solution.py:437
  22.5 1.6 collective-permute-start.5
  24.1 1.3 collective-permute-start.4
  25.4 1.1 pad_maximum_fusion.refs_0_
  26.5 7.2 %collective-permute-done.3 = bf16[48,5120]{1,0:T(8,128)(2,1)S(1)} collective-permute-done((bf16[48,5120]{1,0:T(8,128)(2,1)S(1)}, bf16[48,5120]{1,0:T(8,128)(2,1)S(1)}, u32[]{:S(2)}, u32[]{:S(2)}) %collective-permute-start.3) | collective-permute-done | bytes 491552 | tf_op jit(solution)/shard_map/ppermute | solution.py:437
  34.5 1.3 collective-permute-start.7
  35.8 3.7 %collective-permute-start.6 = (bf16[48,5120]{1,0:T(8,128)(2,1)S(1)}, bf16[48,5120]{1,0:T(8,128)(2,1)S(1)}, u32[]{:S(2)}, u32[]{:S(2)}) collective-permute-start(bf16[48,5120]{1,0:T(8,128)(2,1)S(1)} %collective-permute-done.3), channel_id=1, source_target_pairs={{4,0},{5,1},{6,2},{7,3},{8,12},{9,13},{10,14},{11,15},{20,16},{21,... | collective-permute-start | bytes 1474568 | tf_op jit(solution)/shard_map/ppermute | solution.py:437
  39.5 0.8 constant_dynamic-update-slice_fusion.1
  40.3 0.8 constant_dynamic-update-slice_fusion.refs_1_
  41.2 4.0 %collective-permute-done.7 = bf16[48,5120]{1,0:T(8,128)(2,1)S(1)} collective-permute-done((bf16[48,5120]{1,0:T(8,128)(2,1)S(1)}, bf16[48,5120]{1,0:T(8,128)(2,1)S(1)}, u32[]{:S(2)}, u32[]{:S(2)}) %collective-permute-start.7) | collective-permute-done | bytes 491552 | tf_op jit(solution)/shard_map/ppermute | solution.py:437
  45.2 2.1 %collective-permute-done.6 = bf16[48,5120]{1,0:T(8,128)(2,1)S(1)} collective-permute-done((bf16[48,5120]{1,0:T(8,128)(2,1)S(1)}, bf16[48,5120]{1,0:T(8,128)(2,1)S(1)}, u32[]{:S(2)}, u32[]{:S(2)}) %collective-permute-start.6) | collective-permute-done | bytes 491552 | tf_op jit(solution)/shard_map/ppermute | solution.py:437
  47.4 1.6 collective-permute-start.8
  49.7 7.2 %collective-permute-done.8 = bf16[48,5120]{1,0:T(8,128)(2,1)S(1)} collective-permute-done((bf16[48,5120]{1,0:T(8,128)(2,1)S(1)}, bf16[48,5120]{1,0:T(8,128)(2,1)S(1)}, u32[]{:S(2)}, u32[]{:S(2)}) %collective-permute-start.8) | collective-permute-done | bytes 491552 | tf_op jit(solution)/shard_map/ppermute | solution.py:437
  57.4 2.3 %collective-permute-done.12.refs_7_ = bf16[96,5120]{1,0:T(8,128)(2,1)} collective-permute-done((bf16[96,5120]{1,0:T(8,128)(2,1)S(1)}, bf16[96,5120]{1,0:T(8,128)(2,1)}, u32[]{:S(2)}, u32[]{:S(2)}) %collective-permute-start.12) | collective-permute-done | bytes 983072 | tf_op jit(solution)/shard_map/ppermute | solution.py:437
  59.7 3.5 %settle_weights.1 = (bf16[768,3456]{1,0:T(8,128)(2,1)S(1)}, bf16[1536,768]{1,0:T(8,128)(2,1)S(1)}, f32[4,1792]{1,0:T(4,128)S(1)}, f32[1,1792]{1,0:T(1,128)S(1)},...) custom-call(s32[4]{0:T(128)S(1)} %pad_add_fusion.where_ref.which_ref, bf16[96,5120]{1,0:T(8,128)(2,1)S(1)} %pad_maximum_fusion.refs_0_, ...), custom_call_target="tpu_custom_call" | custom-call | tf_op jit(solution)/shard_map/settle_weights/pallas_call | solution.py:570
  63.2 4.5 %layer_forward.3 = (bf16[128,768]{1,0:T(8,128)(2,1)S(1)}, bf16[128,768]{1,0:T(8,128)(2,1)S(1)}, f32[128,3328]{1,0:T(8,128)S(1)}, f32[128,128]{1,0:T(8,128)S(1)},...) custom-call(s32[4]{0:T(128)S(1)} %pad_add_fusion.where_ref.which_ref, ...), custom_call_target="tpu_custom_call" | custom-call | tf_op jit(solution)/shard_map/layer_forward/pallas_call | solution.py:326
  67.7 1.6 collective-permute-start.13
  69.3 5.5 %collective-permute-done.13.refs_1_.refs_9_ = bf16[128,768]{1,0:T(8,128)(2,1)S(1)} collective-permute-done((bf16[128,768]{1,0:T(8,128)(2,1)S(1)}, bf16[128,768]{1,0:T(8,128)(2,1)S(1)}, u32[]{:S(2)}, u32[]{:S(2)}) %collective-permute-start.13) | collective-permute-done | bytes 196640 | tf_op jit(solution)/shard_map/ppermute | solution.py:793
  74.7 4.5 %layer_forward.4 = (bf16[128,768]{1,0:T(8,128)(2,1)S(1)}, bf16[128,768]{1,0:T(8,128)(2,1)S(1)}, f32[128,3328]{1,0:T(8,128)S(1)}, f32[128,128]{1,0:T(8,128)S(1)},...) custom-call(s32[4]{0:T(128)S(1)} %pad_add_fusion.where_ref.which_ref, ...), custom_call_target="tpu_custom_call" | custom-call | tf_op jit(solution)/shard_map/layer_forward/pallas_call | solution.py:326
  79.2 1.6 collective-permute-start.14
  80.8 9.0 %layer_backward.3 = (f32[128,768]{1,0:T(8,128)S(1)}, bf16[128,768]{1,0:T(8,128)(2,1)S(1)}, bf16[128,3328]{1,0:T(8,128)(2,1)S(1)}, bf16[128,128]{1,0:T(8,128)(2,1...) custom-call(s32[4]{0:T(128)S(1)} %pad_add_fusion.where_ref.which_ref, ...), custom_call_target="tpu_custom_call" | custom-call | tf_op jit(solution)/shard_map/layer_backward/pallas_call | solution.py:349
  89.8 0.6 collective-permute-start.15
  90.5 4.5 %layer_forward.5 = (bf16[128,768]{1,0:T(8,128)(2,1)S(1)}, bf16[128,768]{1,0:T(8,128)(2,1)S(1)}, f32[128,3328]{1,0:T(8,128)S(1)}, f32[128,128]{1,0:T(8,128)S(1)},...) custom-call(s32[4]{0:T(128)S(1)} %pad_add_fusion.where_ref.which_ref, ...), custom_call_target="tpu_custom_call" | custom-call | tf_op jit(solution)/shard_map/layer_forward/pallas_call | solution.py:326
  95.0 0.8 collective-permute-done.15.refs_0_.refs_3_
  95.7 8.6 %layer_backward.4 = (f32[128,768]{1,0:T(8,128)S(1)}, bf16[128,768]{1,0:T(8,128)(2,1)S(1)}, bf16[128,3328]{1,0:T(8,128)(2,1)S(1)}, bf16[128,128]{1,0:T(8,128)(2,1...) custom-call(s32[4]{0:T(128)S(1)} %pad_add_fusion.where_ref.which_ref, ...), custom_call_target="tpu_custom_call" | custom-call | tf_op jit(solution)/shard_map/layer_backward/pallas_call | solution.py:349
  104.4 0.8 collective-permute-start.16
  105.2 4.9 %collective-permute-done.16.refs_0_.refs_8_ = bf16[128,768]{1,0:T(8,128)(2,1)S(1)} collective-permute-done((bf16[128,768]{1,0:T(8,128)(2,1)S(1)}, bf16[128,768]{1,0:T(8,128)(2,1)S(1)}, u32[]{:S(2)}, u32[]{:S(2)}) %collective-permute-start.16) | collective-permute-done | bytes 196640 | tf_op jit(solution)/shard_map/ppermute | solution.py:810
  110.1 9.3 %layer_backward.5 = (f32[128,768]{1,0:T(8,128)S(1)}, bf16[128,768]{1,0:T(8,128)(2,1)}, bf16[128,3328]{1,0:T(8,128)(2,1)S(1)}, bf16[128,128]{1,0:T(8,128)(2,1)S(1...) custom-call(s32[4]{0:T(128)S(1)} %pad_add_fusion.where_ref.which_ref, ...), custom_call_target="tpu_custom_call" | custom-call | tf_op jit(solution)/shard_map/layer_backward/pallas_call | solution.py:349
  119.5 0.7 copy-done.2
  120.2 4.1 %weight_gradients_first.1 = (bf16[96,5120]{1,0:T(8,128)(2,1)S(1)}, bf16[96,5120]{1,0:T(8,128)(2,1)S(1)}, f32[8,128]{1,0:T(8,128)S(1)}, bf16[768,256]{1,0:T(8,128...) custom-call(s32[4]{0:T(128)S(1)} %pad_add_fusion.where_ref.which_ref, ...), custom_call_target="tpu_custom_call" | custom-call | tf_op jit(solution)/shard_map/weight_gradients_first/pallas_call | solution.py:666
  124.4 2.6 %collective-permute-done.17 = bf16[96,5120]{1,0:T(8,128)(2,1)S(1)} collective-permute-done((bf16[96,5120]{1,0:T(8,128)(2,1)S(1)}, bf16[96,5120]{1,0:T(8,128)(2,1)S(1)}, u32[]{:S(2)}, u32[]{:S(2)}) %collective-permute-start.17) | collective-permute-done | bytes 983072 | tf_op jit(solution)/shard_map/ppermute | solution.py:437
  127.3 0.9 slice.93
  128.2 1.5 collective-permute-start.20
  129.7 1.0 copy-done.5
  130.7 1.0 copy-done.7
  131.7 0.8 copy-done.13
  132.5 3.4 %weight_gradients_rest.1 = (bf16[96,5120]{1,0:T(8,128)(2,1)S(1)}, bf16[96,5120]{1,0:T(8,128)(2,1)S(1)}, bf16[96,5120]{1,0:T(8,128)(2,1)S(1)}, bf16[96,5120]{1,0:...) custom-call(s32[4]{0:T(128)S(1)} %pad_add_fusion.where_ref.which_ref, ...), custom_call_target="tpu_custom_call" | custom-call | tf_op jit(solution)/shard_map/weight_gradients_rest/pallas_call | solution.py:683
  137.0 4.7 %collective-permute-done.20 = bf16[48,5120]{1,0:T(8,128)(2,1)} collective-permute-done((bf16[48,5120]{1,0:T(8,128)(2,1)}, bf16[48,5120]{1,0:T(8,128)(2,1)}, u32[]{:S(2)}, u32[]{:S(2)}) %collective-permute-start.20) | collective-permute-done | bytes 491552 | tf_op jit(solution)/shard_map/ppermute | solution.py:437
  141.7 1.5 collective-permute-start.24
  143.3 1.1 fusion.2
  144.4 1.3 collective-permute-start.23
  146.0 1.2 collective-permute-start.22
  147.5 11.1 %collective-permute-done.23 = bf16[48,5120]{1,0:T(8,128)(2,1)S(1)} collective-permute-done((bf16[48,5120]{1,0:T(8,128)(2,1)S(1)}, bf16[48,5120]{1,0:T(8,128)(2,1)S(1)}, u32[]{:S(2)}, u32[]{:S(2)}) %collective-permute-start.23) | collective-permute-done | bytes 491552 | tf_op jit(solution)/shard_map/ppermute | solution.py:437
  158.6 2.2 %collective-permute-start.28 = (f32[8,128]{1,0:T(8,128)S(1)}, f32[8,128]{1,0:T(8,128)S(1)}, u32[]{:S(2)}, u32[]{:S(2)}) collective-permute-start(f32[8,128]{1,0:T(8,128)S(1)} %add.71), channel_id=1, source_target_pairs={{0,4},{1,5},{2,6},{3,7},{4,0},{5,1},{6,2},{7,3},{8,12},{9,13},{10,... | collective-permute-start | bytes 12296 | tf_op jit(solution)/shard_map/ppermute | solution.py:502
  160.9 1.3 collective-permute-start.27
  162.2 1.2 add_convert_fusion.1
  163.4 2.8 %collective-permute-start.26 = (bf16[48,5120]{1,0:T(8,128)(2,1)S(1)}, bf16[48,5120]{1,0:T(8,128)(2,1)S(1)}, u32[]{:S(2)}, u32[]{:S(2)}) collective-permute-start(bf16[48,5120]{1,0:T(8,128)(2,1)S(1)} %add_convert_fusion.1), channel_id=1, source_target_pairs={{4,8},{5,9},{6,10},{7,11},{8,4},{9,5},{10,6},{11,7},{20,24},{21,25... | collective-permute-start | bytes 1474568 | tf_op jit(solution)/shard_map/ppermute | solution.py:437
  166.1 0.6 collective-permute-start.25
  167.0 6.5 %collective-permute-done.27 = bf16[48,5120]{1,0:T(8,128)(2,1)S(1)} collective-permute-done((bf16[48,5120]{1,0:T(8,128)(2,1)S(1)}, bf16[48,5120]{1,0:T(8,128)(2,1)S(1)}, u32[]{:S(2)}, u32[]{:S(2)}) %collective-permute-start.27) | collective-permute-done | bytes 491552 | tf_op jit(solution)/shard_map/ppermute | solution.py:437
  173.5 2.6 %collective-permute-done.26 = bf16[48,5120]{1,0:T(8,128)(2,1)S(1)} collective-permute-done((bf16[48,5120]{1,0:T(8,128)(2,1)S(1)}, bf16[48,5120]{1,0:T(8,128)(2,1)S(1)}, u32[]{:S(2)}, u32[]{:S(2)}) %collective-permute-start.26) | collective-permute-done | bytes 491552 | tf_op jit(solution)/shard_map/ppermute | solution.py:437
  176.1 0.6 collective-permute-done.25
  176.7 0.9 collective-permute-start.33
  177.8 1.8 collective-permute-start.32
  179.8 2.8 %collective-permute-start.31 = (bf16[48,5120]{1,0:T(8,128)(2,1)S(1)}, bf16[48,5120]{1,0:T(8,128)(2,1)S(1)}, u32[]{:S(2)}, u32[]{:S(2)}) collective-permute-start(bf16[48,5120]{1,0:T(8,128)(2,1)S(1)} %add_convert_fusion), channel_id=1, source_target_pairs={{4,8},{5,9},{6,10},{7,11},{8,4},{9,5},{10,6},{11,7},{20,24},{21,25... | collective-permute-start | bytes 1474568 | tf_op jit(solution)/shard_map/ppermute | solution.py:437
  183.1 0.9 maximum_bitcast_fusion
  184.0 0.8 maximum_bitcast_fusion.1
  185.3 6.2 %collective-permute-done.30 = bf16[48,5120]{1,0:T(8,128)(2,1)S(1)} collective-permute-done((bf16[48,5120]{1,0:T(8,128)(2,1)S(1)}, bf16[48,5120]{1,0:T(8,128)(2,1)S(1)}, u32[]{:S(2)}, u32[]{:S(2)}) %collective-permute-start.30) | collective-permute-done | bytes 491552 | tf_op jit(solution)/shard_map/ppermute | solution.py:437
  191.6 1.0 unpack_sums.1
  (91 shorter events, 5.9 us)
Async XLA Ops:
  2.6 13.2 %collective-permute-start = (bf16[48,5120]{1,0:T(8,128)(2,1)}, bf16[48,5120]{1,0:T(8,128)(2,1)S(1)}, u32[]{:S(2)}, u32[]{:S(2)}) collective-permute-start(bf16[48,5120]{1,0:T(8,128)(2,1)} %pack_shard.1), channel_id=1, source_target_pairs={{0,4},{1,5},{2,6},{3,7},{4,0},{5,1},{6,2},{7,3},{8,12},{9,13},{10,... | collective-permute-start | bytes 1474568 | tf_op jit(solution)/shard_map/ppermute | solution.py:437
  2.6 16.2 %collective-permute-start.1 = (bf16[48,5120]{1,0:T(8,128)(2,1)}, bf16[48,5120]{1,0:T(8,128)(2,1)S(1)}, u32[]{:S(2)}, u32[]{:S(2)}) collective-permute-start(bf16[48,5120]{1,0:T(8,128)(2,1)} %pack_shard.1), channel_id=1, source_target_pairs={{4,8},{5,9},{6,10},{7,11},{8,4},{9,5},{10,6},{11,7},{20,24},{21,25... | collective-permute-start | bytes 1474568 | tf_op jit(solution)/shard_map/ppermute | solution.py:437
  7.7 12.7 %collective-permute-start.2 = (bf16[48,5120]{1,0:T(8,128)(2,1)}, bf16[48,5120]{1,0:T(8,128)(2,1)S(1)}, u32[]{:S(2)}, u32[]{:S(2)}) collective-permute-start(bf16[48,5120]{1,0:T(8,128)(2,1)} %pack_shard.1), channel_id=1, source_target_pairs={{0,2},{1,3},{2,0},{3,1},{4,6},{5,7},{6,4},{7,5},{8,10},{9,11},{10,... | collective-permute-start | bytes 1474568 | tf_op jit(solution)/shard_map/ppermute | solution.py:437
  20.3 13.4 %collective-permute-start.3 = (bf16[48,5120]{1,0:T(8,128)(2,1)S(1)}, bf16[48,5120]{1,0:T(8,128)(2,1)S(1)}, u32[]{:S(2)}, u32[]{:S(2)}) collective-permute-start(bf16[48,5120]{1,0:T(8,128)(2,1)S(1)} %collective-permute-done), channel_id=1, source_target_pairs={{4,8},{5,9},{6,10},{7,11},{8,4},{9,5},{10,6},{11,7},{20,24},{21,25... | collective-permute-start | bytes 1474568 | tf_op jit(solution)/shard_map/ppermute | solution.py:437
  22.5 11.6 %collective-permute-start.5 = (bf16[48,5120]{1,0:T(8,128)(2,1)S(1)}, bf16[48,5120]{1,0:T(8,128)(2,1)S(1)}, u32[]{:S(2)}, u32[]{:S(2)}) collective-permute-start(bf16[48,5120]{1,0:T(8,128)(2,1)S(1)} %collective-permute-done), channel_id=1, source_target_pairs={{0,2},{1,3},{2,0},{3,1},{4,6},{5,7},{6,4},{7,5},{8,10},{9,11},{10,... | collective-permute-start | bytes 1474568 | tf_op jit(solution)/shard_map/ppermute | solution.py:437
  24.1 10.3 %collective-permute-start.4 = (bf16[48,5120]{1,0:T(8,128)(2,1)S(1)}, bf16[48,5120]{1,0:T(8,128)(2,1)S(1)}, u32[]{:S(2)}, u32[]{:S(2)}) collective-permute-start(bf16[48,5120]{1,0:T(8,128)(2,1)S(1)} %collective-permute-done.1), channel_id=1, source_target_pairs={{4,0},{5,1},{6,2},{7,3},{8,12},{9,13},{10,14},{11,15},{20,16},{21,... | collective-permute-start | bytes 1474568 | tf_op jit(solution)/shard_map/ppermute | solution.py:437
  34.5 10.6 %collective-permute-start.7 = (bf16[48,5120]{1,0:T(8,128)(2,1)S(1)}, bf16[48,5120]{1,0:T(8,128)(2,1)S(1)}, u32[]{:S(2)}, u32[]{:S(2)}) collective-permute-start(bf16[48,5120]{1,0:T(8,128)(2,1)S(1)} %add.64), channel_id=1, source_target_pairs={{0,2},{1,3},{2,0},{3,1},{4,6},{5,7},{6,4},{7,5},{8,10},{9,11},{10,... | collective-permute-start | bytes 1474568 | tf_op jit(solution)/shard_map/ppermute | solution.py:437
  35.8 11.5 %collective-permute-start.6 = (bf16[48,5120]{1,0:T(8,128)(2,1)S(1)}, bf16[48,5120]{1,0:T(8,128)(2,1)S(1)}, u32[]{:S(2)}, u32[]{:S(2)}) collective-permute-start(bf16[48,5120]{1,0:T(8,128)(2,1)S(1)} %collective-permute-done.3), channel_id=1, source_target_pairs={{4,0},{5,1},{6,2},{7,3},{8,12},{9,13},{10,14},{11,15},{20,16},{21,... | collective-permute-start | bytes 1474568 | tf_op jit(solution)/shard_map/ppermute | solution.py:437
  40.3 17.0 %collective-permute-start.9 = (bf16[96,5120]{1,0:T(8,128)(2,1)S(1)}, bf16[96,5120]{1,0:T(8,128)(2,1)}, u32[]{:S(2)}, u32[]{:S(2)}) collective-permute-start(bf16[96,5120]{1,0:T(8,128)(2,1)S(1)} %pad_maximum_fusion.refs_0_), channel_id=1, source_target_pairs={{0,1},{1,0},{2,3},{3,2},{4,5},{5,4},{6,7},{7,6},{8,9},{9,8},{10,11... | collective-permute-start | bytes 2949128 | tf_op jit(solution)/shard_map/ppermute | solution.py:437
  47.4 9.7 %copy-start.17 = (f32[1,24]{1,0:T(1,128)S(1)}, f32[1,24]{1,0:T(1,128)}, u32[]{:S(2)}) copy-start(f32[1,24]{1,0:T(1,128)} %param.23) | copy-start | bytes 292
  47.4 9.8 %copy-start.16 = (s32[2,128]{1,0:T(2,128)S(1)}, s32[2,128]{1,0:T(2,128)}, u32[]{:S(2)}) copy-start(s32[2,128]{1,0:T(2,128)} %param.14) | copy-start | bytes 3076
  47.4 9.9 %copy-start.18 = (f32[1,24]{1,0:T(1,128)S(1)}, f32[1,24]{1,0:T(1,128)}, u32[]{:S(2)}) copy-start(f32[1,24]{1,0:T(1,128)} %param.22) | copy-start | bytes 292
  47.4 9.9 %copy-start.19 = (f32[1,24]{1,0:T(1,128)S(1)}, f32[1,24]{1,0:T(1,128)}, u32[]{:S(2)}) copy-start(f32[1,24]{1,0:T(1,128)} %param.21) | copy-start | bytes 292
  47.4 9.4 %collective-permute-start.8 = (bf16[48,5120]{1,0:T(8,128)(2,1)S(1)}, bf16[48,5120]{1,0:T(8,128)(2,1)S(1)}, u32[]{:S(2)}, u32[]{:S(2)}) collective-permute-start(bf16[48,5120]{1,0:T(8,128)(2,1)S(1)} %add.65), channel_id=1, source_target_pairs={{0,2},{1,3},{2,0},{3,1},{4,6},{5,7},{6,4},{7,5},{8,10},{9,11},{10,... | collective-permute-start | bytes 1474568 | tf_op jit(solution)/shard_map/ppermute | solution.py:437
  49.0 8.4 %collective-permute-start.10 = (bf16[96,5120]{1,0:T(8,128)(2,1)}, bf16[96,5120]{1,0:T(8,128)(2,1)}, u32[]{:S(2)}, u32[]{:S(2)}) collective-permute-start(bf16[96,5120]{1,0:T(8,128)(2,1)} %constant_dynamic-update-slice_fusion.refs_1_), channel_id=1, source_target_pairs={{0,1},{1,0},{2,3},{3,2},{4,5},{5,4},{6,7},{7,6},{8,9},{9,8},{10,11... | collective-permute-start | bytes 2949128 | tf_op jit(solution)/shard_map/ppermute | solution.py:437
  49.1 8.3 %collective-permute-start.11 = (bf16[96,5120]{1,0:T(8,128)(2,1)S(1)}, bf16[96,5120]{1,0:T(8,128)(2,1)}, u32[]{:S(2)}, u32[]{:S(2)}) collective-permute-start(bf16[96,5120]{1,0:T(8,128)(2,1)S(1)} %pad_maximum_fusion.1.refs_2_), channel_id=1, source_target_pairs={{0,1},{1,0},{2,3},{3,2},{4,5},{5,4},{6,7},{7,6},{8,9},{9,8},{10,11... | collective-permute-start | bytes 2949128 | tf_op jit(solution)/shard_map/ppermute | solution.py:437
  56.9 2.8 %collective-permute-start.12 = (bf16[96,5120]{1,0:T(8,128)(2,1)S(1)}, bf16[96,5120]{1,0:T(8,128)(2,1)}, u32[]{:S(2)}, u32[]{:S(2)}) collective-permute-start(bf16[96,5120]{1,0:T(8,128)(2,1)S(1)} %pad_maximum_fusion.2.refs_3_), channel_id=1, source_target_pairs={{0,1},{1,0},{2,3},{3,2},{4,5},{5,4},{6,7},{7,6},{8,9},{9,8},{10,11... | collective-permute-start | bytes 2949128 | tf_op jit(solution)/shard_map/ppermute | solution.py:437
  57.4 5.9 %copy-start = (bf16[2,128,768]{2,1,0:T(8,128)(2,1)S(1)}, bf16[2,128,768]{2,1,0:T(8,128)(2,1)}, u32[]{:S(2)}) copy-start(bf16[2,128,768]{2,1,0:T(8,128)(2,1)} %refs_1_.5) | copy-start | bytes 1179652
  67.7 13.1 %copy-start.1 = (bf16[2,128,768]{2,1,0:T(8,128)(2,1)S(1)}, bf16[2,128,768]{2,1,0:T(8,128)(2,1)}, u32[]{:S(2)}) copy-start(bf16[2,128,768]{2,1,0:T(8,128)(2,1)} %refs_8_.3) | copy-start | bytes 1179652
  67.7 7.0 %collective-permute-start.13 = (bf16[128,768]{1,0:T(8,128)(2,1)S(1)}, bf16[128,768]{1,0:T(8,128)(2,1)S(1)}, u32[]{:S(2)}, u32[]{:S(2)}) collective-permute-start(bf16[128,768]{1,0:T(8,128)(2,1)S(1)} %get-tuple-element.209), channel_id=1, source_target_pairs={{0,16},{16,0},{1,17},{17,1},{2,18},{18,2},{3,19},{19,3},{4,20},{20... | collective-permute-start | bytes 589832 | tf_op jit(solution)/shard_map/ppermute | solution.py:793
  79.2 10.6 %copy-start.8 = (bf16[128,768]{1,0:T(8,128)(2,1)}, bf16[128,768]{1,0:T(8,128)(2,1)S(1)}, u32[]{:S(2)}) copy-start(bf16[128,768]{1,0:T(8,128)(2,1)S(1)} %get-tuple-element.210) | copy-start | bytes 589828
  79.2 11.2 %collective-permute-start.14 = (bf16[128,768]{1,0:T(8,128)(2,1)S(1)}, bf16[128,768]{1,0:T(8,128)(2,1)S(1)}, u32[]{:S(2)}, u32[]{:S(2)}) collective-permute-start(bf16[128,768]{1,0:T(8,128)(2,1)S(1)} %get-tuple-element.210), channel_id=1, source_target_pairs={{0,16},{16,0},{1,17},{17,1},{2,18},{18,2},{3,19},{19,3},{4,20},{20... | collective-permute-start | bytes 589832 | tf_op jit(solution)/shard_map/ppermute | solution.py:795
  89.8 5.9 %collective-permute-start.15 = (bf16[128,768]{1,0:T(8,128)(2,1)S(1)}, bf16[128,768]{1,0:T(8,128)(2,1)S(1)}, u32[]{:S(2)}, u32[]{:S(2)}) collective-permute-start(bf16[128,768]{1,0:T(8,128)(2,1)S(1)} %get-tuple-element.146), channel_id=1, source_target_pairs={{0,16},{16,0},{1,17},{17,1},{2,18},{18,2},{3,19},{19,3},{4,20},{20... | collective-permute-start | bytes 589832 | tf_op jit(solution)/shard_map/ppermute | solution.py:804
  94.9 9.4 %copy-start.10 = (bf16[128,768]{1,0:T(8,128)(2,1)}, bf16[128,768]{1,0:T(8,128)(2,1)S(1)}, u32[]{:S(2)}) copy-start(bf16[128,768]{1,0:T(8,128)(2,1)S(1)} %get-tuple-element.211) | copy-start | bytes 589828
  104.4 5.7 %collective-permute-start.16 = (bf16[128,768]{1,0:T(8,128)(2,1)S(1)}, bf16[128,768]{1,0:T(8,128)(2,1)S(1)}, u32[]{:S(2)}, u32[]{:S(2)}) collective-permute-start(bf16[128,768]{1,0:T(8,128)(2,1)S(1)} %get-tuple-element.160), channel_id=1, source_target_pairs={{0,16},{16,0},{1,17},{17,1},{2,18},{18,2},{3,19},{19,3},{4,20},{20... | collective-permute-start | bytes 589832 | tf_op jit(solution)/shard_map/ppermute | solution.py:810
  119.5 0.7 copy-start.2
  124.3 2.9 %copy-start.4 = (bf16[768,256]{1,0:T(8,128)(2,1)}, bf16[768,256]{1,0:T(8,128)(2,1)S(1)}, u32[]{:S(2)}) copy-start(bf16[768,256]{1,0:T(8,128)(2,1)S(1)} %get-tuple-element.189.turned_ref) | copy-start | bytes 1179652
  124.3 2.9 %copy-start.6 = (bf16[256,768]{1,0:T(8,128)(2,1)}, bf16[256,768]{1,0:T(8,128)(2,1)S(1)}, u32[]{:S(2)}) copy-start(bf16[256,768]{1,0:T(8,128)(2,1)S(1)} %get-tuple-element.192.gb_ref) | copy-start | bytes 1179652
  124.3 2.9 %copy-start.12 = (f32[16,8,128]{2,1,0:T(8,128)}, f32[16,8,128]{2,1,0:T(8,128)S(1)}, u32[]{:S(2)}) copy-start(f32[16,8,128]{2,1,0:T(8,128)S(1)} %get-tuple-element.194.line_ref) | copy-start | bytes 196612
  124.3 2.6 %collective-permute-start.17 = (bf16[96,5120]{1,0:T(8,128)(2,1)S(1)}, bf16[96,5120]{1,0:T(8,128)(2,1)S(1)}, u32[]{:S(2)}, u32[]{:S(2)}) collective-permute-start(bf16[96,5120]{1,0:T(8,128)(2,1)S(1)} %get-tuple-element.188), channel_id=1, source_target_pairs={{0,1},{1,0},{2,3},{3,2},{4,5},{5,4},{6,7},{7,6},{8,9},{9,8},{10,11... | collective-permute-start | bytes 2949128 | tf_op jit(solution)/shard_map/ppermute | solution.py:437
  127.2 2.4 %copy-start.14 = (f32[96,5120]{1,0:T(8,128)}, f32[96,5120]{1,0:T(8,128)S(1)}, u32[]{:S(2)}) copy-start(f32[96,5120]{1,0:T(8,128)S(1)} %convert_add_fusion.3) | copy-start | bytes 5898244
  128.2 13.6 %collective-permute-start.20 = (bf16[48,5120]{1,0:T(8,128)(2,1)}, bf16[48,5120]{1,0:T(8,128)(2,1)}, u32[]{:S(2)}, u32[]{:S(2)}) collective-permute-start(bf16[48,5120]{1,0:T(8,128)(2,1)} %slice.93), channel_id=1, source_target_pairs={{0,2},{1,3},{2,0},{3,1},{4,6},{5,7},{6,4},{7,5},{8,10},{9,11},{10,... | collective-permute-start | bytes 1474568 | tf_op jit(solution)/shard_map/ppermute | solution.py:437
  129.7 7.4 %collective-permute-start.21 = (f32[8,128]{1,0:T(8,128)S(1)}, f32[8,128]{1,0:T(8,128)S(1)}, u32[]{:S(2)}, u32[]{:S(2)}) collective-permute-start(f32[8,128]{1,0:T(8,128)S(1)} %get-tuple-element.200), channel_id=1, source_target_pairs={{0,1},{1,0},{2,3},{3,2},{4,5},{5,4},{6,7},{7,6},{8,9},{9,8},{10,11... | collective-permute-start | bytes 12296 | tf_op jit(solution)/shard_map/ppermute | solution.py:502
  129.7 1.0 copy-start.5
  130.7 1.0 copy-start.7
  131.7 0.8 copy-start.13
  132.5 10.7 %copy-start.15 = (f32[96,5120]{1,0:T(8,128)S(1)}, f32[96,5120]{1,0:T(8,128)}, u32[]{:S(2)}) copy-start(f32[96,5120]{1,0:T(8,128)} %copy-done.14) | copy-start | bytes 5898244
  136.0 9.8 %collective-permute-start.19 = (bf16[96,5120]{1,0:T(8,128)(2,1)S(1)}, bf16[96,5120]{1,0:T(8,128)(2,1)S(1)}, u32[]{:S(2)}, u32[]{:S(2)}) collective-permute-start(bf16[96,5120]{1,0:T(8,128)(2,1)S(1)} %get-tuple-element.198), channel_id=1, source_target_pairs={{0,1},{1,0},{2,3},{3,2},{4,5},{5,4},{6,7},{7,6},{8,9},{9,8},{10,11... | collective-permute-start | bytes 2949128 | tf_op jit(solution)/shard_map/ppermute | solution.py:437
  136.5 10.7 %collective-permute-start.18 = (bf16[96,5120]{1,0:T(8,128)(2,1)S(1)}, bf16[96,5120]{1,0:T(8,128)(2,1)S(1)}, u32[]{:S(2)}, u32[]{:S(2)}) collective-permute-start(bf16[96,5120]{1,0:T(8,128)(2,1)S(1)} %get-tuple-element.196), channel_id=1, source_target_pairs={{0,1},{1,0},{2,3},{3,2},{4,5},{5,4},{6,7},{7,6},{8,9},{9,8},{10,11... | collective-permute-start | bytes 2949128 | tf_op jit(solution)/shard_map/ppermute | solution.py:437
  136.6 30.1 %collective-permute-start.29 = (bf16[96,5120]{1,0:T(8,128)(2,1)S(1)}, bf16[96,5120]{1,0:T(8,128)(2,1)S(1)}, u32[]{:S(2)}, u32[]{:S(2)}) collective-permute-start(bf16[96,5120]{1,0:T(8,128)(2,1)S(1)} %get-tuple-element.216), channel_id=1, source_target_pairs={{0,1},{1,0},{2,3},{3,2},{4,5},{5,4},{6,7},{7,6},{8,9},{9,8},{10,11... | collective-permute-start | bytes 2949128 | tf_op jit(solution)/shard_map/ppermute | solution.py:437
  141.7 4.0 %collective-permute-start.24 = (f32[8,128]{1,0:T(8,128)S(1)}, f32[8,128]{1,0:T(8,128)S(1)}, u32[]{:S(2)}, u32[]{:S(2)}) collective-permute-start(f32[8,128]{1,0:T(8,128)S(1)} %add.69), channel_id=1, source_target_pairs={{0,2},{1,3},{2,0},{3,1},{4,6},{5,7},{6,4},{7,5},{8,10},{9,11},{10,... | collective-permute-start | bytes 12296 | tf_op jit(solution)/shard_map/ppermute | solution.py:502
  144.4 14.2 %collective-permute-start.23 = (bf16[48,5120]{1,0:T(8,128)(2,1)S(1)}, bf16[48,5120]{1,0:T(8,128)(2,1)S(1)}, u32[]{:S(2)}, u32[]{:S(2)}) collective-permute-start(bf16[48,5120]{1,0:T(8,128)(2,1)S(1)} %fusion.2), channel_id=1, source_target_pairs={{0,4},{1,5},{2,6},{3,7},{12,8},{13,9},{14,10},{15,11},{16,20},{17,... | collective-permute-start | bytes 1474568 | tf_op jit(solution)/shard_map/ppermute | solution.py:437
  146.0 12.5 %collective-permute-start.22 = (bf16[48,5120]{1,0:T(8,128)(2,1)S(1)}, bf16[48,5120]{1,0:T(8,128)(2,1)S(1)}, u32[]{:S(2)}, u32[]{:S(2)}) collective-permute-start(bf16[48,5120]{1,0:T(8,128)(2,1)S(1)} %slice.91), channel_id=1, source_target_pairs={{0,2},{1,3},{2,0},{3,1},{4,6},{5,7},{6,4},{7,5},{8,10},{9,11},{10,... | collective-permute-start | bytes 1474568 | tf_op jit(solution)/shard_map/ppermute | solution.py:437
  158.6 8.4 %collective-permute-start.28 = (f32[8,128]{1,0:T(8,128)S(1)}, f32[8,128]{1,0:T(8,128)S(1)}, u32[]{:S(2)}, u32[]{:S(2)}) collective-permute-start(f32[8,128]{1,0:T(8,128)S(1)} %add.71), channel_id=1, source_target_pairs={{0,4},{1,5},{2,6},{3,7},{4,0},{5,1},{6,2},{7,3},{8,12},{9,13},{10,... | collective-permute-start | bytes 12296 | tf_op jit(solution)/shard_map/ppermute | solution.py:502
  160.9 12.7 %collective-permute-start.27 = (bf16[48,5120]{1,0:T(8,128)(2,1)S(1)}, bf16[48,5120]{1,0:T(8,128)(2,1)S(1)}, u32[]{:S(2)}, u32[]{:S(2)}) collective-permute-start(bf16[48,5120]{1,0:T(8,128)(2,1)S(1)} %fusion.3), channel_id=1, source_target_pairs={{0,4},{1,5},{2,6},{3,7},{12,8},{13,9},{14,10},{15,11},{16,20},{17,... | collective-permute-start | bytes 1474568 | tf_op jit(solution)/shard_map/ppermute | solution.py:437
  163.4 12.7 %collective-permute-start.26 = (bf16[48,5120]{1,0:T(8,128)(2,1)S(1)}, bf16[48,5120]{1,0:T(8,128)(2,1)S(1)}, u32[]{:S(2)}, u32[]{:S(2)}) collective-permute-start(bf16[48,5120]{1,0:T(8,128)(2,1)S(1)} %add_convert_fusion.1), channel_id=1, source_target_pairs={{4,8},{5,9},{6,10},{7,11},{8,4},{9,5},{10,6},{11,7},{20,24},{21,25... | collective-permute-start | bytes 1474568 | tf_op jit(solution)/shard_map/ppermute | solution.py:437
  166.1 10.6 %collective-permute-start.25 = (bf16[48,5120]{1,0:T(8,128)(2,1)S(1)}, bf16[48,5120]{1,0:T(8,128)(2,1)S(1)}, u32[]{:S(2)}, u32[]{:S(2)}) collective-permute-start(bf16[48,5120]{1,0:T(8,128)(2,1)S(1)} %slice.92), channel_id=1, source_target_pairs={{0,2},{1,3},{2,0},{3,1},{4,6},{5,7},{6,4},{7,5},{8,10},{9,11},{10,... | collective-permute-start | bytes 1474568 | tf_op jit(solution)/shard_map/ppermute | solution.py:437
  167.0 15.9 %copy-start.3 = (f32[128,768]{1,0:T(8,128)S(1)}, f32[128,768]{1,0:T(8,128)}, u32[]{:S(2)}) copy-start(f32[128,768]{1,0:T(8,128)} %copy-done.2) | copy-start | bytes 1179652
  176.7 8.1 %collective-permute-start.33 = (f32[8,128]{1,0:T(8,128)S(1)}, f32[8,128]{1,0:T(8,128)S(1)}, u32[]{:S(2)}, u32[]{:S(2)}) collective-permute-start(f32[8,128]{1,0:T(8,128)S(1)} %add.74), channel_id=1, source_target_pairs={{0,8},{1,9},{2,10},{3,11},{4,12},{5,13},{6,14},{7,15},{8,0},{9,1},... | collective-permute-start | bytes 12296 | tf_op jit(solution)/shard_map/ppermute | solution.py:502
  177.8 5.2 %copy-start.9 = (bf16[128,768]{1,0:T(8,128)(2,1)S(1)}, bf16[128,768]{1,0:T(8,128)(2,1)}, u32[]{:S(2)}) copy-start(bf16[128,768]{1,0:T(8,128)(2,1)} %copy-done.8) | copy-start | bytes 589828
  177.8 5.2 %copy-start.11 = (bf16[128,768]{1,0:T(8,128)(2,1)S(1)}, bf16[128,768]{1,0:T(8,128)(2,1)}, u32[]{:S(2)}) copy-start(bf16[128,768]{1,0:T(8,128)(2,1)} %copy-done.10) | copy-start | bytes 589828
  177.8 13.8 %collective-permute-start.32 = (bf16[48,5120]{1,0:T(8,128)(2,1)S(1)}, bf16[48,5120]{1,0:T(8,128)(2,1)S(1)}, u32[]{:S(2)}, u32[]{:S(2)}) collective-permute-start(bf16[48,5120]{1,0:T(8,128)(2,1)S(1)} %fusion.1), channel_id=1, source_target_pairs={{0,4},{1,5},{2,6},{3,7},{4,0},{5,1},{6,2},{7,3},{8,12},{9,13},{10,... | collective-permute-start | bytes 1474568 | tf_op jit(solution)/shard_map/ppermute | solution.py:437
  179.8 11.8 %collective-permute-start.31 = (bf16[48,5120]{1,0:T(8,128)(2,1)S(1)}, bf16[48,5120]{1,0:T(8,128)(2,1)S(1)}, u32[]{:S(2)}, u32[]{:S(2)}) collective-permute-start(bf16[48,5120]{1,0:T(8,128)(2,1)S(1)} %add_convert_fusion), channel_id=1, source_target_pairs={{4,8},{5,9},{6,10},{7,11},{8,4},{9,5},{10,6},{11,7},{20,24},{21,25... | collective-permute-start | bytes 1474568 | tf_op jit(solution)/shard_map/ppermute | solution.py:437
  182.6 8.9 %collective-permute-start.30 = (bf16[48,5120]{1,0:T(8,128)(2,1)S(1)}, bf16[48,5120]{1,0:T(8,128)(2,1)S(1)}, u32[]{:S(2)}, u32[]{:S(2)}) collective-permute-start(bf16[48,5120]{1,0:T(8,128)(2,1)S(1)} %slice.90), channel_id=1, source_target_pairs={{0,2},{1,3},{2,0},{3,1},{4,6},{5,7},{6,4},{7,5},{8,10},{9,11},{10,... | collective-permute-start | bytes 1474568 | tf_op jit(solution)/shard_map/ppermute | solution.py:437
where the time goes:
time: 196 us; the launch traced here: 193 us
  waiting for transfers between devices  79.8 us (41%)
  Pallas kernels  54.4 us (28%)
  starting transfers between devices  42.8 us (22%)
  other arithmetic  7.21 us (4%)
  local copies, waits for them, and re-layouts  7.1 us (4%)
    ppermute x26, waiting for transfers between devices, routed(): return lax.ppermute(value, 'dp', pairs)  68.7 us
    ppermute x26, starting transfers between devices, routed(): return lax.ppermute(value, 'dp', pairs)  33.6 us
    pallas_call x3, Pallas kernels, backward_layer(): pl.pallas_call(functools.partial(bwd_kernel, tuple((tuple((index for _, i...  27 us
    pallas_call x3, Pallas kernels, forward_layer(): pl.pallas_call(functools.partial(fwd_kernel, tuple((index for _, index in...  13.4 us
    ppermute x1, waiting for transfers between devices, shards(): r0 = lax.ppermute(f0[0], 'section', up)  5.46 us
    ppermute x1, waiting for transfers between devices, shards(): d1 = lax.ppermute(b1[1], 'section', down)  4.89 us
    ppermute x4, starting transfers between devices, summed(): lax.ppermute(vectors, 'dp', [(i, i ^ step) for i in range(4 * Z_CHIPS)])  4.59 us
    unnamed x41, local copies, waits for them, and re-layouts  4.5 us
  transfers between devices with their start and end apart: 34, of which 20 were waited for; matrix products, arithmetic and copies ran while one was open for 5% of the time, Pallas kernels for 9%

commit v1 on v0

--- a/solution.py
+++ b/solution.py
@@ -269,7 +269,7 @@
         dy_st = halves(dy)
         l1 = decay(cum, cum_t, linked, 2 * j)
         l2 = decay(cum, cum_t, linked, 2 * j + 1)
-        dm = near(dot_nt, dy_st, xw)
+        dm = dot_nt(dy_st.astype(BF16), xw.astype(BF16))
         dcross = dcross + dm[:length] * l1 + dm[length:] * l2
         m = jnp.concatenate([cross * l1, cross * l2], axis=0)
         dxw = near(dot_tn, m, dy_st)
@@ -488,8 +488,8 @@
     return [own_pair, near_pair, second_pair, last_pair, own_core, near_core, second_core, routed(last_pair, to_core)]
 
 
-def scatter_slots(first_pair, rest, vectors):
-    rows = first_pair[0].shape[0] // 2
+def scatter_slots(first_blocks, rest, vectors):
+    rows = first_blocks[0].shape[0]
 
     def met(kept, value):
         total = kept.astype(F32) + value.astype(F32)
@@ -501,11 +501,13 @@
     def summed(step):
         return vectors + lax.ppermute(vectors, "dp", [(i, i ^ step) for i in range(4 * Z_CHIPS)])
 
-    far, last = met(first_pair[0], routed(first_pair[1], to_core))
+    kept_far, kept_near, sent_far, sent_near = first_blocks
+    far = low(kept_far.astype(F32) + routed(sent_far, to_core).astype(F32))
+    last = kept_near.astype(F32) + routed(behind(sent_near, far), to_core).astype(F32)
     kept, sent = rest(far)
+    came = routed(far, to_y)
     vectors = behind(vectors, far)
     vectors = summed(1)
-    came = routed(far, to_y)
     over = [routed(block, to_core) for block in sent]
     far, second = met(kept[2], over[2])
     came, vectors = lax.optimization_barrier((came, vectors))
@@ -590,22 +592,22 @@
     return [owner for slot in range(4) for pair in (owners[slot], owners[4 + slot]) for owner in pair]
 
 
-def write_slot(slot, turned, mixed, gp_ref, gb_ref, gdt_ref, line_ref, kept_ref, sent_ref, where_ref):
-    rows, width, feat = kept_ref.shape[0] // 2, gp_ref.shape[1], gb_ref.shape[1]
+def write_slot(slot, turned, mixed, gp_ref, gb_ref, gdt_ref, line_ref, out_refs, where_ref):
+    rows, width, feat = turned.shape[0] // 16, gp_ref.shape[1], gb_ref.shape[1]
     blocks = mixed.shape[0] // turned.shape[0]
     last = width + blocks * feat
     mine = turned[4 * slot * rows : 4 * (slot + 1) * rows, :]
 
     def put(at, term):
-        kept_ref[:, at] = term[: 2 * rows].astype(BF16)
-        sent_ref[:, at] = term[2 * rows :].astype(BF16)
+        for part, (ref, to) in enumerate(out_refs):
+            ref[to : to + rows, at] = term[part * rows : (part + 1) * rows].astype(BF16)
 
     for c in range(width // 256):
         put(cols(c, 256), dot_nn(mine, gp_ref[:, cols(c, 256)]))
     put(slice(last, last + LANES), dot_nn(mine, gdt_ref[...]))
     owners = slot_blocks(where_ref)[4 * slot : 4 * slot + 4]
     for part, owner in enumerate(owners):
-        ref, to = (kept_ref, sent_ref)[part // 2], part % 2 * rows
+        ref, to = out_refs[part]
         for b in range(blocks):
             start = ((4 * slot + part) * blocks + b) * rows
             at = slice(width + b * feat, width + (b + 1) * feat)
@@ -615,14 +617,44 @@
         ref[to + 16 : to + rows, last + LANES :] = jnp.zeros((rows - 16, LANES), BF16)
 
 
-def first_weight_kernel(rows, chans, where_ref, *refs):
-    sources, smalls, outs, scratch = refs[:20], refs[20:32], refs[32:41], refs[41:]
-    kept_ref, sent_ref, vec_ref, turned_ref, mixed_ref, gp_ref, gb_ref, gdt_ref, line_ref = outs
-    n_ref, mix_ref, flat_ref, wide_ref, sems = scratch
-    tok, feat, inner = sources[0].shape[0], n_ref.shape[1], mix_ref.shape[1]
+def turn_kernel(rows, where_ref, n_first, mix_first, n_last, mix_last, n_both, mix_both, turned_ref, mixed_ref, flat_ref, wide_ref):
+    tok, feat = n_both.shape
+    many = mix_both.shape[1] // feat * rows
+
+    def early(one, other):
+        return jnp.where(where_ref[0] == 0, one[...], other[...])
+
+    flat_ref[:, :tok] = early(n_first, n_last).T
+    flat_ref[:, tok:] = n_both[...].T
+    wide_ref[:, :tok] = early(mix_first, mix_last).T
+    wide_ref[:, tok:] = mix_both[...].T
+    for i, owner in enumerate(slot_blocks(where_ref)):
+        turned_ref[i * rows : (i + 1) * rows, :] = flat_ref[pl.ds(pl.multiple_of(owner * rows, 16), rows), :]
+        mixed_ref[i * many : (i + 1) * many, :] = wide_ref[pl.ds(pl.multiple_of(owner * many, 16), many), :]
+
+
+def turn(where, first, last, both, rows):
+    tok, feat = both[0].shape
+    inner = both[1].shape[1]
+    return pl.pallas_call(
+        functools.partial(turn_kernel, rows),
+        in_specs=[SMEM_SPEC] + [VMEM_SPEC] * 6,
+        out_specs=[VMEM_SPEC] * 2,
+        out_shape=(shape_of((feat, 2 * tok), BF16), shape_of((inner, 2 * tok), BF16)),
+        scratch_shapes=[pltpu.VMEM((feat, 2 * tok), BF16), pltpu.VMEM((inner, 2 * tok), BF16)],
+        compiler_params=PARAMS,
+        name="turn_rows",
+    )(where, *first, *last, *both)
+
+
+def first_weight_kernel(rows, chans, where_ref, turned_ref, mixed_ref, *refs):
+    sources, smalls, outs, sems = refs[:12], refs[12:24], refs[24:33], refs[33]
+    vec_ref, gp_ref, gb_ref, gdt_ref, line_ref = outs[4:]
+    feat, inner = turned_ref.shape[0], mixed_ref.shape[0]
+    tok = turned_ref.shape[1] // 2
     blocks = inner // feat
-    into = [ref.at[part * tok : (part + 1) * tok] for part in range(2) for ref in (n_ref, mix_ref, gp_ref, gb_ref, gdt_ref)]
-    take(where_ref, [[(source, None) for source in sources[10 * i : 10 * i + 10]] for i in range(2)], into, sems)
+    into = [ref.at[part * tok : (part + 1) * tok] for part in range(2) for ref in (gp_ref, gb_ref, gdt_ref)]
+    take(where_ref, [[(source, None) for source in sources[6 * i : 6 * i + 6]] for i in range(2)], into, sems)
     early = jnp.where(where_ref[0] == 0, 0.0, 1.0)
     sums = [one[...] + early * zero[...] + (1.0 - early) * two[...] for zero, one, two in zip(smalls[0::3], smalls[1::3], smalls[2::3])]
     vec_ref[...] = sums[3]
@@ -632,52 +664,36 @@
         block = cut(pieces[0], chans, i)
         block = jnp.where(row == TAPS + 1, jnp.broadcast_to(cut(pieces[1], blocks * rows, i)[0:1], block.shape), block)
         line_ref[i] = jnp.where(row == TAPS + 2, jnp.broadcast_to(cut(pieces[2], rows, i)[0:1], block.shape), block)
-    owners = slot_blocks(where_ref)
-    taken(into, sems, 0, 5)
-    flat_ref[...] = n_ref[...].T
-    for i, owner in enumerate(owners):
-        turned_ref[i * rows : (i + 1) * rows, :] = flat_ref[pl.ds(pl.multiple_of(owner * rows, 16), rows), :]
-    taken(into, sems, 1, 6)
-    wide_ref[...] = mix_ref[...].T
-    many = blocks * rows
-    for i, owner in enumerate(owners):
-        mixed_ref[i * many : (i + 1) * many, :] = wide_ref[pl.ds(pl.multiple_of(owner * many, 16), many), :]
-    taken(into, sems, 2, 7, 3, 8, 4, 9)
-    write_slot(3, turned_ref, mixed_ref, gp_ref, gb_ref, gdt_ref, line_ref, kept_ref, sent_ref, where_ref)
+    taken(into, sems, 0, 1, 2, 3, 4, 5)
+    write_slot(3, turned_ref, mixed_ref, gp_ref, gb_ref, gdt_ref, line_ref, [(ref, 0) for ref in outs[:4]], where_ref)
 
 
 def rest_weight_kernel(where_ref, turned_ref, mixed_ref, gp_ref, gb_ref, gdt_ref, line_ref, *outs):
     for slot in (2, 1, 0):
-        write_slot(slot, turned_ref, mixed_ref, gp_ref, gb_ref, gdt_ref, line_ref, outs[slot], outs[3 + slot], where_ref)
-
-
-def weight_terms(where, one, other, smalls, rows, chans):
-    tok, feat = one[0].shape
-    inner, width = one[1].shape[1], one[2].shape[1]
-    pair = shape_of((2 * rows, width + inner + 2 * LANES), BF16)
+        targets = [(ref, to) for ref in (outs[slot], outs[3 + slot]) for to in (0, outs[slot].shape[0] // 2)]
+        write_slot(slot, turned_ref, mixed_ref, gp_ref, gb_ref, gdt_ref, line_ref, targets, where_ref)
+
+
+def weight_terms(where, turned, one, other, smalls, rows, chans):
+    feat, inner = turned[0].shape[0], turned[1].shape[0]
+    tok, width = one[0].shape
+    full = width + inner + 2 * LANES
+    block, pair = shape_of((rows, full), BF16), shape_of((2 * rows, full), BF16)
     shared = (
-        shape_of((feat, 2 * tok), BF16),
-        shape_of((inner, 2 * tok), BF16),
         shape_of((2 * tok, width), BF16),
         shape_of((2 * tok, feat), BF16),
         shape_of((2 * tok, LANES), BF16),
         shape_of((feat // rows, 8, LANES)),
     )
-    kept, sent, vectors, *common = pl.pallas_call(
+    *blocks, vectors, gp, gb, gdt, lines = pl.pallas_call(
         functools.partial(first_weight_kernel, rows, chans),
-        in_specs=[SMEM_SPEC] + [HBM_SPEC] * 20 + [VMEM_SPEC] * 12,
+        in_specs=[SMEM_SPEC] + [VMEM_SPEC] * 2 + [HBM_SPEC] * 12 + [VMEM_SPEC] * 12,
         out_specs=[VMEM_SPEC] * 9,
-        out_shape=(pair, pair, shape_of((8, LANES))) + shared,
-        scratch_shapes=[
-            pltpu.VMEM((2 * tok, feat), BF16),
-            pltpu.VMEM((2 * tok, inner), BF16),
-            pltpu.VMEM((feat, 2 * tok), BF16),
-            pltpu.VMEM((inner, 2 * tok), BF16),
-            pltpu.SemaphoreType.DMA((10,)),
-        ],
+        out_shape=(block,) * 4 + (shape_of((8, LANES)),) + shared,
+        scratch_shapes=[pltpu.SemaphoreType.DMA((6,))],
         compiler_params=PARAMS,
         name="weight_gradients_first",
-    )(where, *one, *other, *smalls)
+    )(where, *turned, *one, *other, *smalls)
 
     def rest(after):
         outs = pl.pallas_call(
@@ -687,10 +703,10 @@
             out_shape=(pair,) * 6,
             compiler_params=PARAMS,
             name="weight_gradients_rest",
-        )(where, behind(common[0], after), *common[1:])
+        )(where, *turned, behind(gp, after), gb, gdt, lines)
         return outs[:3], outs[3:]
 
-    return (kept, sent), vectors, rest
+    return blocks, vectors, rest
 
 
 def unpack_kernel(own_ref, second_ref, near_ref, wm_ref, wo_ref, wdt_ref, cw_ref, cb_ref, gg_ref, ng_ref, square):
@@ -808,13 +824,17 @@
     ]
     b1 = backward_layer(2, where, ids, weights, now)
     d1 = lax.ppermute(b1[1], "section", down)
+    if aligned:
+        rows_of = (f0[1], f0[5]), (f2[1], f2[5]), (f1[1], behind(f1[5], b1[1]))
+        turned = turn(where, *rows_of, rows)
     b2 = backward_layer(1, where, ids, weights, [[(d1, None), (inputs, 1)] + kept])
     dch, din, dgin, dhp = tuple(choose(two, zero) + one for zero, one, two in zip(b0[4:], b1[4:], b2[4:]))
     on_first = (f0[1], f0[5], b1[2], d0, b1[3]), (f1[1], f1[5], b2[2], d1, b2[3])
     on_last = (f2[1], f2[5], b1[2], cotangent[1], b1[3]), (f1[1], f1[5], b0[2], cotangent[0], b0[3])
     if aligned:
         smalls = [part[i] for i in (4, 5, 6, 7) for part in (b0, b1, b2)]
-        first_pair, vectors, rest = weight_terms(where, on_first[0] + on_first[1], on_last[0] + on_last[1], smalls, rows, chans)
+        one, other = (pair[0][2:] + pair[1][2:] for pair in (on_first, on_last))
+        first_blocks, vectors, rest = weight_terms(where, turned, one, other, smalls, rows, chans)
     else:
         n, mix, gp, gb, gdt = tuple(
             jnp.concatenate([choose(on_first[0][i], on_last[0][i]), choose(on_first[1][i], on_last[1][i])], axis=0) for i in range(5)
@@ -835,7 +855,7 @@
         parts = [dot_tn(n, gp), wide, dot_tn(n, gdt), jnp.concatenate(own, axis=0)]
         packed_grad = jnp.concatenate([part.astype(BF16) for part in parts], axis=1)
     if aligned:
-        terms, vectors, started = scatter_slots(first_pair, rest, vectors)
+        terms, vectors, started = scatter_slots(first_blocks, rest, vectors)
         heads_sum = vectors[:, :heads]
     else:
         summed = lax.psum_scatter(packed_grad, "dp", scatter_dimension=0, tiled=True)

time: 196 us -> 193 us (0.985)
  local copies, waits for them, and re-layouts: 7.1 us -> 3.62 us
    unnamed x41, local copies, waits for them, and re-layouts: 4.5 us -> 1.91 us
    ppermute x26 -> x27, waiting for transfers between devices: 68.7 us -> 70 us  [routed(): return lax.ppermute(value, 'dp', pairs)]
    convert_element_type x5 -> x6, other arithmetic: 2.82 us -> 4.1 us  [low(): return value.astype(BF16)]
    ppermute x26 -> x27, starting transfers between devices: 33.6 us -> 33 us  [routed(): return lax.ppermute(value, 'dp', pairs)]
  transfers between devices with their start and end apart: 34 -> 35, of which waited for: 20 -> 20; matrix products, arithmetic and copies ran while one was open for 5% -> 5% of each run, Pallas kernels for 9% -> 9%
where the time goes in v1:
time: 193 us; the launch traced here: 190 us
  waiting for transfers between devices  80.1 us (42%)
  Pallas kernels  54.3 us (28%)
  starting transfers between devices  42.6 us (22%)
  other arithmetic  8.24 us (4%)
  local copies, waits for them, and re-layouts  3.62 us (2%)
    ppermute x27, waiting for transfers between devices, routed(): return lax.ppermute(value, 'dp', pairs)  70 us
    ppermute x27, starting transfers between devices, routed(): return lax.ppermute(value, 'dp', pairs)  33 us
    pallas_call x3, Pallas kernels, backward_layer(): pl.pallas_call(functools.partial(bwd_kernel, tuple((tuple((index for _, i...  26.5 us
    pallas_call x3, Pallas kernels, forward_layer(): pl.pallas_call(functools.partial(fwd_kernel, tuple((index for _, index in...  13.4 us
    ppermute x1, waiting for transfers between devices, shards(): r0 = lax.ppermute(f0[0], 'section', up)  5.45 us
    ppermute x4, starting transfers between devices, summed(): lax.ppermute(vectors, 'dp', [(i, i ^ step) for i in range(4 * Z_CHIPS)])  5.09 us
    convert_element_type x6, other arithmetic, low(): return value.astype(BF16)  4.1 us
    ppermute x1, waiting for transfers between devices, shards(): d1 = lax.ppermute(b1[1], 'section', down)  3.89 us
  transfers between devices with their start and end apart: 35, of which 20 were waited for; matrix products, arithmetic and copies ran while one was open for 5% of the time, Pallas kernels for 9%

profile of v1, /device:TPU:8, one launch (start us, length us, event | category | flops | bytes accessed | tf_op | source)
XLA Modules:
  0.0 190.4 jit_solution(7274780859316815749)
XLA Ops:
  0.6 2.0 %pack_shard.1 = bf16[48,5120]{1,0:T(8,128)(2,1)} custom-call(bf16[48,3328]{1,0:T(8,128)(2,1)} %bitcast.40, bf16[96,768]{1,0:T(8,128)(2,1)} %bitcast.41, bf16[24,48]{1,0:T(8,128)(2,1)} %bitcast.42, bf16[4,112]{1,0:T(4,128)(2,1)} %bitcast.43, bf16[1,112]{1,0:T(2,128)(2,1)} %cb_ref.1, bf16[1,96]{1,0:T(2,128)(2,1)} %gg_ref.1, bf16[1,48]{1,0:T(2,128)(2,1)} %ng_ref.1), custom_call_target="tpu_custom_call" | custom-call | tf_op jit(solution)/shard_map/pack_shard/pallas_call | solution.py:413
  2.6 5.0 %collective-permute-start.1 = (bf16[48,5120]{1,0:T(8,128)(2,1)}, bf16[48,5120]{1,0:T(8,128)(2,1)S(1)}, u32[]{:S(2)}, u32[]{:S(2)}) collective-permute-start(bf16[48,5120]{1,0:T(8,128)(2,1)} %pack_shard.1), channel_id=1, source_target_pairs={{4,8},{5,9},{6,10},{7,11},{8,4},{9,5},{10,6},{11,7},{20,24},{21,25... | collective-permute-start | bytes 1474568 | tf_op jit(solution)/shard_map/ppermute | solution.py:437
  7.7 1.6 collective-permute-start.2
  9.2 6.5 %collective-permute-done = bf16[48,5120]{1,0:T(8,128)(2,1)S(1)} collective-permute-done((bf16[48,5120]{1,0:T(8,128)(2,1)}, bf16[48,5120]{1,0:T(8,128)(2,1)S(1)}, u32[]{:S(2)}, u32[]{:S(2)}) %collective-permute-start) | collective-permute-done | bytes 491552 | tf_op jit(solution)/shard_map/ppermute | solution.py:437
  15.8 3.0 %collective-permute-done.1 = bf16[48,5120]{1,0:T(8,128)(2,1)S(1)} collective-permute-done((bf16[48,5120]{1,0:T(8,128)(2,1)}, bf16[48,5120]{1,0:T(8,128)(2,1)S(1)}, u32[]{:S(2)}, u32[]{:S(2)}) %collective-permute-start.1) | collective-permute-done | bytes 491552 | tf_op jit(solution)/shard_map/ppermute | solution.py:437
  18.8 1.5 collective-permute-done.2
  20.3 2.2 %collective-permute-start.3 = (bf16[48,5120]{1,0:T(8,128)(2,1)S(1)}, bf16[48,5120]{1,0:T(8,128)(2,1)S(1)}, u32[]{:S(2)}, u32[]{:S(2)}) collective-permute-start(bf16[48,5120]{1,0:T(8,128)(2,1)S(1)} %collective-permute-done), channel_id=1, source_target_pairs={{4,8},{5,9},{6,10},{7,11},{8,4},{9,5},{10,6},{11,7},{20,24},{21,25... | collective-permute-start | bytes 1474568 | tf_op jit(solution)/shard_map/ppermute | solution.py:437
  22.5 1.6 collective-permute-start.5
  24.1 1.3 collective-permute-start.4
  25.4 1.1 pad_maximum_fusion.refs_0_
  26.5 7.2 %collective-permute-done.3 = bf16[48,5120]{1,0:T(8,128)(2,1)S(1)} collective-permute-done((bf16[48,5120]{1,0:T(8,128)(2,1)S(1)}, bf16[48,5120]{1,0:T(8,128)(2,1)S(1)}, u32[]{:S(2)}, u32[]{:S(2)}) %collective-permute-start.3) | collective-permute-done | bytes 491552 | tf_op jit(solution)/shard_map/ppermute | solution.py:437
  34.5 1.3 collective-permute-start.7
  35.8 3.7 %collective-permute-start.6 = (bf16[48,5120]{1,0:T(8,128)(2,1)S(1)}, bf16[48,5120]{1,0:T(8,128)(2,1)S(1)}, u32[]{:S(2)}, u32[]{:S(2)}) collective-permute-start(bf16[48,5120]{1,0:T(8,128)(2,1)S(1)} %collective-permute-done.3), channel_id=1, source_target_pairs={{4,0},{5,1},{6,2},{7,3},{8,12},{9,13},{10,14},{11,15},{20,16},{21,... | collective-permute-start | bytes 1474568 | tf_op jit(solution)/shard_map/ppermute | solution.py:437
  39.5 0.8 constant_dynamic-update-slice_fusion.1
  40.3 0.8 constant_dynamic-update-slice_fusion.refs_1_
  41.2 4.0 %collective-permute-done.7 = bf16[48,5120]{1,0:T(8,128)(2,1)S(1)} collective-permute-done((bf16[48,5120]{1,0:T(8,128)(2,1)S(1)}, bf16[48,5120]{1,0:T(8,128)(2,1)S(1)}, u32[]{:S(2)}, u32[]{:S(2)}) %collective-permute-start.7) | collective-permute-done | bytes 491552 | tf_op jit(solution)/shard_map/ppermute | solution.py:437
  45.2 2.1 %collective-permute-done.6 = bf16[48,5120]{1,0:T(8,128)(2,1)S(1)} collective-permute-done((bf16[48,5120]{1,0:T(8,128)(2,1)S(1)}, bf16[48,5120]{1,0:T(8,128)(2,1)S(1)}, u32[]{:S(2)}, u32[]{:S(2)}) %collective-permute-start.6) | collective-permute-done | bytes 491552 | tf_op jit(solution)/shard_map/ppermute | solution.py:437
  47.4 1.6 collective-permute-start.8
  49.1 0.6 collective-permute-start.11
  49.7 7.2 %collective-permute-done.8 = bf16[48,5120]{1,0:T(8,128)(2,1)S(1)} collective-permute-done((bf16[48,5120]{1,0:T(8,128)(2,1)S(1)}, bf16[48,5120]{1,0:T(8,128)(2,1)S(1)}, u32[]{:S(2)}, u32[]{:S(2)}) %collective-permute-start.8) | collective-permute-done | bytes 491552 | tf_op jit(solution)/shard_map/ppermute | solution.py:437
  57.4 2.3 %collective-permute-done.12.refs_7_ = bf16[96,5120]{1,0:T(8,128)(2,1)} collective-permute-done((bf16[96,5120]{1,0:T(8,128)(2,1)S(1)}, bf16[96,5120]{1,0:T(8,128)(2,1)}, u32[]{:S(2)}, u32[]{:S(2)}) %collective-permute-start.12) | collective-permute-done | bytes 983072 | tf_op jit(solution)/shard_map/ppermute | solution.py:437
  59.7 3.5 %settle_weights.1 = (bf16[768,3456]{1,0:T(8,128)(2,1)S(1)}, bf16[1536,768]{1,0:T(8,128)(2,1)S(1)}, f32[4,1792]{1,0:T(4,128)S(1)}, f32[1,1792]{1,0:T(1,128)S(1)},...) custom-call(s32[4]{0:T(128)S(1)} %pad_add_fusion.where_ref.which_ref, bf16[96,5120]{1,0:T(8,128)(2,1)S(1)} %pad_maximum_fusion.refs_0_, ...), custom_call_target="tpu_custom_call" | custom-call | tf_op jit(solution)/shard_map/settle_weights/pallas_call | solution.py:572
  63.2 4.5 %layer_forward.3 = (bf16[128,768]{1,0:T(8,128)(2,1)S(1)}, bf16[128,768]{1,0:T(8,128)(2,1)S(1)}, f32[128,3328]{1,0:T(8,128)S(1)}, f32[128,128]{1,0:T(8,128)S(1)},...) custom-call(s32[4]{0:T(128)S(1)} %pad_add_fusion.where_ref.which_ref, ...), custom_call_target="tpu_custom_call" | custom-call | tf_op jit(solution)/shard_map/layer_forward/pallas_call | solution.py:326
  67.7 1.6 collective-permute-start.13
  69.3 5.5 %collective-permute-done.13.refs_1_.refs_9_ = bf16[128,768]{1,0:T(8,128)(2,1)S(1)} collective-permute-done((bf16[128,768]{1,0:T(8,128)(2,1)S(1)}, bf16[128,768]{1,0:T(8,128)(2,1)S(1)}, u32[]{:S(2)}, u32[]{:S(2)}) %collective-permute-start.13) | collective-permute-done | bytes 196640 | tf_op jit(solution)/shard_map/ppermute | solution.py:809
  74.7 4.5 %layer_forward.4 = (bf16[128,768]{1,0:T(8,128)(2,1)S(1)}, bf16[128,768]{1,0:T(8,128)(2,1)S(1)}, f32[128,3328]{1,0:T(8,128)S(1)}, f32[128,128]{1,0:T(8,128)S(1)},...) custom-call(s32[4]{0:T(128)S(1)} %pad_add_fusion.where_ref.which_ref, ...), custom_call_target="tpu_custom_call" | custom-call | tf_op jit(solution)/shard_map/layer_forward/pallas_call | solution.py:326
  79.2 1.5 collective-permute-start.14
  80.8 8.9 %layer_backward.3 = (f32[128,768]{1,0:T(8,128)S(1)}, bf16[128,768]{1,0:T(8,128)(2,1)S(1)}, bf16[128,3328]{1,0:T(8,128)(2,1)S(1)}, bf16[128,128]{1,0:T(8,128)(2,1...) custom-call(s32[4]{0:T(128)S(1)} %pad_add_fusion.where_ref.which_ref, ...), custom_call_target="tpu_custom_call" | custom-call | tf_op jit(solution)/shard_map/layer_backward/pallas_call | solution.py:349
  89.7 0.6 collective-permute-start.15
  90.3 4.5 %layer_forward.5 = (bf16[128,768]{1,0:T(8,128)(2,1)S(1)}, bf16[128,768]{1,0:T(8,128)(2,1)S(1)}, f32[128,3328]{1,0:T(8,128)S(1)}, f32[128,128]{1,0:T(8,128)S(1)},...) custom-call(s32[4]{0:T(128)S(1)} %pad_add_fusion.where_ref.which_ref, ...), custom_call_target="tpu_custom_call" | custom-call | tf_op jit(solution)/shard_map/layer_forward/pallas_call | solution.py:326
  94.8 0.8 collective-permute-done.15.refs_0_.refs_1_
  95.6 8.5 %layer_backward.4 = (f32[128,768]{1,0:T(8,128)S(1)}, bf16[128,768]{1,0:T(8,128)(2,1)S(1)}, bf16[128,3328]{1,0:T(8,128)(2,1)S(1)}, bf16[128,128]{1,0:T(8,128)(2,1...) custom-call(s32[4]{0:T(128)S(1)} %pad_add_fusion.where_ref.which_ref, ...), custom_call_target="tpu_custom_call" | custom-call | tf_op jit(solution)/shard_map/layer_backward/pallas_call | solution.py:349
  104.2 0.8 collective-permute-start.16
  105.0 1.0 turn_rows.1
  106.0 3.9 %collective-permute-done.16.refs_0_.refs_4_ = bf16[128,768]{1,0:T(8,128)(2,1)S(1)} collective-permute-done((bf16[128,768]{1,0:T(8,128)(2,1)S(1)}, bf16[128,768]{1,0:T(8,128)(2,1)S(1)}, u32[]{:S(2)}, u32[]{:S(2)}) %collective-permute-start.16) | collective-permute-done | bytes 196640 | tf_op jit(solution)/shard_map/ppermute | solution.py:826
  109.9 9.1 %layer_backward.5 = (f32[128,768]{1,0:T(8,128)S(1)}, bf16[128,768]{1,0:T(8,128)(2,1)}, bf16[128,3328]{1,0:T(8,128)(2,1)S(1)}, bf16[128,128]{1,0:T(8,128)(2,1)S(1...) custom-call(s32[4]{0:T(128)S(1)} %pad_add_fusion.where_ref.which_ref, ...), custom_call_target="tpu_custom_call" | custom-call | tf_op jit(solution)/shard_map/layer_backward/pallas_call | solution.py:349
  119.0 3.4 %weight_gradients_first.1 = (bf16[48,5120]{1,0:T(8,128)(2,1)S(1)}, bf16[48,5120]{1,0:T(8,128)(2,1)S(1)}, bf16[48,5120]{1,0:T(8,128)(2,1)S(1)}, bf16[48,5120]{1,0...) custom-call(s32[4]{0:T(128)S(1)} %pad_add_fusion.where_ref.which_ref, ...), custom_call_target="tpu_custom_call" | custom-call | tf_op jit(solution)/shard_map/weight_gradients_first/pallas_call | solution.py:688
  122.6 1.9 collective-permute-done.17
  124.4 0.9 add_convert_fusion.2
  125.3 1.5 collective-permute-start.20
  127.4 1.0 copy-done.9
  128.3 3.4 %weight_gradients_rest.1 = (bf16[96,5120]{1,0:T(8,128)(2,1)S(1)}, bf16[96,5120]{1,0:T(8,128)(2,1)S(1)}, bf16[96,5120]{1,0:T(8,128)(2,1)S(1)}, bf16[96,5120]{1,0:...) custom-call(s32[4]{0:T(128)S(1)} %pad_add_fusion.where_ref.which_ref, ...), custom_call_target="tpu_custom_call" | custom-call | tf_op jit(solution)/shard_map/weight_gradients_rest/pallas_call | solution.py:699
  132.4 6.5 %collective-permute-done.20 = bf16[48,5120]{1,0:T(8,128)(2,1)} collective-permute-done((bf16[48,5120]{1,0:T(8,128)(2,1)}, bf16[48,5120]{1,0:T(8,128)(2,1)}, u32[]{:S(2)}, u32[]{:S(2)}) %collective-permute-start.20) | collective-permute-done | bytes 491552 | tf_op jit(solution)/shard_map/ppermute | solution.py:437
  138.9 1.5 collective-permute-start.25
  140.4 1.4 fusion.2
  141.8 1.3 collective-permute-start.24
  143.4 1.0 collective-permute-start.22
  144.7 11.3 %collective-permute-done.24 = bf16[48,5120]{1,0:T(8,128)(2,1)S(1)} collective-permute-done((bf16[48,5120]{1,0:T(8,128)(2,1)S(1)}, bf16[48,5120]{1,0:T(8,128)(2,1)S(1)}, u32[]{:S(2)}, u32[]{:S(2)}) %collective-permute-start.24) | collective-permute-done | bytes 491552 | tf_op jit(solution)/shard_map/ppermute | solution.py:437
  156.0 2.2 %collective-permute-start.29 = (f32[8,128]{1,0:T(8,128)S(1)}, f32[8,128]{1,0:T(8,128)S(1)}, u32[]{:S(2)}, u32[]{:S(2)}) collective-permute-start(f32[8,128]{1,0:T(8,128)S(1)} %add.75), channel_id=1, source_target_pairs={{0,4},{1,5},{2,6},{3,7},{4,0},{5,1},{6,2},{7,3},{8,12},{9,13},{10,... | collective-permute-start | bytes 12296 | tf_op jit(solution)/shard_map/ppermute | solution.py:502
  158.2 1.3 collective-permute-start.28
  159.5 1.4 add_convert_fusion.1
  161.0 2.8 %collective-permute-start.27 = (bf16[48,5120]{1,0:T(8,128)(2,1)S(1)}, bf16[48,5120]{1,0:T(8,128)(2,1)S(1)}, u32[]{:S(2)}, u32[]{:S(2)}) collective-permute-start(bf16[48,5120]{1,0:T(8,128)(2,1)S(1)} %add_convert_fusion.1), channel_id=1, source_target_pairs={{4,8},{5,9},{6,10},{7,11},{8,4},{9,5},{10,6},{11,7},{20,24},{21,25... | collective-permute-start | bytes 1474568 | tf_op jit(solution)/shard_map/ppermute | solution.py:437
  163.7 0.6 collective-permute-start.26
  164.6 6.3 %collective-permute-done.28 = bf16[48,5120]{1,0:T(8,128)(2,1)S(1)} collective-permute-done((bf16[48,5120]{1,0:T(8,128)(2,1)S(1)}, bf16[48,5120]{1,0:T(8,128)(2,1)S(1)}, u32[]{:S(2)}, u32[]{:S(2)}) %collective-permute-start.28) | collective-permute-done | bytes 491552 | tf_op jit(solution)/shard_map/ppermute | solution.py:437
  170.9 2.8 %collective-permute-done.27 = bf16[48,5120]{1,0:T(8,128)(2,1)S(1)} collective-permute-done((bf16[48,5120]{1,0:T(8,128)(2,1)S(1)}, bf16[48,5120]{1,0:T(8,128)(2,1)S(1)}, u32[]{:S(2)}, u32[]{:S(2)}) %collective-permute-start.27) | collective-permute-done | bytes 491552 | tf_op jit(solution)/shard_map/ppermute | solution.py:437
  173.7 0.6 collective-permute-done.26
  174.3 0.9 collective-permute-start.34
  175.4 1.8 collective-permute-start.33
  177.4 2.8 %collective-permute-start.32 = (bf16[48,5120]{1,0:T(8,128)(2,1)S(1)}, bf16[48,5120]{1,0:T(8,128)(2,1)S(1)}, u32[]{:S(2)}, u32[]{:S(2)}) collective-permute-start(bf16[48,5120]{1,0:T(8,128)(2,1)S(1)} %add_convert_fusion), channel_id=1, source_target_pairs={{4,8},{5,9},{6,10},{7,11},{8,4},{9,5},{10,6},{11,7},{20,24},{21,25... | collective-permute-start | bytes 1474568 | tf_op jit(solution)/shard_map/ppermute | solution.py:437
  180.7 0.9 maximum_bitcast_fusion
  181.6 0.8 maximum_bitcast_fusion.1
  182.4 0.5 fusion.4
  182.9 6.1 %collective-permute-done.31 = bf16[48,5120]{1,0:T(8,128)(2,1)S(1)} collective-permute-done((bf16[48,5120]{1,0:T(8,128)(2,1)S(1)}, bf16[48,5120]{1,0:T(8,128)(2,1)S(1)}, u32[]{:S(2)}, u32[]{:S(2)}) %collective-permute-start.31) | collective-permute-done | bytes 491552 | tf_op jit(solution)/shard_map/ppermute | solution.py:437
  189.2 1.0 unpack_sums.1
  (93 shorter events, 4.6 us)
Async XLA Ops:
  2.6 13.2 %collective-permute-start = (bf16[48,5120]{1,0:T(8,128)(2,1)}, bf16[48,5120]{1,0:T(8,128)(2,1)S(1)}, u32[]{:S(2)}, u32[]{:S(2)}) collective-permute-start(bf16[48,5120]{1,0:T(8,128)(2,1)} %pack_shard.1), channel_id=1, source_target_pairs={{0,4},{1,5},{2,6},{3,7},{4,0},{5,1},{6,2},{7,3},{8,12},{9,13},{10,... | collective-permute-start | bytes 1474568 | tf_op jit(solution)/shard_map/ppermute | solution.py:437
  2.6 16.2 %collective-permute-start.1 = (bf16[48,5120]{1,0:T(8,128)(2,1)}, bf16[48,5120]{1,0:T(8,128)(2,1)S(1)}, u32[]{:S(2)}, u32[]{:S(2)}) collective-permute-start(bf16[48,5120]{1,0:T(8,128)(2,1)} %pack_shard.1), channel_id=1, source_target_pairs={{4,8},{5,9},{6,10},{7,11},{8,4},{9,5},{10,6},{11,7},{20,24},{21,25... | collective-permute-start | bytes 1474568 | tf_op jit(solution)/shard_map/ppermute | solution.py:437
  7.7 12.7 %collective-permute-start.2 = (bf16[48,5120]{1,0:T(8,128)(2,1)}, bf16[48,5120]{1,0:T(8,128)(2,1)S(1)}, u32[]{:S(2)}, u32[]{:S(2)}) collective-permute-start(bf16[48,5120]{1,0:T(8,128)(2,1)} %pack_shard.1), channel_id=1, source_target_pairs={{0,2},{1,3},{2,0},{3,1},{4,6},{5,7},{6,4},{7,5},{8,10},{9,11},{10,... | collective-permute-start | bytes 1474568 | tf_op jit(solution)/shard_map/ppermute | solution.py:437
  20.3 13.4 %collective-permute-start.3 = (bf16[48,5120]{1,0:T(8,128)(2,1)S(1)}, bf16[48,5120]{1,0:T(8,128)(2,1)S(1)}, u32[]{:S(2)}, u32[]{:S(2)}) collective-permute-start(bf16[48,5120]{1,0:T(8,128)(2,1)S(1)} %collective-permute-done), channel_id=1, source_target_pairs={{4,8},{5,9},{6,10},{7,11},{8,4},{9,5},{10,6},{11,7},{20,24},{21,25... | collective-permute-start | bytes 1474568 | tf_op jit(solution)/shard_map/ppermute | solution.py:437
  22.5 11.6 %collective-permute-start.5 = (bf16[48,5120]{1,0:T(8,128)(2,1)S(1)}, bf16[48,5120]{1,0:T(8,128)(2,1)S(1)}, u32[]{:S(2)}, u32[]{:S(2)}) collective-permute-start(bf16[48,5120]{1,0:T(8,128)(2,1)S(1)} %collective-permute-done), channel_id=1, source_target_pairs={{0,2},{1,3},{2,0},{3,1},{4,6},{5,7},{6,4},{7,5},{8,10},{9,11},{10,... | collective-permute-start | bytes 1474568 | tf_op jit(solution)/shard_map/ppermute | solution.py:437
  24.1 10.3 %collective-permute-start.4 = (bf16[48,5120]{1,0:T(8,128)(2,1)S(1)}, bf16[48,5120]{1,0:T(8,128)(2,1)S(1)}, u32[]{:S(2)}, u32[]{:S(2)}) collective-permute-start(bf16[48,5120]{1,0:T(8,128)(2,1)S(1)} %collective-permute-done.1), channel_id=1, source_target_pairs={{4,0},{5,1},{6,2},{7,3},{8,12},{9,13},{10,14},{11,15},{20,16},{21,... | collective-permute-start | bytes 1474568 | tf_op jit(solution)/shard_map/ppermute | solution.py:437
  34.5 10.6 %collective-permute-start.7 = (bf16[48,5120]{1,0:T(8,128)(2,1)S(1)}, bf16[48,5120]{1,0:T(8,128)(2,1)S(1)}, u32[]{:S(2)}, u32[]{:S(2)}) collective-permute-start(bf16[48,5120]{1,0:T(8,128)(2,1)S(1)} %add.67), channel_id=1, source_target_pairs={{0,2},{1,3},{2,0},{3,1},{4,6},{5,7},{6,4},{7,5},{8,10},{9,11},{10,... | collective-permute-start | bytes 1474568 | tf_op jit(solution)/shard_map/ppermute | solution.py:437
  35.8 11.5 %collective-permute-start.6 = (bf16[48,5120]{1,0:T(8,128)(2,1)S(1)}, bf16[48,5120]{1,0:T(8,128)(2,1)S(1)}, u32[]{:S(2)}, u32[]{:S(2)}) collective-permute-start(bf16[48,5120]{1,0:T(8,128)(2,1)S(1)} %collective-permute-done.3), channel_id=1, source_target_pairs={{4,0},{5,1},{6,2},{7,3},{8,12},{9,13},{10,14},{11,15},{20,16},{21,... | collective-permute-start | bytes 1474568 | tf_op jit(solution)/shard_map/ppermute | solution.py:437
  40.3 17.0 %collective-permute-start.9 = (bf16[96,5120]{1,0:T(8,128)(2,1)S(1)}, bf16[96,5120]{1,0:T(8,128)(2,1)}, u32[]{:S(2)}, u32[]{:S(2)}) collective-permute-start(bf16[96,5120]{1,0:T(8,128)(2,1)S(1)} %pad_maximum_fusion.refs_0_), channel_id=1, source_target_pairs={{0,1},{1,0},{2,3},{3,2},{4,5},{5,4},{6,7},{7,6},{8,9},{9,8},{10,11... | collective-permute-start | bytes 2949128 | tf_op jit(solution)/shard_map/ppermute | solution.py:437
  47.4 9.7 %copy-start.17 = (f32[1,24]{1,0:T(1,128)S(1)}, f32[1,24]{1,0:T(1,128)}, u32[]{:S(2)}) copy-start(f32[1,24]{1,0:T(1,128)} %param.23) | copy-start | bytes 292
  47.4 9.8 %copy-start.16 = (s32[2,128]{1,0:T(2,128)S(1)}, s32[2,128]{1,0:T(2,128)}, u32[]{:S(2)}) copy-start(s32[2,128]{1,0:T(2,128)} %param.14) | copy-start | bytes 3076
  47.4 9.9 %copy-start.18 = (f32[1,24]{1,0:T(1,128)S(1)}, f32[1,24]{1,0:T(1,128)}, u32[]{:S(2)}) copy-start(f32[1,24]{1,0:T(1,128)} %param.22) | copy-start | bytes 292
  47.4 9.9 %copy-start.19 = (f32[1,24]{1,0:T(1,128)S(1)}, f32[1,24]{1,0:T(1,128)}, u32[]{:S(2)}) copy-start(f32[1,24]{1,0:T(1,128)} %param.21) | copy-start | bytes 292
  47.4 9.4 %collective-permute-start.8 = (bf16[48,5120]{1,0:T(8,128)(2,1)S(1)}, bf16[48,5120]{1,0:T(8,128)(2,1)S(1)}, u32[]{:S(2)}, u32[]{:S(2)}) collective-permute-start(bf16[48,5120]{1,0:T(8,128)(2,1)S(1)} %add.68), channel_id=1, source_target_pairs={{0,2},{1,3},{2,0},{3,1},{4,6},{5,7},{6,4},{7,5},{8,10},{9,11},{10,... | collective-permute-start | bytes 1474568 | tf_op jit(solution)/shard_map/ppermute | solution.py:437
  49.0 8.4 %collective-permute-start.10 = (bf16[96,5120]{1,0:T(8,128)(2,1)}, bf16[96,5120]{1,0:T(8,128)(2,1)}, u32[]{:S(2)}, u32[]{:S(2)}) collective-permute-start(bf16[96,5120]{1,0:T(8,128)(2,1)} %constant_dynamic-update-slice_fusion.refs_1_), channel_id=1, source_target_pairs={{0,1},{1,0},{2,3},{3,2},{4,5},{5,4},{6,7},{7,6},{8,9},{9,8},{10,11... | collective-permute-start | bytes 2949128 | tf_op jit(solution)/shard_map/ppermute | solution.py:437
  49.1 8.3 %collective-permute-start.11 = (bf16[96,5120]{1,0:T(8,128)(2,1)S(1)}, bf16[96,5120]{1,0:T(8,128)(2,1)}, u32[]{:S(2)}, u32[]{:S(2)}) collective-permute-start(bf16[96,5120]{1,0:T(8,128)(2,1)S(1)} %pad_maximum_fusion.1.refs_2_), channel_id=1, source_target_pairs={{0,1},{1,0},{2,3},{3,2},{4,5},{5,4},{6,7},{7,6},{8,9},{9,8},{10,11... | collective-permute-start | bytes 2949128 | tf_op jit(solution)/shard_map/ppermute | solution.py:437
  56.9 2.8 %collective-permute-start.12 = (bf16[96,5120]{1,0:T(8,128)(2,1)S(1)}, bf16[96,5120]{1,0:T(8,128)(2,1)}, u32[]{:S(2)}, u32[]{:S(2)}) collective-permute-start(bf16[96,5120]{1,0:T(8,128)(2,1)S(1)} %pad_maximum_fusion.2.refs_3_), channel_id=1, source_target_pairs={{0,1},{1,0},{2,3},{3,2},{4,5},{5,4},{6,7},{7,6},{8,9},{9,8},{10,11... | collective-permute-start | bytes 2949128 | tf_op jit(solution)/shard_map/ppermute | solution.py:437
  57.4 5.9 %copy-start = (bf16[2,128,768]{2,1,0:T(8,128)(2,1)S(1)}, bf16[2,128,768]{2,1,0:T(8,128)(2,1)}, u32[]{:S(2)}) copy-start(bf16[2,128,768]{2,1,0:T(8,128)(2,1)} %refs_1_.5) | copy-start | bytes 1179652
  67.7 11.5 %copy-start.10 = (bf16[128,768]{1,0:T(8,128)(2,1)}, bf16[128,768]{1,0:T(8,128)(2,1)S(1)}, u32[]{:S(2)}) copy-start(bf16[128,768]{1,0:T(8,128)(2,1)S(1)} %get-tuple-element.217) | copy-start | bytes 589828
  67.7 13.1 %copy-start.1 = (bf16[2,128,768]{2,1,0:T(8,128)(2,1)S(1)}, bf16[2,128,768]{2,1,0:T(8,128)(2,1)}, u32[]{:S(2)}) copy-start(bf16[2,128,768]{2,1,0:T(8,128)(2,1)} %refs_8_.3) | copy-start | bytes 1179652
  67.7 7.0 %collective-permute-start.13 = (bf16[128,768]{1,0:T(8,128)(2,1)S(1)}, bf16[128,768]{1,0:T(8,128)(2,1)S(1)}, u32[]{:S(2)}, u32[]{:S(2)}) collective-permute-start(bf16[128,768]{1,0:T(8,128)(2,1)S(1)} %get-tuple-element.217), channel_id=1, source_target_pairs={{0,16},{16,0},{1,17},{17,1},{2,18},{18,2},{3,19},{19,3},{4,20},{20... | collective-permute-start | bytes 589832 | tf_op jit(solution)/shard_map/ppermute | solution.py:809
  79.2 10.5 %copy-start.12 = (bf16[128,768]{1,0:T(8,128)(2,1)}, bf16[128,768]{1,0:T(8,128)(2,1)S(1)}, u32[]{:S(2)}) copy-start(bf16[128,768]{1,0:T(8,128)(2,1)S(1)} %get-tuple-element.218) | copy-start | bytes 589828
  79.2 11.1 %collective-permute-start.14 = (bf16[128,768]{1,0:T(8,128)(2,1)S(1)}, bf16[128,768]{1,0:T(8,128)(2,1)S(1)}, u32[]{:S(2)}, u32[]{:S(2)}) collective-permute-start(bf16[128,768]{1,0:T(8,128)(2,1)S(1)} %get-tuple-element.218), channel_id=1, source_target_pairs={{0,16},{16,0},{1,17},{17,1},{2,18},{18,2},{3,19},{19,3},{4,20},{20... | collective-permute-start | bytes 589832 | tf_op jit(solution)/shard_map/ppermute | solution.py:811
  89.7 5.1 %copy-start.2 = (f32[128,768]{1,0:T(8,128)}, f32[128,768]{1,0:T(8,128)S(1)}, u32[]{:S(2)}) copy-start(f32[128,768]{1,0:T(8,128)S(1)} %get-tuple-element.221) | copy-start | bytes 1179652
  89.7 5.9 %collective-permute-start.15 = (bf16[128,768]{1,0:T(8,128)(2,1)S(1)}, bf16[128,768]{1,0:T(8,128)(2,1)S(1)}, u32[]{:S(2)}, u32[]{:S(2)}) collective-permute-start(bf16[128,768]{1,0:T(8,128)(2,1)S(1)} %get-tuple-element.150), channel_id=1, source_target_pairs={{0,16},{16,0},{1,17},{17,1},{2,18},{18,2},{3,19},{19,3},{4,20},{20... | collective-permute-start | bytes 589832 | tf_op jit(solution)/shard_map/ppermute | solution.py:820
  94.8 9.3 %copy-start.14 = (bf16[128,768]{1,0:T(8,128)(2,1)}, bf16[128,768]{1,0:T(8,128)(2,1)S(1)}, u32[]{:S(2)}) copy-start(bf16[128,768]{1,0:T(8,128)(2,1)S(1)} %get-tuple-element.219) | copy-start | bytes 589828
  104.1 14.9 %copy-start.4 = (f32[128,768]{1,0:T(8,128)}, f32[128,768]{1,0:T(8,128)S(1)}, u32[]{:S(2)}) copy-start(f32[128,768]{1,0:T(8,128)S(1)} %get-tuple-element.220) | copy-start | bytes 1179652
  104.2 5.7 %collective-permute-start.16 = (bf16[128,768]{1,0:T(8,128)(2,1)S(1)}, bf16[128,768]{1,0:T(8,128)(2,1)S(1)}, u32[]{:S(2)}, u32[]{:S(2)}) collective-permute-start(bf16[128,768]{1,0:T(8,128)(2,1)S(1)} %get-tuple-element.164), channel_id=1, source_target_pairs={{0,16},{16,0},{1,17},{17,1},{2,18},{18,2},{3,19},{19,3},{4,20},{20... | collective-permute-start | bytes 589832 | tf_op jit(solution)/shard_map/ppermute | solution.py:826
  119.0 3.5 %copy-start.6 = (f32[128,768]{1,0:T(8,128)}, f32[128,768]{1,0:T(8,128)S(1)}, u32[]{:S(2)}) copy-start(f32[128,768]{1,0:T(8,128)S(1)} %get-tuple-element.222) | copy-start | bytes 1179652
  122.5 2.8 %copy-start.8 = (bf16[256,768]{1,0:T(8,128)(2,1)}, bf16[256,768]{1,0:T(8,128)(2,1)S(1)}, u32[]{:S(2)}) copy-start(bf16[256,768]{1,0:T(8,128)(2,1)S(1)} %get-tuple-element.197.gb_ref) | copy-start | bytes 1179652
  122.5 1.9 %collective-permute-start.17 = (bf16[48,5120]{1,0:T(8,128)(2,1)S(1)}, bf16[48,5120]{1,0:T(8,128)(2,1)S(1)}, u32[]{:S(2)}, u32[]{:S(2)}) collective-permute-start(bf16[48,5120]{1,0:T(8,128)(2,1)S(1)} %get-tuple-element.195), channel_id=1, source_target_pairs={{0,1},{1,0},{2,3},{3,2},{4,5},{5,4},{6,7},{7,6},{8,9},{9,8},{10,11... | collective-permute-start | bytes 1474568 | tf_op jit(solution)/shard_map/ppermute | solution.py:437
  125.3 13.6 %collective-permute-start.20 = (bf16[48,5120]{1,0:T(8,128)(2,1)}, bf16[48,5120]{1,0:T(8,128)(2,1)}, u32[]{:S(2)}, u32[]{:S(2)}) collective-permute-start(bf16[48,5120]{1,0:T(8,128)(2,1)} %add_convert_fusion.2), channel_id=1, source_target_pairs={{0,2},{1,3},{2,0},{3,1},{4,6},{5,7},{6,4},{7,5},{8,10},{9,11},{10,... | collective-permute-start | bytes 1474568 | tf_op jit(solution)/shard_map/ppermute | solution.py:437
  126.8 13.6 %collective-permute-start.23 = (bf16[48,5120]{1,0:T(8,128)(2,1)}, bf16[48,5120]{1,0:T(8,128)(2,1)}, u32[]{:S(2)}, u32[]{:S(2)}) collective-permute-start(bf16[48,5120]{1,0:T(8,128)(2,1)} %get-tuple-element.210), channel_id=1, source_target_pairs={{0,1},{1,0},{2,3},{3,2},{4,5},{5,4},{6,7},{7,6},{8,9},{9,8},{10,11... | collective-permute-start | bytes 1474568 | tf_op jit(solution)/shard_map/ppermute | solution.py:437
  126.8 5.5 %collective-permute-start.21 = (f32[8,128]{1,0:T(8,128)S(1)}, f32[8,128]{1,0:T(8,128)S(1)}, u32[]{:S(2)}, u32[]{:S(2)}) collective-permute-start(f32[8,128]{1,0:T(8,128)S(1)} %get-tuple-element.205), channel_id=1, source_target_pairs={{0,1},{1,0},{2,3},{3,2},{4,5},{5,4},{6,7},{7,6},{8,9},{9,8},{10,11... | collective-permute-start | bytes 12296 | tf_op jit(solution)/shard_map/ppermute | solution.py:502
  127.4 1.0 copy-start.9
  131.8 11.3 %collective-permute-start.19 = (bf16[96,5120]{1,0:T(8,128)(2,1)S(1)}, bf16[96,5120]{1,0:T(8,128)(2,1)S(1)}, u32[]{:S(2)}, u32[]{:S(2)}) collective-permute-start(bf16[96,5120]{1,0:T(8,128)(2,1)S(1)} %get-tuple-element.203), channel_id=1, source_target_pairs={{0,1},{1,0},{2,3},{3,2},{4,5},{5,4},{6,7},{7,6},{8,9},{9,8},{10,11... | collective-permute-start | bytes 2949128 | tf_op jit(solution)/shard_map/ppermute | solution.py:437
  131.8 12.5 %collective-permute-start.18 = (bf16[96,5120]{1,0:T(8,128)(2,1)S(1)}, bf16[96,5120]{1,0:T(8,128)(2,1)S(1)}, u32[]{:S(2)}, u32[]{:S(2)}) collective-permute-start(bf16[96,5120]{1,0:T(8,128)(2,1)S(1)} %get-tuple-element.201), channel_id=1, source_target_pairs={{0,1},{1,0},{2,3},{3,2},{4,5},{5,4},{6,7},{7,6},{8,9},{9,8},{10,11... | collective-permute-start | bytes 2949128 | tf_op jit(solution)/shard_map/ppermute | solution.py:437
  132.3 31.9 %collective-permute-start.30 = (bf16[96,5120]{1,0:T(8,128)(2,1)S(1)}, bf16[96,5120]{1,0:T(8,128)(2,1)S(1)}, u32[]{:S(2)}, u32[]{:S(2)}) collective-permute-start(bf16[96,5120]{1,0:T(8,128)(2,1)S(1)} %get-tuple-element.224), channel_id=1, source_target_pairs={{0,1},{1,0},{2,3},{3,2},{4,5},{5,4},{6,7},{7,6},{8,9},{9,8},{10,11... | collective-permute-start | bytes 2949128 | tf_op jit(solution)/shard_map/ppermute | solution.py:437
  138.9 4.2 %collective-permute-start.25 = (f32[8,128]{1,0:T(8,128)S(1)}, f32[8,128]{1,0:T(8,128)S(1)}, u32[]{:S(2)}, u32[]{:S(2)}) collective-permute-start(f32[8,128]{1,0:T(8,128)S(1)} %add.72), channel_id=1, source_target_pairs={{0,2},{1,3},{2,0},{3,1},{4,6},{5,7},{6,4},{7,5},{8,10},{9,11},{10,... | collective-permute-start | bytes 12296 | tf_op jit(solution)/shard_map/ppermute | solution.py:502
  141.8 14.2 %collective-permute-start.24 = (bf16[48,5120]{1,0:T(8,128)(2,1)S(1)}, bf16[48,5120]{1,0:T(8,128)(2,1)S(1)}, u32[]{:S(2)}, u32[]{:S(2)}) collective-permute-start(bf16[48,5120]{1,0:T(8,128)(2,1)S(1)} %fusion.2), channel_id=1, source_target_pairs={{0,4},{1,5},{2,6},{3,7},{12,8},{13,9},{14,10},{15,11},{16,20},{17,... | collective-permute-start | bytes 1474568 | tf_op jit(solution)/shard_map/ppermute | solution.py:437
  143.4 12.6 %collective-permute-start.22 = (bf16[48,5120]{1,0:T(8,128)(2,1)S(1)}, bf16[48,5120]{1,0:T(8,128)(2,1)S(1)}, u32[]{:S(2)}, u32[]{:S(2)}) collective-permute-start(bf16[48,5120]{1,0:T(8,128)(2,1)S(1)} %slice.74), channel_id=1, source_target_pairs={{0,2},{1,3},{2,0},{3,1},{4,6},{5,7},{6,4},{7,5},{8,10},{9,11},{10,... | collective-permute-start | bytes 1474568 | tf_op jit(solution)/shard_map/ppermute | solution.py:437
  156.0 8.6 %collective-permute-start.29 = (f32[8,128]{1,0:T(8,128)S(1)}, f32[8,128]{1,0:T(8,128)S(1)}, u32[]{:S(2)}, u32[]{:S(2)}) collective-permute-start(f32[8,128]{1,0:T(8,128)S(1)} %add.75), channel_id=1, source_target_pairs={{0,4},{1,5},{2,6},{3,7},{4,0},{5,1},{6,2},{7,3},{8,12},{9,13},{10,... | collective-permute-start | bytes 12296 | tf_op jit(solution)/shard_map/ppermute | solution.py:502
  158.2 12.7 %collective-permute-start.28 = (bf16[48,5120]{1,0:T(8,128)(2,1)S(1)}, bf16[48,5120]{1,0:T(8,128)(2,1)S(1)}, u32[]{:S(2)}, u32[]{:S(2)}) collective-permute-start(bf16[48,5120]{1,0:T(8,128)(2,1)S(1)} %fusion.3), channel_id=1, source_target_pairs={{0,4},{1,5},{2,6},{3,7},{12,8},{13,9},{14,10},{15,11},{16,20},{17,... | collective-permute-start | bytes 1474568 | tf_op jit(solution)/shard_map/ppermute | solution.py:437
  161.0 12.7 %collective-permute-start.27 = (bf16[48,5120]{1,0:T(8,128)(2,1)S(1)}, bf16[48,5120]{1,0:T(8,128)(2,1)S(1)}, u32[]{:S(2)}, u32[]{:S(2)}) collective-permute-start(bf16[48,5120]{1,0:T(8,128)(2,1)S(1)} %add_convert_fusion.1), channel_id=1, source_target_pairs={{4,8},{5,9},{6,10},{7,11},{8,4},{9,5},{10,6},{11,7},{20,24},{21,25... | collective-permute-start | bytes 1474568 | tf_op jit(solution)/shard_map/ppermute | solution.py:437
  163.7 10.6 %collective-permute-start.26 = (bf16[48,5120]{1,0:T(8,128)(2,1)S(1)}, bf16[48,5120]{1,0:T(8,128)(2,1)S(1)}, u32[]{:S(2)}, u32[]{:S(2)}) collective-permute-start(bf16[48,5120]{1,0:T(8,128)(2,1)S(1)} %slice.75), channel_id=1, source_target_pairs={{0,2},{1,3},{2,0},{3,1},{4,6},{5,7},{6,4},{7,5},{8,10},{9,11},{10,... | collective-permute-start | bytes 1474568 | tf_op jit(solution)/shard_map/ppermute | solution.py:437
  164.6 15.9 %copy-start.3 = (f32[128,768]{1,0:T(8,128)S(1)}, f32[128,768]{1,0:T(8,128)}, u32[]{:S(2)}) copy-start(f32[128,768]{1,0:T(8,128)} %copy-done.2) | copy-start | bytes 1179652
  164.6 15.9 %copy-start.5 = (f32[128,768]{1,0:T(8,128)S(1)}, f32[128,768]{1,0:T(8,128)}, u32[]{:S(2)}) copy-start(f32[128,768]{1,0:T(8,128)} %copy-done.4) | copy-start | bytes 1179652
  164.6 15.9 %copy-start.7 = (f32[128,768]{1,0:T(8,128)S(1)}, f32[128,768]{1,0:T(8,128)}, u32[]{:S(2)}) copy-start(f32[128,768]{1,0:T(8,128)} %copy-done.6) | copy-start | bytes 1179652
  174.3 8.1 %collective-permute-start.34 = (f32[8,128]{1,0:T(8,128)S(1)}, f32[8,128]{1,0:T(8,128)S(1)}, u32[]{:S(2)}, u32[]{:S(2)}) collective-permute-start(f32[8,128]{1,0:T(8,128)S(1)} %add.78), channel_id=1, source_target_pairs={{0,8},{1,9},{2,10},{3,11},{4,12},{5,13},{6,14},{7,15},{8,0},{9,1},... | collective-permute-start | bytes 12296 | tf_op jit(solution)/shard_map/ppermute | solution.py:502
  175.4 5.2 %copy-start.11 = (bf16[128,768]{1,0:T(8,128)(2,1)S(1)}, bf16[128,768]{1,0:T(8,128)(2,1)}, u32[]{:S(2)}) copy-start(bf16[128,768]{1,0:T(8,128)(2,1)} %copy-done.10) | copy-start | bytes 589828
  175.4 5.2 %copy-start.13 = (bf16[128,768]{1,0:T(8,128)(2,1)S(1)}, bf16[128,768]{1,0:T(8,128)(2,1)}, u32[]{:S(2)}) copy-start(bf16[128,768]{1,0:T(8,128)(2,1)} %copy-done.12) | copy-start | bytes 589828
  175.4 5.2 %copy-start.15 = (bf16[128,768]{1,0:T(8,128)(2,1)S(1)}, bf16[128,768]{1,0:T(8,128)(2,1)}, u32[]{:S(2)}) copy-start(bf16[128,768]{1,0:T(8,128)(2,1)} %copy-done.14) | copy-start | bytes 589828
  175.4 13.7 %collective-permute-start.33 = (bf16[48,5120]{1,0:T(8,128)(2,1)S(1)}, bf16[48,5120]{1,0:T(8,128)(2,1)S(1)}, u32[]{:S(2)}, u32[]{:S(2)}) collective-permute-start(bf16[48,5120]{1,0:T(8,128)(2,1)S(1)} %fusion.1), channel_id=1, source_target_pairs={{0,4},{1,5},{2,6},{3,7},{4,0},{5,1},{6,2},{7,3},{8,12},{9,13},{10,... | collective-permute-start | bytes 1474568 | tf_op jit(solution)/shard_map/ppermute | solution.py:437
  177.4 11.8 %collective-permute-start.32 = (bf16[48,5120]{1,0:T(8,128)(2,1)S(1)}, bf16[48,5120]{1,0:T(8,128)(2,1)S(1)}, u32[]{:S(2)}, u32[]{:S(2)}) collective-permute-start(bf16[48,5120]{1,0:T(8,128)(2,1)S(1)} %add_convert_fusion), channel_id=1, source_target_pairs={{4,8},{5,9},{6,10},{7,11},{8,4},{9,5},{10,6},{11,7},{20,24},{21,25... | collective-permute-start | bytes 1474568 | tf_op jit(solution)/shard_map/ppermute | solution.py:437
  180.2 8.9 %collective-permute-start.31 = (bf16[48,5120]{1,0:T(8,128)(2,1)S(1)}, bf16[48,5120]{1,0:T(8,128)(2,1)S(1)}, u32[]{:S(2)}, u32[]{:S(2)}) collective-permute-start(bf16[48,5120]{1,0:T(8,128)(2,1)S(1)} %slice.73), channel_id=1, source_target_pairs={{0,2},{1,3},{2,0},{3,1},{4,6},{5,7},{6,4},{7,5},{8,10},{9,11},{10,... | collective-permute-start | bytes 1474568 | tf_op jit(solution)/shard_map/ppermute | solution.py:437

commit v2 on v1

--- a/solution.py
+++ b/solution.py
@@ -453,14 +453,6 @@
     return (3 - z, y, c) if z in (1, 2) else None
 
 
-def to_ends(z, y, c):
-    return (z ^ 1, y, c) if z in (1, 2) else None
-
-
-def from_ends(z, y, c):
-    return (z ^ 1, y, c) if z in (0, 3) else None
-
-
 def slot_places(z):
     return (z, z + 1 - 2 * lax.rem(z, 2), jnp.where(z < 2, 2, 1), jnp.where(z < 2, 3, 0))
 
@@ -475,11 +467,11 @@
 
     near, second, own_y = lax.optimization_barrier((routed(own, to_near), routed(own, to_middle), routed(own, to_y)))
     own_pair = pair(own, own_y)
-    last, ends, near_y = lax.optimization_barrier((routed(near, to_middle), routed(second, to_ends), routed(near, to_y)))
+    last, ends, near_y = lax.optimization_barrier((routed(near, to_middle), routed(second, to_near), routed(near, to_y)))
     second = second + ends
     near_pair = pair(near, near_y)
     own_core = routed(behind(own_pair, ends), to_core)
-    ends, second_y = lax.optimization_barrier((routed(last, to_ends), routed(second, to_y)))
+    ends, second_y = lax.optimization_barrier((routed(last, to_near), routed(second, to_y)))
     last = last + ends
     second_pair = pair(second, second_y)
     near_core = routed(behind(near_pair, ends), to_core)
@@ -512,12 +504,12 @@
     far, second = met(kept[2], over[2])
     came, vectors = lax.optimization_barrier((came, vectors))
     came, last = routed(behind(far, came), to_y), last + came.astype(F32)
-    line = routed(low(last), from_ends)
+    line = routed(low(last), to_near)
     vectors = summed(2)
     far, near = met(kept[1], over[1])
     came, line, vectors = lax.optimization_barrier((came, line, vectors))
     last, second = last + line.astype(F32), second + came.astype(F32)
-    came, line, ends = routed(behind(far, came), to_y), routed(low(last), to_middle), routed(low(second), from_ends)
+    came, line, ends = routed(behind(far, came), to_y), routed(low(last), to_middle), routed(low(second), to_near)
     vectors = summed(4)
     far, own = met(kept[0], over[0])
     came, line, ends, vectors = lax.optimization_barrier((came, line, ends, vectors))

time: 193 us -> 189 us (0.979)
  starting transfers between devices: 42.6 us -> 34.5 us
  waiting for transfers between devices: 80.1 us -> 83.9 us
    ppermute x27, starting transfers between devices: 33 us -> 27.8 us  [routed(): return lax.ppermute(value, 'dp', pairs)]
    ppermute x27, waiting for transfers between devices: 70 us -> 73 us  [routed(): return lax.ppermute(value, 'dp', pairs)]
    ppermute x4, starting transfers between devices: 5.09 us -> 2.15 us  [summed(): lax.ppermute(vectors, 'dp', [(i, i ^ step) for i in range(4 * Z_CHIPS)])]
  transfers between devices with their start and end apart: 35 -> 35, of which waited for: 20 -> 21; matrix products, arithmetic and copies ran while one was open for 5% -> 5% of each run, Pallas kernels for 9% -> 10%
where the time goes in v2:
time: 189 us; the launch traced here: 186 us
  waiting for transfers between devices  83.9 us (44%)
  Pallas kernels  54.3 us (29%)
  starting transfers between devices  34.5 us (18%)
  other arithmetic  8.23 us (4%)
  local copies, waits for them, and re-layouts  3.61 us (2%)
    ppermute x27, waiting for transfers between devices, routed(): return lax.ppermute(value, 'dp', pairs)  73 us
    ppermute x27, starting transfers between devices, routed(): return lax.ppermute(value, 'dp', pairs)  27.8 us
    pallas_call x3, Pallas kernels, backward_layer(): pl.pallas_call(functools.partial(bwd_kernel, tuple((tuple((index for _, i...  26.5 us
    pallas_call x3, Pallas kernels, forward_layer(): pl.pallas_call(functools.partial(fwd_kernel, tuple((index for _, index in...  13.4 us
    ppermute x1, waiting for transfers between devices, shards(): r0 = lax.ppermute(f0[0], 'section', up)  5.45 us
    convert_element_type x6, other arithmetic, low(): return value.astype(BF16)  4.1 us
    ppermute x1, waiting for transfers between devices, shards(): d1 = lax.ppermute(b1[1], 'section', down)  3.89 us
  transfers between devices with their start and end apart: 35, of which 21 were waited for; matrix products, arithmetic and copies ran while one was open for 5% of the time, Pallas kernels for 10%

profile of v2, /device:TPU:8, one launch (start us, length us, event | category | flops | bytes accessed | tf_op | source)
XLA Modules:
  0.0 185.9 jit_solution(1600137289615915995)
XLA Ops:
  0.6 2.0 %pack_shard.1 = bf16[48,5120]{1,0:T(8,128)(2,1)} custom-call(bf16[48,3328]{1,0:T(8,128)(2,1)} %bitcast.40, bf16[96,768]{1,0:T(8,128)(2,1)} %bitcast.41, bf16[24,48]{1,0:T(8,128)(2,1)} %bitcast.42, bf16[4,112]{1,0:T(4,128)(2,1)} %bitcast.43, bf16[1,112]{1,0:T(2,128)(2,1)} %cb_ref.1, bf16[1,96]{1,0:T(2,128)(2,1)} %gg_ref.1, bf16[1,48]{1,0:T(2,128)(2,1)} %ng_ref.1), custom_call_target="tpu_custom_call" | custom-call | tf_op jit(solution)/shard_map/pack_shard/pallas_call | solution.py:413
  2.6 5.0 %collective-permute-start.1 = (bf16[48,5120]{1,0:T(8,128)(2,1)}, bf16[48,5120]{1,0:T(8,128)(2,1)S(1)}, u32[]{:S(2)}, u32[]{:S(2)}) collective-permute-start(bf16[48,5120]{1,0:T(8,128)(2,1)} %pack_shard.1), channel_id=1, source_target_pairs={{4,8},{5,9},{6,10},{7,11},{8,4},{9,5},{10,6},{11,7},{20,24},{21,25... | collective-permute-start | bytes 1474568 | tf_op jit(solution)/shard_map/ppermute | solution.py:437
  7.7 1.6 collective-permute-start.2
  9.2 6.5 %collective-permute-done = bf16[48,5120]{1,0:T(8,128)(2,1)S(1)} collective-permute-done((bf16[48,5120]{1,0:T(8,128)(2,1)}, bf16[48,5120]{1,0:T(8,128)(2,1)S(1)}, u32[]{:S(2)}, u32[]{:S(2)}) %collective-permute-start) | collective-permute-done | bytes 491552 | tf_op jit(solution)/shard_map/ppermute | solution.py:437
  15.8 3.0 %collective-permute-done.1 = bf16[48,5120]{1,0:T(8,128)(2,1)S(1)} collective-permute-done((bf16[48,5120]{1,0:T(8,128)(2,1)}, bf16[48,5120]{1,0:T(8,128)(2,1)S(1)}, u32[]{:S(2)}, u32[]{:S(2)}) %collective-permute-start.1) | collective-permute-done | bytes 491552 | tf_op jit(solution)/shard_map/ppermute | solution.py:437
  18.8 1.5 collective-permute-done.2
  20.3 2.2 %collective-permute-start.3 = (bf16[48,5120]{1,0:T(8,128)(2,1)S(1)}, bf16[48,5120]{1,0:T(8,128)(2,1)S(1)}, u32[]{:S(2)}, u32[]{:S(2)}) collective-permute-start(bf16[48,5120]{1,0:T(8,128)(2,1)S(1)} %collective-permute-done), channel_id=1, source_target_pairs={{4,8},{5,9},{6,10},{7,11},{8,4},{9,5},{10,6},{11,7},{20,24},{21,25... | collective-permute-start | bytes 1474568 | tf_op jit(solution)/shard_map/ppermute | solution.py:437
  22.5 1.6 collective-permute-start.5
  24.1 1.1 pad_maximum_fusion.refs_0_
  25.2 8.5 %collective-permute-done.3 = bf16[48,5120]{1,0:T(8,128)(2,1)S(1)} collective-permute-done((bf16[48,5120]{1,0:T(8,128)(2,1)S(1)}, bf16[48,5120]{1,0:T(8,128)(2,1)S(1)}, u32[]{:S(2)}, u32[]{:S(2)}) %collective-permute-start.3) | collective-permute-done | bytes 491552 | tf_op jit(solution)/shard_map/ppermute | solution.py:437
  34.1 1.2 collective-permute-done.4
  35.5 0.6 collective-permute-start.7
  36.3 0.8 constant_dynamic-update-slice_fusion.1
  37.1 0.8 constant_dynamic-update-slice_fusion.refs_1_
  38.0 8.6 %collective-permute-done.7 = bf16[48,5120]{1,0:T(8,128)(2,1)S(1)} collective-permute-done((bf16[48,5120]{1,0:T(8,128)(2,1)S(1)}, bf16[48,5120]{1,0:T(8,128)(2,1)S(1)}, u32[]{:S(2)}, u32[]{:S(2)}) %collective-permute-start.7) | collective-permute-done | bytes 491552 | tf_op jit(solution)/shard_map/ppermute | solution.py:437
  46.8 1.0 collective-permute-start.8
  47.9 0.6 collective-permute-start.11
  48.4 7.9 %collective-permute-done.8 = bf16[48,5120]{1,0:T(8,128)(2,1)S(1)} collective-permute-done((bf16[48,5120]{1,0:T(8,128)(2,1)S(1)}, bf16[48,5120]{1,0:T(8,128)(2,1)S(1)}, u32[]{:S(2)}, u32[]{:S(2)}) %collective-permute-start.8) | collective-permute-done | bytes 491552 | tf_op jit(solution)/shard_map/ppermute | solution.py:437
  56.9 2.3 %collective-permute-done.12.refs_7_ = bf16[96,5120]{1,0:T(8,128)(2,1)} collective-permute-done((bf16[96,5120]{1,0:T(8,128)(2,1)S(1)}, bf16[96,5120]{1,0:T(8,128)(2,1)}, u32[]{:S(2)}, u32[]{:S(2)}) %collective-permute-start.12) | collective-permute-done | bytes 983072 | tf_op jit(solution)/shard_map/ppermute | solution.py:437
  59.2 3.5 %settle_weights.1 = (bf16[768,3456]{1,0:T(8,128)(2,1)S(1)}, bf16[1536,768]{1,0:T(8,128)(2,1)S(1)}, f32[4,1792]{1,0:T(4,128)S(1)}, f32[1,1792]{1,0:T(1,128)S(1)},...) custom-call(s32[4]{0:T(128)S(1)} %pad_add_fusion.where_ref.which_ref, bf16[96,5120]{1,0:T(8,128)(2,1)S(1)} %pad_maximum_fusion.refs_0_, ...), custom_call_target="tpu_custom_call" | custom-call | tf_op jit(solution)/shard_map/settle_weights/pallas_call | solution.py:564
  62.7 4.5 %layer_forward.3 = (bf16[128,768]{1,0:T(8,128)(2,1)S(1)}, bf16[128,768]{1,0:T(8,128)(2,1)S(1)}, f32[128,3328]{1,0:T(8,128)S(1)}, f32[128,128]{1,0:T(8,128)S(1)},...) custom-call(s32[4]{0:T(128)S(1)} %pad_add_fusion.where_ref.which_ref, ...), custom_call_target="tpu_custom_call" | custom-call | tf_op jit(solution)/shard_map/layer_forward/pallas_call | solution.py:326
  67.2 1.6 collective-permute-start.13
  68.8 5.5 %collective-permute-done.13.refs_1_.refs_9_ = bf16[128,768]{1,0:T(8,128)(2,1)S(1)} collective-permute-done((bf16[128,768]{1,0:T(8,128)(2,1)S(1)}, bf16[128,768]{1,0:T(8,128)(2,1)S(1)}, u32[]{:S(2)}, u32[]{:S(2)}) %collective-permute-start.13) | collective-permute-done | bytes 196640 | tf_op jit(solution)/shard_map/ppermute | solution.py:801
  74.2 4.5 %layer_forward.4 = (bf16[128,768]{1,0:T(8,128)(2,1)S(1)}, bf16[128,768]{1,0:T(8,128)(2,1)S(1)}, f32[128,3328]{1,0:T(8,128)S(1)}, f32[128,128]{1,0:T(8,128)S(1)},...) custom-call(s32[4]{0:T(128)S(1)} %pad_add_fusion.where_ref.which_ref, ...), custom_call_target="tpu_custom_call" | custom-call | tf_op jit(solution)/shard_map/layer_forward/pallas_call | solution.py:326
  78.7 1.6 collective-permute-start.14
  80.3 8.9 %layer_backward.3 = (f32[128,768]{1,0:T(8,128)S(1)}, bf16[128,768]{1,0:T(8,128)(2,1)S(1)}, bf16[128,3328]{1,0:T(8,128)(2,1)S(1)}, bf16[128,128]{1,0:T(8,128)(2,1...) custom-call(s32[4]{0:T(128)S(1)} %pad_add_fusion.where_ref.which_ref, ...), custom_call_target="tpu_custom_call" | custom-call | tf_op jit(solution)/shard_map/layer_backward/pallas_call | solution.py:349
  89.2 0.6 collective-permute-start.15
  89.8 4.5 %layer_forward.5 = (bf16[128,768]{1,0:T(8,128)(2,1)S(1)}, bf16[128,768]{1,0:T(8,128)(2,1)S(1)}, f32[128,3328]{1,0:T(8,128)S(1)}, f32[128,128]{1,0:T(8,128)S(1)},...) custom-call(s32[4]{0:T(128)S(1)} %pad_add_fusion.where_ref.which_ref, ...), custom_call_target="tpu_custom_call" | custom-call | tf_op jit(solution)/shard_map/layer_forward/pallas_call | solution.py:326
  94.3 0.8 collective-permute-done.15.refs_0_.refs_1_
  95.1 8.5 %layer_backward.4 = (f32[128,768]{1,0:T(8,128)S(1)}, bf16[128,768]{1,0:T(8,128)(2,1)S(1)}, bf16[128,3328]{1,0:T(8,128)(2,1)S(1)}, bf16[128,128]{1,0:T(8,128)(2,1...) custom-call(s32[4]{0:T(128)S(1)} %pad_add_fusion.where_ref.which_ref, ...), custom_call_target="tpu_custom_call" | custom-call | tf_op jit(solution)/shard_map/layer_backward/pallas_call | solution.py:349
  103.6 0.8 collective-permute-start.16
  104.5 1.0 turn_rows.1
  105.5 3.9 %collective-permute-done.16.refs_0_.refs_4_ = bf16[128,768]{1,0:T(8,128)(2,1)S(1)} collective-permute-done((bf16[128,768]{1,0:T(8,128)(2,1)S(1)}, bf16[128,768]{1,0:T(8,128)(2,1)S(1)}, u32[]{:S(2)}, u32[]{:S(2)}) %collective-permute-start.16) | collective-permute-done | bytes 196640 | tf_op jit(solution)/shard_map/ppermute | solution.py:818
  109.4 9.1 %layer_backward.5 = (f32[128,768]{1,0:T(8,128)S(1)}, bf16[128,768]{1,0:T(8,128)(2,1)}, bf16[128,3328]{1,0:T(8,128)(2,1)S(1)}, bf16[128,128]{1,0:T(8,128)(2,1)S(1...) custom-call(s32[4]{0:T(128)S(1)} %pad_add_fusion.where_ref.which_ref, ...), custom_call_target="tpu_custom_call" | custom-call | tf_op jit(solution)/shard_map/layer_backward/pallas_call | solution.py:349
  118.5 3.4 %weight_gradients_first.1 = (bf16[48,5120]{1,0:T(8,128)(2,1)S(1)}, bf16[48,5120]{1,0:T(8,128)(2,1)S(1)}, bf16[48,5120]{1,0:T(8,128)(2,1)S(1)}, bf16[48,5120]{1,0...) custom-call(s32[4]{0:T(128)S(1)} %pad_add_fusion.where_ref.which_ref, ...), custom_call_target="tpu_custom_call" | custom-call | tf_op jit(solution)/shard_map/weight_gradients_first/pallas_call | solution.py:680
  122.1 1.9 collective-permute-done.17
  123.9 0.9 add_convert_fusion.2
  124.8 0.6 collective-permute-start.20
  125.9 1.0 copy-done.9
  126.9 3.4 %weight_gradients_rest.1 = (bf16[96,5120]{1,0:T(8,128)(2,1)S(1)}, bf16[96,5120]{1,0:T(8,128)(2,1)S(1)}, bf16[96,5120]{1,0:T(8,128)(2,1)S(1)}, bf16[96,5120]{1,0:...) custom-call(s32[4]{0:T(128)S(1)} %pad_add_fusion.where_ref.which_ref, ...), custom_call_target="tpu_custom_call" | custom-call | tf_op jit(solution)/shard_map/weight_gradients_rest/pallas_call | solution.py:691
  131.0 7.4 %collective-permute-done.20 = bf16[48,5120]{1,0:T(8,128)(2,1)} collective-permute-done((bf16[48,5120]{1,0:T(8,128)(2,1)}, bf16[48,5120]{1,0:T(8,128)(2,1)}, u32[]{:S(2)}, u32[]{:S(2)}) %collective-permute-start.20) | collective-permute-done | bytes 491552 | tf_op jit(solution)/shard_map/ppermute | solution.py:437
  138.4 0.6 collective-permute-start.25
  139.0 1.4 fusion.2
  140.3 0.9 collective-permute-start.24
  141.2 0.8 collective-permute-done.25
  142.3 0.6 collective-permute-start.22
  143.2 9.3 %collective-permute-done.24 = bf16[48,5120]{1,0:T(8,128)(2,1)S(1)} collective-permute-done((bf16[48,5120]{1,0:T(8,128)(2,1)S(1)}, bf16[48,5120]{1,0:T(8,128)(2,1)S(1)}, u32[]{:S(2)}, u32[]{:S(2)}) %collective-permute-start.24) | collective-permute-done | bytes 491552 | tf_op jit(solution)/shard_map/ppermute | solution.py:437
  152.5 1.1 collective-permute-done.22
  153.6 1.0 collective-permute-start.29
  154.7 1.1 collective-permute-start.28
  155.8 1.4 add_convert_fusion.1
  157.2 3.0 %collective-permute-start.27 = (bf16[48,5120]{1,0:T(8,128)(2,1)S(1)}, bf16[48,5120]{1,0:T(8,128)(2,1)S(1)}, u32[]{:S(2)}, u32[]{:S(2)}) collective-permute-start(bf16[48,5120]{1,0:T(8,128)(2,1)S(1)} %add_convert_fusion.1), channel_id=1, source_target_pairs={{4,8},{5,9},{6,10},{7,11},{8,4},{9,5},{10,6},{11,7},{20,24},{21,25... | collective-permute-start | bytes 1474568 | tf_op jit(solution)/shard_map/ppermute | solution.py:437
  160.3 1.1 collective-permute-start.26
  161.7 3.6 %collective-permute-done.28 = bf16[48,5120]{1,0:T(8,128)(2,1)S(1)} collective-permute-done((bf16[48,5120]{1,0:T(8,128)(2,1)S(1)}, bf16[48,5120]{1,0:T(8,128)(2,1)S(1)}, u32[]{:S(2)}, u32[]{:S(2)}) %collective-permute-start.28) | collective-permute-done | bytes 491552 | tf_op jit(solution)/shard_map/ppermute | solution.py:437
  165.4 3.7 %collective-permute-done.27 = bf16[48,5120]{1,0:T(8,128)(2,1)S(1)} collective-permute-done((bf16[48,5120]{1,0:T(8,128)(2,1)S(1)}, bf16[48,5120]{1,0:T(8,128)(2,1)S(1)}, u32[]{:S(2)}, u32[]{:S(2)}) %collective-permute-start.27) | collective-permute-done | bytes 491552 | tf_op jit(solution)/shard_map/ppermute | solution.py:437
  169.0 0.9 collective-permute-done.26
  170.2 2.3 %collective-permute-start.33 = (bf16[48,5120]{1,0:T(8,128)(2,1)S(1)}, bf16[48,5120]{1,0:T(8,128)(2,1)S(1)}, u32[]{:S(2)}, u32[]{:S(2)}) collective-permute-start(bf16[48,5120]{1,0:T(8,128)(2,1)S(1)} %fusion.1), channel_id=1, source_target_pairs={{0,4},{1,5},{2,6},{3,7},{4,0},{5,1},{6,2},{7,3},{8,12},{9,13},{10,... | collective-permute-start | bytes 1474568 | tf_op jit(solution)/shard_map/ppermute | solution.py:437
  172.7 3.0 %collective-permute-start.32 = (bf16[48,5120]{1,0:T(8,128)(2,1)S(1)}, bf16[48,5120]{1,0:T(8,128)(2,1)S(1)}, u32[]{:S(2)}, u32[]{:S(2)}) collective-permute-start(bf16[48,5120]{1,0:T(8,128)(2,1)S(1)} %add_convert_fusion), channel_id=1, source_target_pairs={{4,8},{5,9},{6,10},{7,11},{8,4},{9,5},{10,6},{11,7},{20,24},{21,25... | collective-permute-start | bytes 1474568 | tf_op jit(solution)/shard_map/ppermute | solution.py:437
  175.7 1.5 collective-permute-start.31
  177.4 0.9 maximum_bitcast_fusion
  178.3 0.8 maximum_bitcast_fusion.1
  179.1 0.5 fusion.4
  179.6 5.0 %collective-permute-done.31 = bf16[48,5120]{1,0:T(8,128)(2,1)S(1)} collective-permute-done((bf16[48,5120]{1,0:T(8,128)(2,1)S(1)}, bf16[48,5120]{1,0:T(8,128)(2,1)S(1)}, u32[]{:S(2)}, u32[]{:S(2)}) %collective-permute-start.31) | collective-permute-done | bytes 491552 | tf_op jit(solution)/shard_map/ppermute | solution.py:437
  184.7 1.0 unpack_sums.1
  (93 shorter events, 4.3 us)
Async XLA Ops:
  2.6 13.2 %collective-permute-start = (bf16[48,5120]{1,0:T(8,128)(2,1)}, bf16[48,5120]{1,0:T(8,128)(2,1)S(1)}, u32[]{:S(2)}, u32[]{:S(2)}) collective-permute-start(bf16[48,5120]{1,0:T(8,128)(2,1)} %pack_shard.1), channel_id=1, source_target_pairs={{0,4},{1,5},{2,6},{3,7},{4,0},{5,1},{6,2},{7,3},{8,12},{9,13},{10,... | collective-permute-start | bytes 1474568 | tf_op jit(solution)/shard_map/ppermute | solution.py:437
  2.6 16.2 %collective-permute-start.1 = (bf16[48,5120]{1,0:T(8,128)(2,1)}, bf16[48,5120]{1,0:T(8,128)(2,1)S(1)}, u32[]{:S(2)}, u32[]{:S(2)}) collective-permute-start(bf16[48,5120]{1,0:T(8,128)(2,1)} %pack_shard.1), channel_id=1, source_target_pairs={{4,8},{5,9},{6,10},{7,11},{8,4},{9,5},{10,6},{11,7},{20,24},{21,25... | collective-permute-start | bytes 1474568 | tf_op jit(solution)/shard_map/ppermute | solution.py:437
  7.7 12.7 %collective-permute-start.2 = (bf16[48,5120]{1,0:T(8,128)(2,1)}, bf16[48,5120]{1,0:T(8,128)(2,1)S(1)}, u32[]{:S(2)}, u32[]{:S(2)}) collective-permute-start(bf16[48,5120]{1,0:T(8,128)(2,1)} %pack_shard.1), channel_id=1, source_target_pairs={{0,2},{1,3},{2,0},{3,1},{4,6},{5,7},{6,4},{7,5},{8,10},{9,11},{10,... | collective-permute-start | bytes 1474568 | tf_op jit(solution)/shard_map/ppermute | solution.py:437
  20.3 13.4 %collective-permute-start.3 = (bf16[48,5120]{1,0:T(8,128)(2,1)S(1)}, bf16[48,5120]{1,0:T(8,128)(2,1)S(1)}, u32[]{:S(2)}, u32[]{:S(2)}) collective-permute-start(bf16[48,5120]{1,0:T(8,128)(2,1)S(1)} %collective-permute-done), channel_id=1, source_target_pairs={{4,8},{5,9},{6,10},{7,11},{8,4},{9,5},{10,6},{11,7},{20,24},{21,25... | collective-permute-start | bytes 1474568 | tf_op jit(solution)/shard_map/ppermute | solution.py:437
  22.5 11.6 %collective-permute-start.5 = (bf16[48,5120]{1,0:T(8,128)(2,1)S(1)}, bf16[48,5120]{1,0:T(8,128)(2,1)S(1)}, u32[]{:S(2)}, u32[]{:S(2)}) collective-permute-start(bf16[48,5120]{1,0:T(8,128)(2,1)S(1)} %collective-permute-done), channel_id=1, source_target_pairs={{0,2},{1,3},{2,0},{3,1},{4,6},{5,7},{6,4},{7,5},{8,10},{9,11},{10,... | collective-permute-start | bytes 1474568 | tf_op jit(solution)/shard_map/ppermute | solution.py:437
  24.1 11.2 %collective-permute-start.4 = (bf16[48,5120]{1,0:T(8,128)(2,1)S(1)}, bf16[48,5120]{1,0:T(8,128)(2,1)S(1)}, u32[]{:S(2)}, u32[]{:S(2)}) collective-permute-start(bf16[48,5120]{1,0:T(8,128)(2,1)S(1)} %collective-permute-done.1), channel_id=1, source_target_pairs={{0,4},{1,5},{2,6},{3,7},{4,0},{5,1},{6,2},{7,3},{8,12},{9,13},{10,... | collective-permute-start | bytes 1474568 | tf_op jit(solution)/shard_map/ppermute | solution.py:437
  35.5 11.2 %collective-permute-start.7 = (bf16[48,5120]{1,0:T(8,128)(2,1)S(1)}, bf16[48,5120]{1,0:T(8,128)(2,1)S(1)}, u32[]{:S(2)}, u32[]{:S(2)}) collective-permute-start(bf16[48,5120]{1,0:T(8,128)(2,1)S(1)} %add.67), channel_id=1, source_target_pairs={{0,2},{1,3},{2,0},{3,1},{4,6},{5,7},{6,4},{7,5},{8,10},{9,11},{10,... | collective-permute-start | bytes 1474568 | tf_op jit(solution)/shard_map/ppermute | solution.py:437
  36.0 10.6 %collective-permute-start.6 = (bf16[48,5120]{1,0:T(8,128)(2,1)S(1)}, bf16[48,5120]{1,0:T(8,128)(2,1)S(1)}, u32[]{:S(2)}, u32[]{:S(2)}) collective-permute-start(bf16[48,5120]{1,0:T(8,128)(2,1)S(1)} %collective-permute-done.3), channel_id=1, source_target_pairs={{0,4},{1,5},{2,6},{3,7},{4,0},{5,1},{6,2},{7,3},{8,12},{9,13},{10,... | collective-permute-start | bytes 1474568 | tf_op jit(solution)/shard_map/ppermute | solution.py:437
  37.1 19.7 %collective-permute-start.9 = (bf16[96,5120]{1,0:T(8,128)(2,1)S(1)}, bf16[96,5120]{1,0:T(8,128)(2,1)}, u32[]{:S(2)}, u32[]{:S(2)}) collective-permute-start(bf16[96,5120]{1,0:T(8,128)(2,1)S(1)} %pad_maximum_fusion.refs_0_), channel_id=1, source_target_pairs={{0,1},{1,0},{2,3},{3,2},{4,5},{5,4},{6,7},{7,6},{8,9},{9,8},{10,11... | collective-permute-start | bytes 2949128 | tf_op jit(solution)/shard_map/ppermute | solution.py:437
  46.7 9.8 %copy-start.17 = (f32[1,24]{1,0:T(1,128)S(1)}, f32[1,24]{1,0:T(1,128)}, u32[]{:S(2)}) copy-start(f32[1,24]{1,0:T(1,128)} %param.23) | copy-start | bytes 292
  46.7 10.0 %copy-start.16 = (s32[2,128]{1,0:T(2,128)S(1)}, s32[2,128]{1,0:T(2,128)}, u32[]{:S(2)}) copy-start(s32[2,128]{1,0:T(2,128)} %param.14) | copy-start | bytes 3076
  46.8 10.1 %copy-start.18 = (f32[1,24]{1,0:T(1,128)S(1)}, f32[1,24]{1,0:T(1,128)}, u32[]{:S(2)}) copy-start(f32[1,24]{1,0:T(1,128)} %param.22) | copy-start | bytes 292
  46.8 10.0 %copy-start.19 = (f32[1,24]{1,0:T(1,128)S(1)}, f32[1,24]{1,0:T(1,128)}, u32[]{:S(2)}) copy-start(f32[1,24]{1,0:T(1,128)} %param.21) | copy-start | bytes 292
  46.8 9.6 %collective-permute-start.8 = (bf16[48,5120]{1,0:T(8,128)(2,1)S(1)}, bf16[48,5120]{1,0:T(8,128)(2,1)S(1)}, u32[]{:S(2)}, u32[]{:S(2)}) collective-permute-start(bf16[48,5120]{1,0:T(8,128)(2,1)S(1)} %add.68), channel_id=1, source_target_pairs={{0,2},{1,3},{2,0},{3,1},{4,6},{5,7},{6,4},{7,5},{8,10},{9,11},{10,... | collective-permute-start | bytes 1474568 | tf_op jit(solution)/shard_map/ppermute | solution.py:437
  47.8 9.1 %collective-permute-start.10 = (bf16[96,5120]{1,0:T(8,128)(2,1)}, bf16[96,5120]{1,0:T(8,128)(2,1)}, u32[]{:S(2)}, u32[]{:S(2)}) collective-permute-start(bf16[96,5120]{1,0:T(8,128)(2,1)} %constant_dynamic-update-slice_fusion.refs_1_), channel_id=1, source_target_pairs={{0,1},{1,0},{2,3},{3,2},{4,5},{5,4},{6,7},{7,6},{8,9},{9,8},{10,11... | collective-permute-start | bytes 2949128 | tf_op jit(solution)/shard_map/ppermute | solution.py:437
  47.9 9.0 %collective-permute-start.11 = (bf16[96,5120]{1,0:T(8,128)(2,1)S(1)}, bf16[96,5120]{1,0:T(8,128)(2,1)}, u32[]{:S(2)}, u32[]{:S(2)}) collective-permute-start(bf16[96,5120]{1,0:T(8,128)(2,1)S(1)} %pad_maximum_fusion.1.refs_2_), channel_id=1, source_target_pairs={{0,1},{1,0},{2,3},{3,2},{4,5},{5,4},{6,7},{7,6},{8,9},{9,8},{10,11... | collective-permute-start | bytes 2949128 | tf_op jit(solution)/shard_map/ppermute | solution.py:437
  56.4 2.8 %collective-permute-start.12 = (bf16[96,5120]{1,0:T(8,128)(2,1)S(1)}, bf16[96,5120]{1,0:T(8,128)(2,1)}, u32[]{:S(2)}, u32[]{:S(2)}) collective-permute-start(bf16[96,5120]{1,0:T(8,128)(2,1)S(1)} %pad_maximum_fusion.2.refs_3_), channel_id=1, source_target_pairs={{0,1},{1,0},{2,3},{3,2},{4,5},{5,4},{6,7},{7,6},{8,9},{9,8},{10,11... | collective-permute-start | bytes 2949128 | tf_op jit(solution)/shard_map/ppermute | solution.py:437
  56.8 5.9 %copy-start = (bf16[2,128,768]{2,1,0:T(8,128)(2,1)S(1)}, bf16[2,128,768]{2,1,0:T(8,128)(2,1)}, u32[]{:S(2)}) copy-start(bf16[2,128,768]{2,1,0:T(8,128)(2,1)} %refs_1_.5) | copy-start | bytes 1179652
  67.2 11.5 %copy-start.10 = (bf16[128,768]{1,0:T(8,128)(2,1)}, bf16[128,768]{1,0:T(8,128)(2,1)S(1)}, u32[]{:S(2)}) copy-start(bf16[128,768]{1,0:T(8,128)(2,1)S(1)} %get-tuple-element.217) | copy-start | bytes 589828
  67.2 13.1 %copy-start.1 = (bf16[2,128,768]{2,1,0:T(8,128)(2,1)S(1)}, bf16[2,128,768]{2,1,0:T(8,128)(2,1)}, u32[]{:S(2)}) copy-start(bf16[2,128,768]{2,1,0:T(8,128)(2,1)} %refs_8_.3) | copy-start | bytes 1179652
  67.2 7.0 %collective-permute-start.13 = (bf16[128,768]{1,0:T(8,128)(2,1)S(1)}, bf16[128,768]{1,0:T(8,128)(2,1)S(1)}, u32[]{:S(2)}, u32[]{:S(2)}) collective-permute-start(bf16[128,768]{1,0:T(8,128)(2,1)S(1)} %get-tuple-element.217), channel_id=1, source_target_pairs={{0,16},{16,0},{1,17},{17,1},{2,18},{18,2},{3,19},{19,3},{4,20},{20... | collective-permute-start | bytes 589832 | tf_op jit(solution)/shard_map/ppermute | solution.py:801
  78.7 10.5 %copy-start.12 = (bf16[128,768]{1,0:T(8,128)(2,1)}, bf16[128,768]{1,0:T(8,128)(2,1)S(1)}, u32[]{:S(2)}) copy-start(bf16[128,768]{1,0:T(8,128)(2,1)S(1)} %get-tuple-element.218) | copy-start | bytes 589828
  78.7 11.1 %collective-permute-start.14 = (bf16[128,768]{1,0:T(8,128)(2,1)S(1)}, bf16[128,768]{1,0:T(8,128)(2,1)S(1)}, u32[]{:S(2)}, u32[]{:S(2)}) collective-permute-start(bf16[128,768]{1,0:T(8,128)(2,1)S(1)} %get-tuple-element.218), channel_id=1, source_target_pairs={{0,16},{16,0},{1,17},{17,1},{2,18},{18,2},{3,19},{19,3},{4,20},{20... | collective-permute-start | bytes 589832 | tf_op jit(solution)/shard_map/ppermute | solution.py:803
  89.2 5.1 %copy-start.2 = (f32[128,768]{1,0:T(8,128)}, f32[128,768]{1,0:T(8,128)S(1)}, u32[]{:S(2)}) copy-start(f32[128,768]{1,0:T(8,128)S(1)} %get-tuple-element.221) | copy-start | bytes 1179652
  89.2 5.9 %collective-permute-start.15 = (bf16[128,768]{1,0:T(8,128)(2,1)S(1)}, bf16[128,768]{1,0:T(8,128)(2,1)S(1)}, u32[]{:S(2)}, u32[]{:S(2)}) collective-permute-start(bf16[128,768]{1,0:T(8,128)(2,1)S(1)} %get-tuple-element.150), channel_id=1, source_target_pairs={{0,16},{16,0},{1,17},{17,1},{2,18},{18,2},{3,19},{19,3},{4,20},{20... | collective-permute-start | bytes 589832 | tf_op jit(solution)/shard_map/ppermute | solution.py:812
  94.3 9.3 %copy-start.14 = (bf16[128,768]{1,0:T(8,128)(2,1)}, bf16[128,768]{1,0:T(8,128)(2,1)S(1)}, u32[]{:S(2)}) copy-start(bf16[128,768]{1,0:T(8,128)(2,1)S(1)} %get-tuple-element.219) | copy-start | bytes 589828
  103.6 14.9 %copy-start.4 = (f32[128,768]{1,0:T(8,128)}, f32[128,768]{1,0:T(8,128)S(1)}, u32[]{:S(2)}) copy-start(f32[128,768]{1,0:T(8,128)S(1)} %get-tuple-element.220) | copy-start | bytes 1179652
  103.6 5.7 %collective-permute-start.16 = (bf16[128,768]{1,0:T(8,128)(2,1)S(1)}, bf16[128,768]{1,0:T(8,128)(2,1)S(1)}, u32[]{:S(2)}, u32[]{:S(2)}) collective-permute-start(bf16[128,768]{1,0:T(8,128)(2,1)S(1)} %get-tuple-element.164), channel_id=1, source_target_pairs={{0,16},{16,0},{1,17},{17,1},{2,18},{18,2},{3,19},{19,3},{4,20},{20... | collective-permute-start | bytes 589832 | tf_op jit(solution)/shard_map/ppermute | solution.py:818
  118.5 3.5 %copy-start.6 = (f32[128,768]{1,0:T(8,128)}, f32[128,768]{1,0:T(8,128)S(1)}, u32[]{:S(2)}) copy-start(f32[128,768]{1,0:T(8,128)S(1)} %get-tuple-element.222) | copy-start | bytes 1179652
  122.0 2.8 %copy-start.8 = (bf16[256,768]{1,0:T(8,128)(2,1)}, bf16[256,768]{1,0:T(8,128)(2,1)S(1)}, u32[]{:S(2)}) copy-start(bf16[256,768]{1,0:T(8,128)(2,1)S(1)} %get-tuple-element.197.gb_ref) | copy-start | bytes 1179652
  122.0 1.9 %collective-permute-start.17 = (bf16[48,5120]{1,0:T(8,128)(2,1)S(1)}, bf16[48,5120]{1,0:T(8,128)(2,1)S(1)}, u32[]{:S(2)}, u32[]{:S(2)}) collective-permute-start(bf16[48,5120]{1,0:T(8,128)(2,1)S(1)} %get-tuple-element.195), channel_id=1, source_target_pairs={{0,1},{1,0},{2,3},{3,2},{4,5},{5,4},{6,7},{7,6},{8,9},{9,8},{10,11... | collective-permute-start | bytes 1474568 | tf_op jit(solution)/shard_map/ppermute | solution.py:437
  124.8 13.6 %collective-permute-start.20 = (bf16[48,5120]{1,0:T(8,128)(2,1)}, bf16[48,5120]{1,0:T(8,128)(2,1)}, u32[]{:S(2)}, u32[]{:S(2)}) collective-permute-start(bf16[48,5120]{1,0:T(8,128)(2,1)} %add_convert_fusion.2), channel_id=1, source_target_pairs={{0,2},{1,3},{2,0},{3,1},{4,6},{5,7},{6,4},{7,5},{8,10},{9,11},{10,... | collective-permute-start | bytes 1474568 | tf_op jit(solution)/shard_map/ppermute | solution.py:437
  125.4 13.6 %collective-permute-start.23 = (bf16[48,5120]{1,0:T(8,128)(2,1)}, bf16[48,5120]{1,0:T(8,128)(2,1)}, u32[]{:S(2)}, u32[]{:S(2)}) collective-permute-start(bf16[48,5120]{1,0:T(8,128)(2,1)} %get-tuple-element.210), channel_id=1, source_target_pairs={{0,1},{1,0},{2,3},{3,2},{4,5},{5,4},{6,7},{7,6},{8,9},{9,8},{10,11... | collective-permute-start | bytes 1474568 | tf_op jit(solution)/shard_map/ppermute | solution.py:437
  125.4 5.5 %collective-permute-start.21 = (f32[8,128]{1,0:T(8,128)S(1)}, f32[8,128]{1,0:T(8,128)S(1)}, u32[]{:S(2)}, u32[]{:S(2)}) collective-permute-start(f32[8,128]{1,0:T(8,128)S(1)} %get-tuple-element.205), channel_id=1, source_target_pairs={{0,1},{1,0},{2,3},{3,2},{4,5},{5,4},{6,7},{7,6},{8,9},{9,8},{10,11... | collective-permute-start | bytes 12296 | tf_op jit(solution)/shard_map/ppermute | solution.py:494
  125.9 1.0 copy-start.9
  130.3 11.7 %collective-permute-start.19 = (bf16[96,5120]{1,0:T(8,128)(2,1)S(1)}, bf16[96,5120]{1,0:T(8,128)(2,1)S(1)}, u32[]{:S(2)}, u32[]{:S(2)}) collective-permute-start(bf16[96,5120]{1,0:T(8,128)(2,1)S(1)} %get-tuple-element.203), channel_id=1, source_target_pairs={{0,1},{1,0},{2,3},{3,2},{4,5},{5,4},{6,7},{7,6},{8,9},{9,8},{10,11... | collective-permute-start | bytes 2949128 | tf_op jit(solution)/shard_map/ppermute | solution.py:437
  130.4 12.5 %collective-permute-start.18 = (bf16[96,5120]{1,0:T(8,128)(2,1)S(1)}, bf16[96,5120]{1,0:T(8,128)(2,1)S(1)}, u32[]{:S(2)}, u32[]{:S(2)}) collective-permute-start(bf16[96,5120]{1,0:T(8,128)(2,1)S(1)} %get-tuple-element.201), channel_id=1, source_target_pairs={{0,1},{1,0},{2,3},{3,2},{4,5},{5,4},{6,7},{7,6},{8,9},{9,8},{10,11... | collective-permute-start | bytes 2949128 | tf_op jit(solution)/shard_map/ppermute | solution.py:437
  130.9 30.5 %collective-permute-start.30 = (bf16[96,5120]{1,0:T(8,128)(2,1)S(1)}, bf16[96,5120]{1,0:T(8,128)(2,1)S(1)}, u32[]{:S(2)}, u32[]{:S(2)}) collective-permute-start(bf16[96,5120]{1,0:T(8,128)(2,1)S(1)} %get-tuple-element.224), channel_id=1, source_target_pairs={{0,1},{1,0},{2,3},{3,2},{4,5},{5,4},{6,7},{7,6},{8,9},{9,8},{10,11... | collective-permute-start | bytes 2949128 | tf_op jit(solution)/shard_map/ppermute | solution.py:437
  138.4 3.6 %collective-permute-start.25 = (f32[8,128]{1,0:T(8,128)S(1)}, f32[8,128]{1,0:T(8,128)S(1)}, u32[]{:S(2)}, u32[]{:S(2)}) collective-permute-start(f32[8,128]{1,0:T(8,128)S(1)} %add.72), channel_id=1, source_target_pairs={{0,2},{1,3},{2,0},{3,1},{4,6},{5,7},{6,4},{7,5},{8,10},{9,11},{10,... | collective-permute-start | bytes 12296 | tf_op jit(solution)/shard_map/ppermute | solution.py:494
  140.3 12.2 %collective-permute-start.24 = (bf16[48,5120]{1,0:T(8,128)(2,1)S(1)}, bf16[48,5120]{1,0:T(8,128)(2,1)S(1)}, u32[]{:S(2)}, u32[]{:S(2)}) collective-permute-start(bf16[48,5120]{1,0:T(8,128)(2,1)S(1)} %fusion.2), channel_id=1, source_target_pairs={{0,4},{1,5},{2,6},{3,7},{4,0},{5,1},{6,2},{7,3},{8,12},{9,13},{10,... | collective-permute-start | bytes 1474568 | tf_op jit(solution)/shard_map/ppermute | solution.py:437
  142.3 11.4 %collective-permute-start.22 = (bf16[48,5120]{1,0:T(8,128)(2,1)S(1)}, bf16[48,5120]{1,0:T(8,128)(2,1)S(1)}, u32[]{:S(2)}, u32[]{:S(2)}) collective-permute-start(bf16[48,5120]{1,0:T(8,128)(2,1)S(1)} %slice.74), channel_id=1, source_target_pairs={{0,2},{1,3},{2,0},{3,1},{4,6},{5,7},{6,4},{7,5},{8,10},{9,11},{10,... | collective-permute-start | bytes 1474568 | tf_op jit(solution)/shard_map/ppermute | solution.py:437
  153.6 8.0 %collective-permute-start.29 = (f32[8,128]{1,0:T(8,128)S(1)}, f32[8,128]{1,0:T(8,128)S(1)}, u32[]{:S(2)}, u32[]{:S(2)}) collective-permute-start(f32[8,128]{1,0:T(8,128)S(1)} %add.75), channel_id=1, source_target_pairs={{0,4},{1,5},{2,6},{3,7},{4,0},{5,1},{6,2},{7,3},{8,12},{9,13},{10,... | collective-permute-start | bytes 12296 | tf_op jit(solution)/shard_map/ppermute | solution.py:494
  154.7 10.6 %collective-permute-start.28 = (bf16[48,5120]{1,0:T(8,128)(2,1)S(1)}, bf16[48,5120]{1,0:T(8,128)(2,1)S(1)}, u32[]{:S(2)}, u32[]{:S(2)}) collective-permute-start(bf16[48,5120]{1,0:T(8,128)(2,1)S(1)} %fusion.3), channel_id=1, source_target_pairs={{0,4},{1,5},{2,6},{3,7},{4,0},{5,1},{6,2},{7,3},{8,12},{9,13},{10,... | collective-permute-start | bytes 1474568 | tf_op jit(solution)/shard_map/ppermute | solution.py:437
  157.2 11.8 %collective-permute-start.27 = (bf16[48,5120]{1,0:T(8,128)(2,1)S(1)}, bf16[48,5120]{1,0:T(8,128)(2,1)S(1)}, u32[]{:S(2)}, u32[]{:S(2)}) collective-permute-start(bf16[48,5120]{1,0:T(8,128)(2,1)S(1)} %add_convert_fusion.1), channel_id=1, source_target_pairs={{4,8},{5,9},{6,10},{7,11},{8,4},{9,5},{10,6},{11,7},{20,24},{21,25... | collective-permute-start | bytes 1474568 | tf_op jit(solution)/shard_map/ppermute | solution.py:437
  160.3 9.6 %collective-permute-start.26 = (bf16[48,5120]{1,0:T(8,128)(2,1)S(1)}, bf16[48,5120]{1,0:T(8,128)(2,1)S(1)}, u32[]{:S(2)}, u32[]{:S(2)}) collective-permute-start(bf16[48,5120]{1,0:T(8,128)(2,1)S(1)} %slice.75), channel_id=1, source_target_pairs={{0,2},{1,3},{2,0},{3,1},{4,6},{5,7},{6,4},{7,5},{8,10},{9,11},{10,... | collective-permute-start | bytes 1474568 | tf_op jit(solution)/shard_map/ppermute | solution.py:437
  161.7 15.5 %copy-start.3 = (f32[128,768]{1,0:T(8,128)S(1)}, f32[128,768]{1,0:T(8,128)}, u32[]{:S(2)}) copy-start(f32[128,768]{1,0:T(8,128)} %copy-done.2) | copy-start | bytes 1179652
  161.7 15.5 %copy-start.5 = (f32[128,768]{1,0:T(8,128)S(1)}, f32[128,768]{1,0:T(8,128)}, u32[]{:S(2)}) copy-start(f32[128,768]{1,0:T(8,128)} %copy-done.4) | copy-start | bytes 1179652
  161.7 15.5 %copy-start.7 = (f32[128,768]{1,0:T(8,128)S(1)}, f32[128,768]{1,0:T(8,128)}, u32[]{:S(2)}) copy-start(f32[128,768]{1,0:T(8,128)} %copy-done.6) | copy-start | bytes 1179652
  169.9 9.2 %collective-permute-start.34 = (f32[8,128]{1,0:T(8,128)S(1)}, f32[8,128]{1,0:T(8,128)S(1)}, u32[]{:S(2)}, u32[]{:S(2)}) collective-permute-start(f32[8,128]{1,0:T(8,128)S(1)} %add.78), channel_id=1, source_target_pairs={{0,8},{1,9},{2,10},{3,11},{4,12},{5,13},{6,14},{7,15},{8,0},{9,1},... | collective-permute-start | bytes 12296 | tf_op jit(solution)/shard_map/ppermute | solution.py:494
  170.1 7.1 %copy-start.11 = (bf16[128,768]{1,0:T(8,128)(2,1)S(1)}, bf16[128,768]{1,0:T(8,128)(2,1)}, u32[]{:S(2)}) copy-start(bf16[128,768]{1,0:T(8,128)(2,1)} %copy-done.10) | copy-start | bytes 589828
  170.2 7.1 %copy-start.13 = (bf16[128,768]{1,0:T(8,128)(2,1)S(1)}, bf16[128,768]{1,0:T(8,128)(2,1)}, u32[]{:S(2)}) copy-start(bf16[128,768]{1,0:T(8,128)(2,1)} %copy-done.12) | copy-start | bytes 589828
  170.2 7.1 %copy-start.15 = (bf16[128,768]{1,0:T(8,128)(2,1)S(1)}, bf16[128,768]{1,0:T(8,128)(2,1)}, u32[]{:S(2)}) copy-start(bf16[128,768]{1,0:T(8,128)(2,1)} %copy-done.14) | copy-start | bytes 589828
  170.2 14.5 %collective-permute-start.33 = (bf16[48,5120]{1,0:T(8,128)(2,1)S(1)}, bf16[48,5120]{1,0:T(8,128)(2,1)S(1)}, u32[]{:S(2)}, u32[]{:S(2)}) collective-permute-start(bf16[48,5120]{1,0:T(8,128)(2,1)S(1)} %fusion.1), channel_id=1, source_target_pairs={{0,4},{1,5},{2,6},{3,7},{4,0},{5,1},{6,2},{7,3},{8,12},{9,13},{10,... | collective-permute-start | bytes 1474568 | tf_op jit(solution)/shard_map/ppermute | solution.py:437
  172.7 12.0 %collective-permute-start.32 = (bf16[48,5120]{1,0:T(8,128)(2,1)S(1)}, bf16[48,5120]{1,0:T(8,128)(2,1)S(1)}, u32[]{:S(2)}, u32[]{:S(2)}) collective-permute-start(bf16[48,5120]{1,0:T(8,128)(2,1)S(1)} %add_convert_fusion), channel_id=1, source_target_pairs={{4,8},{5,9},{6,10},{7,11},{8,4},{9,5},{10,6},{11,7},{20,24},{21,25... | collective-permute-start | bytes 1474568 | tf_op jit(solution)/shard_map/ppermute | solution.py:437
  175.7 8.9 %collective-permute-start.31 = (bf16[48,5120]{1,0:T(8,128)(2,1)S(1)}, bf16[48,5120]{1,0:T(8,128)(2,1)S(1)}, u32[]{:S(2)}, u32[]{:S(2)}) collective-permute-start(bf16[48,5120]{1,0:T(8,128)(2,1)S(1)} %slice.73), channel_id=1, source_target_pairs={{0,2},{1,3},{2,0},{3,1},{4,6},{5,7},{6,4},{7,5},{8,10},{9,11},{10,... | collective-permute-start | bytes 1474568 | tf_op jit(solution)/shard_map/ppermute | solution.py:437

commit v3 on v2

--- a/solution.py
+++ b/solution.py
@@ -516,7 +516,9 @@
     near, second = near + came.astype(F32) + line.astype(F32), second + ends.astype(F32)
     started = came
     came = routed(behind(far, came), to_y)
-    near, second = routed(low(near), to_near), routed(low(second), to_middle)
+    near = low(near)
+    vectors = behind(vectors, near)
+    near, second = routed(near, to_near), routed(low(second), to_middle)
     vectors = summed(8)
     return (own + came.astype(F32), second, near), vectors, started
 

time: 189 us -> 189 us (level)
    ppermute x27, starting transfers between devices: 27.8 us -> 25.5 us  [routed(): return lax.ppermute(value, 'dp', pairs)]
    ppermute x4, starting transfers between devices: 2.15 us -> 4.41 us  [summed(): lax.ppermute(vectors, 'dp', [(i, i ^ step) for i in range(4 * Z_CHIPS)])]
  transfers between devices with their start and end apart: 35 -> 35, of which waited for: 21 -> 22; matrix products, arithmetic and copies ran while one was open for 5% -> 5% of each run, Pallas kernels for 10% -> 10%
where the time goes in v3:
time: 189 us; the launch traced here: 186 us
  waiting for transfers between devices  83.9 us (44%)
  Pallas kernels  54.3 us (29%)
  starting transfers between devices  34.4 us (18%)
  other arithmetic  8.23 us (4%)
  local copies, waits for them, and re-layouts  3.61 us (2%)
    ppermute x27, waiting for transfers between devices, routed(): return lax.ppermute(value, 'dp', pairs)  72.6 us
    pallas_call x3, Pallas kernels, backward_layer(): pl.pallas_call(functools.partial(bwd_kernel, tuple((tuple((index for _, i...  26.5 us
    ppermute x27, starting transfers between devices, routed(): return lax.ppermute(value, 'dp', pairs)  25.5 us
    pallas_call x3, Pallas kernels, forward_layer(): pl.pallas_call(functools.partial(fwd_kernel, tuple((index for _, index in...  13.4 us
    ppermute x1, waiting for transfers between devices, shards(): r0 = lax.ppermute(f0[0], 'section', up)  5.45 us
    ppermute x4, starting transfers between devices, summed(): lax.ppermute(vectors, 'dp', [(i, i ^ step) for i in range(4 * Z_CHIPS)])  4.41 us
    convert_element_type x6, other arithmetic, low(): return value.astype(BF16)  4.1 us
    ppermute x1, waiting for transfers between devices, shards(): d1 = lax.ppermute(b1[1], 'section', down)  3.89 us
  transfers between devices with their start and end apart: 35, of which 22 were waited for; matrix products, arithmetic and copies ran while one was open for 5% of the time, Pallas kernels for 10%

profile of v3, /device:TPU:8, one launch (start us, length us, event | category | flops | bytes accessed | tf_op | source)
XLA Modules:
  0.0 185.9 jit_solution(16630741659524902273)
XLA Ops:
  0.6 2.0 %pack_shard.1 = bf16[48,5120]{1,0:T(8,128)(2,1)} custom-call(bf16[48,3328]{1,0:T(8,128)(2,1)} %bitcast.40, bf16[96,768]{1,0:T(8,128)(2,1)} %bitcast.41, bf16[24,48]{1,0:T(8,128)(2,1)} %bitcast.42, bf16[4,112]{1,0:T(4,128)(2,1)} %bitcast.43, bf16[1,112]{1,0:T(2,128)(2,1)} %cb_ref.1, bf16[1,96]{1,0:T(2,128)(2,1)} %gg_ref.1, bf16[1,48]{1,0:T(2,128)(2,1)} %ng_ref.1), custom_call_target="tpu_custom_call" | custom-call | tf_op jit(solution)/shard_map/pack_shard/pallas_call | solution.py:413
  2.6 5.0 %collective-permute-start.1 = (bf16[48,5120]{1,0:T(8,128)(2,1)}, bf16[48,5120]{1,0:T(8,128)(2,1)S(1)}, u32[]{:S(2)}, u32[]{:S(2)}) collective-permute-start(bf16[48,5120]{1,0:T(8,128)(2,1)} %pack_shard.1), channel_id=1, source_target_pairs={{4,8},{5,9},{6,10},{7,11},{8,4},{9,5},{10,6},{11,7},{20,24},{21,25... | collective-permute-start | bytes 1474568 | tf_op jit(solution)/shard_map/ppermute | solution.py:437
  7.7 1.6 collective-permute-start.2
  9.2 6.5 %collective-permute-done = bf16[48,5120]{1,0:T(8,128)(2,1)S(1)} collective-permute-done((bf16[48,5120]{1,0:T(8,128)(2,1)}, bf16[48,5120]{1,0:T(8,128)(2,1)S(1)}, u32[]{:S(2)}, u32[]{:S(2)}) %collective-permute-start) | collective-permute-done | bytes 491552 | tf_op jit(solution)/shard_map/ppermute | solution.py:437
  15.8 3.0 %collective-permute-done.1 = bf16[48,5120]{1,0:T(8,128)(2,1)S(1)} collective-permute-done((bf16[48,5120]{1,0:T(8,128)(2,1)}, bf16[48,5120]{1,0:T(8,128)(2,1)S(1)}, u32[]{:S(2)}, u32[]{:S(2)}) %collective-permute-start.1) | collective-permute-done | bytes 491552 | tf_op jit(solution)/shard_map/ppermute | solution.py:437
  18.8 1.5 collective-permute-done.2
  20.3 2.2 %collective-permute-start.3 = (bf16[48,5120]{1,0:T(8,128)(2,1)S(1)}, bf16[48,5120]{1,0:T(8,128)(2,1)S(1)}, u32[]{:S(2)}, u32[]{:S(2)}) collective-permute-start(bf16[48,5120]{1,0:T(8,128)(2,1)S(1)} %collective-permute-done), channel_id=1, source_target_pairs={{4,8},{5,9},{6,10},{7,11},{8,4},{9,5},{10,6},{11,7},{20,24},{21,25... | collective-permute-start | bytes 1474568 | tf_op jit(solution)/shard_map/ppermute | solution.py:437
  22.5 1.6 collective-permute-start.5
  24.1 1.1 pad_maximum_fusion.refs_0_
  25.2 8.5 %collective-permute-done.3 = bf16[48,5120]{1,0:T(8,128)(2,1)S(1)} collective-permute-done((bf16[48,5120]{1,0:T(8,128)(2,1)S(1)}, bf16[48,5120]{1,0:T(8,128)(2,1)S(1)}, u32[]{:S(2)}, u32[]{:S(2)}) %collective-permute-start.3) | collective-permute-done | bytes 491552 | tf_op jit(solution)/shard_map/ppermute | solution.py:437
  34.1 1.2 collective-permute-done.4
  35.5 0.6 collective-permute-start.7
  36.3 0.8 constant_dynamic-update-slice_fusion.1
  37.1 0.8 constant_dynamic-update-slice_fusion.refs_1_
  38.0 8.6 %collective-permute-done.7 = bf16[48,5120]{1,0:T(8,128)(2,1)S(1)} collective-permute-done((bf16[48,5120]{1,0:T(8,128)(2,1)S(1)}, bf16[48,5120]{1,0:T(8,128)(2,1)S(1)}, u32[]{:S(2)}, u32[]{:S(2)}) %collective-permute-start.7) | collective-permute-done | bytes 491552 | tf_op jit(solution)/shard_map/ppermute | solution.py:437
  46.8 1.0 collective-permute-start.8
  47.9 0.6 collective-permute-start.11
  48.4 7.9 %collective-permute-done.8 = bf16[48,5120]{1,0:T(8,128)(2,1)S(1)} collective-permute-done((bf16[48,5120]{1,0:T(8,128)(2,1)S(1)}, bf16[48,5120]{1,0:T(8,128)(2,1)S(1)}, u32[]{:S(2)}, u32[]{:S(2)}) %collective-permute-start.8) | collective-permute-done | bytes 491552 | tf_op jit(solution)/shard_map/ppermute | solution.py:437
  56.9 2.3 %collective-permute-done.12.refs_7_ = bf16[96,5120]{1,0:T(8,128)(2,1)} collective-permute-done((bf16[96,5120]{1,0:T(8,128)(2,1)S(1)}, bf16[96,5120]{1,0:T(8,128)(2,1)}, u32[]{:S(2)}, u32[]{:S(2)}) %collective-permute-start.12) | collective-permute-done | bytes 983072 | tf_op jit(solution)/shard_map/ppermute | solution.py:437
  59.2 3.5 %settle_weights.1 = (bf16[768,3456]{1,0:T(8,128)(2,1)S(1)}, bf16[1536,768]{1,0:T(8,128)(2,1)S(1)}, f32[4,1792]{1,0:T(4,128)S(1)}, f32[1,1792]{1,0:T(1,128)S(1)},...) custom-call(s32[4]{0:T(128)S(1)} %pad_add_fusion.where_ref.which_ref, bf16[96,5120]{1,0:T(8,128)(2,1)S(1)} %pad_maximum_fusion.refs_0_, ...), custom_call_target="tpu_custom_call" | custom-call | tf_op jit(solution)/shard_map/settle_weights/pallas_call | solution.py:566
  62.7 4.5 %layer_forward.3 = (bf16[128,768]{1,0:T(8,128)(2,1)S(1)}, bf16[128,768]{1,0:T(8,128)(2,1)S(1)}, f32[128,3328]{1,0:T(8,128)S(1)}, f32[128,128]{1,0:T(8,128)S(1)},...) custom-call(s32[4]{0:T(128)S(1)} %pad_add_fusion.where_ref.which_ref, ...), custom_call_target="tpu_custom_call" | custom-call | tf_op jit(solution)/shard_map/layer_forward/pallas_call | solution.py:326
  67.2 1.6 collective-permute-start.13
  68.8 5.5 %collective-permute-done.13.refs_1_.refs_9_ = bf16[128,768]{1,0:T(8,128)(2,1)S(1)} collective-permute-done((bf16[128,768]{1,0:T(8,128)(2,1)S(1)}, bf16[128,768]{1,0:T(8,128)(2,1)S(1)}, u32[]{:S(2)}, u32[]{:S(2)}) %collective-permute-start.13) | collective-permute-done | bytes 196640 | tf_op jit(solution)/shard_map/ppermute | solution.py:803
  74.2 4.5 %layer_forward.4 = (bf16[128,768]{1,0:T(8,128)(2,1)S(1)}, bf16[128,768]{1,0:T(8,128)(2,1)S(1)}, f32[128,3328]{1,0:T(8,128)S(1)}, f32[128,128]{1,0:T(8,128)S(1)},...) custom-call(s32[4]{0:T(128)S(1)} %pad_add_fusion.where_ref.which_ref, ...), custom_call_target="tpu_custom_call" | custom-call | tf_op jit(solution)/shard_map/layer_forward/pallas_call | solution.py:326
  78.7 1.6 collective-permute-start.14
  80.3 8.9 %layer_backward.3 = (f32[128,768]{1,0:T(8,128)S(1)}, bf16[128,768]{1,0:T(8,128)(2,1)S(1)}, bf16[128,3328]{1,0:T(8,128)(2,1)S(1)}, bf16[128,128]{1,0:T(8,128)(2,1...) custom-call(s32[4]{0:T(128)S(1)} %pad_add_fusion.where_ref.which_ref, ...), custom_call_target="tpu_custom_call" | custom-call | tf_op jit(solution)/shard_map/layer_backward/pallas_call | solution.py:349
  89.2 0.6 collective-permute-start.15
  89.8 4.5 %layer_forward.5 = (bf16[128,768]{1,0:T(8,128)(2,1)S(1)}, bf16[128,768]{1,0:T(8,128)(2,1)S(1)}, f32[128,3328]{1,0:T(8,128)S(1)}, f32[128,128]{1,0:T(8,128)S(1)},...) custom-call(s32[4]{0:T(128)S(1)} %pad_add_fusion.where_ref.which_ref, ...), custom_call_target="tpu_custom_call" | custom-call | tf_op jit(solution)/shard_map/layer_forward/pallas_call | solution.py:326
  94.3 0.8 collective-permute-done.15.refs_0_.refs_1_
  95.1 8.5 %layer_backward.4 = (f32[128,768]{1,0:T(8,128)S(1)}, bf16[128,768]{1,0:T(8,128)(2,1)S(1)}, bf16[128,3328]{1,0:T(8,128)(2,1)S(1)}, bf16[128,128]{1,0:T(8,128)(2,1...) custom-call(s32[4]{0:T(128)S(1)} %pad_add_fusion.where_ref.which_ref, ...), custom_call_target="tpu_custom_call" | custom-call | tf_op jit(solution)/shard_map/layer_backward/pallas_call | solution.py:349
  103.6 0.8 collective-permute-start.16
  104.5 1.0 turn_rows.1
  105.5 3.9 %collective-permute-done.16.refs_0_.refs_4_ = bf16[128,768]{1,0:T(8,128)(2,1)S(1)} collective-permute-done((bf16[128,768]{1,0:T(8,128)(2,1)S(1)}, bf16[128,768]{1,0:T(8,128)(2,1)S(1)}, u32[]{:S(2)}, u32[]{:S(2)}) %collective-permute-start.16) | collective-permute-done | bytes 196640 | tf_op jit(solution)/shard_map/ppermute | solution.py:820
  109.4 9.1 %layer_backward.5 = (f32[128,768]{1,0:T(8,128)S(1)}, bf16[128,768]{1,0:T(8,128)(2,1)}, bf16[128,3328]{1,0:T(8,128)(2,1)S(1)}, bf16[128,128]{1,0:T(8,128)(2,1)S(1...) custom-call(s32[4]{0:T(128)S(1)} %pad_add_fusion.where_ref.which_ref, ...), custom_call_target="tpu_custom_call" | custom-call | tf_op jit(solution)/shard_map/layer_backward/pallas_call | solution.py:349
  118.5 3.4 %weight_gradients_first.1 = (bf16[48,5120]{1,0:T(8,128)(2,1)S(1)}, bf16[48,5120]{1,0:T(8,128)(2,1)S(1)}, bf16[48,5120]{1,0:T(8,128)(2,1)S(1)}, bf16[48,5120]{1,0...) custom-call(s32[4]{0:T(128)S(1)} %pad_add_fusion.where_ref.which_ref, ...), custom_call_target="tpu_custom_call" | custom-call | tf_op jit(solution)/shard_map/weight_gradients_first/pallas_call | solution.py:682
  122.1 1.9 collective-permute-done.17
  123.9 0.9 add_convert_fusion.2
  124.8 0.6 collective-permute-start.20
  125.9 1.0 copy-done.9
  126.9 3.4 %weight_gradients_rest.1 = (bf16[96,5120]{1,0:T(8,128)(2,1)S(1)}, bf16[96,5120]{1,0:T(8,128)(2,1)S(1)}, bf16[96,5120]{1,0:T(8,128)(2,1)S(1)}, bf16[96,5120]{1,0:...) custom-call(s32[4]{0:T(128)S(1)} %pad_add_fusion.where_ref.which_ref, ...), custom_call_target="tpu_custom_call" | custom-call | tf_op jit(solution)/shard_map/weight_gradients_rest/pallas_call | solution.py:693
  131.0 7.4 %collective-permute-done.20 = bf16[48,5120]{1,0:T(8,128)(2,1)} collective-permute-done((bf16[48,5120]{1,0:T(8,128)(2,1)}, bf16[48,5120]{1,0:T(8,128)(2,1)}, u32[]{:S(2)}, u32[]{:S(2)}) %collective-permute-start.20) | collective-permute-done | bytes 491552 | tf_op jit(solution)/shard_map/ppermute | solution.py:437
  138.4 0.6 collective-permute-start.25
  139.0 1.4 fusion.2
  140.3 0.9 collective-permute-start.24
  141.2 0.8 collective-permute-done.25
  142.3 0.6 collective-permute-start.22
  143.2 9.3 %collective-permute-done.24 = bf16[48,5120]{1,0:T(8,128)(2,1)S(1)} collective-permute-done((bf16[48,5120]{1,0:T(8,128)(2,1)S(1)}, bf16[48,5120]{1,0:T(8,128)(2,1)S(1)}, u32[]{:S(2)}, u32[]{:S(2)}) %collective-permute-start.24) | collective-permute-done | bytes 491552 | tf_op jit(solution)/shard_map/ppermute | solution.py:437
  152.5 1.1 collective-permute-done.22
  153.6 1.0 collective-permute-start.29
  154.7 1.1 collective-permute-start.28
  155.8 1.4 add_convert_fusion.1
  157.2 3.0 %collective-permute-start.27 = (bf16[48,5120]{1,0:T(8,128)(2,1)S(1)}, bf16[48,5120]{1,0:T(8,128)(2,1)S(1)}, u32[]{:S(2)}, u32[]{:S(2)}) collective-permute-start(bf16[48,5120]{1,0:T(8,128)(2,1)S(1)} %add_convert_fusion.1), channel_id=1, source_target_pairs={{4,8},{5,9},{6,10},{7,11},{8,4},{9,5},{10,6},{11,7},{20,24},{21,25... | collective-permute-start | bytes 1474568 | tf_op jit(solution)/shard_map/ppermute | solution.py:437
  160.3 1.1 collective-permute-start.26
  161.7 3.6 %collective-permute-done.28 = bf16[48,5120]{1,0:T(8,128)(2,1)S(1)} collective-permute-done((bf16[48,5120]{1,0:T(8,128)(2,1)S(1)}, bf16[48,5120]{1,0:T(8,128)(2,1)S(1)}, u32[]{:S(2)}, u32[]{:S(2)}) %collective-permute-start.28) | collective-permute-done | bytes 491552 | tf_op jit(solution)/shard_map/ppermute | solution.py:437
  165.4 3.6 %collective-permute-done.27 = bf16[48,5120]{1,0:T(8,128)(2,1)S(1)} collective-permute-done((bf16[48,5120]{1,0:T(8,128)(2,1)S(1)}, bf16[48,5120]{1,0:T(8,128)(2,1)S(1)}, u32[]{:S(2)}, u32[]{:S(2)}) %collective-permute-start.27) | collective-permute-done | bytes 491552 | tf_op jit(solution)/shard_map/ppermute | solution.py:437
  168.9 0.9 collective-permute-done.26
  170.2 2.3 %collective-permute-start.34 = (f32[8,128]{1,0:T(8,128)S(1)}, f32[8,128]{1,0:T(8,128)S(1)}, u32[]{:S(2)}, u32[]{:S(2)}) collective-permute-start(f32[8,128]{1,0:T(8,128)S(1)} %add.78), channel_id=1, source_target_pairs={{0,8},{1,9},{2,10},{3,11},{4,12},{5,13},{6,14},{7,15},{8,0},{9,1},... | collective-permute-start | bytes 12296 | tf_op jit(solution)/shard_map/ppermute | solution.py:494
  172.7 3.0 %collective-permute-start.32 = (bf16[48,5120]{1,0:T(8,128)(2,1)S(1)}, bf16[48,5120]{1,0:T(8,128)(2,1)S(1)}, u32[]{:S(2)}, u32[]{:S(2)}) collective-permute-start(bf16[48,5120]{1,0:T(8,128)(2,1)S(1)} %add_convert_fusion), channel_id=1, source_target_pairs={{4,8},{5,9},{6,10},{7,11},{8,4},{9,5},{10,6},{11,7},{20,24},{21,25... | collective-permute-start | bytes 1474568 | tf_op jit(solution)/shard_map/ppermute | solution.py:437
  175.7 1.5 collective-permute-start.31
  177.4 0.9 maximum_bitcast_fusion
  178.3 0.8 maximum_bitcast_fusion.1
  179.5 0.5 fusion.4
  180.0 4.6 %collective-permute-done.31 = bf16[48,5120]{1,0:T(8,128)(2,1)S(1)} collective-permute-done((bf16[48,5120]{1,0:T(8,128)(2,1)S(1)}, bf16[48,5120]{1,0:T(8,128)(2,1)S(1)}, u32[]{:S(2)}, u32[]{:S(2)}) %collective-permute-start.31) | collective-permute-done | bytes 491552 | tf_op jit(solution)/shard_map/ppermute | solution.py:437
  184.7 1.0 unpack_sums.1
  (93 shorter events, 4.7 us)
Async XLA Ops:
  2.6 13.2 %collective-permute-start = (bf16[48,5120]{1,0:T(8,128)(2,1)}, bf16[48,5120]{1,0:T(8,128)(2,1)S(1)}, u32[]{:S(2)}, u32[]{:S(2)}) collective-permute-start(bf16[48,5120]{1,0:T(8,128)(2,1)} %pack_shard.1), channel_id=1, source_target_pairs={{0,4},{1,5},{2,6},{3,7},{4,0},{5,1},{6,2},{7,3},{8,12},{9,13},{10,... | collective-permute-start | bytes 1474568 | tf_op jit(solution)/shard_map/ppermute | solution.py:437
  2.6 16.2 %collective-permute-start.1 = (bf16[48,5120]{1,0:T(8,128)(2,1)}, bf16[48,5120]{1,0:T(8,128)(2,1)S(1)}, u32[]{:S(2)}, u32[]{:S(2)}) collective-permute-start(bf16[48,5120]{1,0:T(8,128)(2,1)} %pack_shard.1), channel_id=1, source_target_pairs={{4,8},{5,9},{6,10},{7,11},{8,4},{9,5},{10,6},{11,7},{20,24},{21,25... | collective-permute-start | bytes 1474568 | tf_op jit(solution)/shard_map/ppermute | solution.py:437
  7.7 12.7 %collective-permute-start.2 = (bf16[48,5120]{1,0:T(8,128)(2,1)}, bf16[48,5120]{1,0:T(8,128)(2,1)S(1)}, u32[]{:S(2)}, u32[]{:S(2)}) collective-permute-start(bf16[48,5120]{1,0:T(8,128)(2,1)} %pack_shard.1), channel_id=1, source_target_pairs={{0,2},{1,3},{2,0},{3,1},{4,6},{5,7},{6,4},{7,5},{8,10},{9,11},{10,... | collective-permute-start | bytes 1474568 | tf_op jit(solution)/shard_map/ppermute | solution.py:437
  20.3 13.4 %collective-permute-start.3 = (bf16[48,5120]{1,0:T(8,128)(2,1)S(1)}, bf16[48,5120]{1,0:T(8,128)(2,1)S(1)}, u32[]{:S(2)}, u32[]{:S(2)}) collective-permute-start(bf16[48,5120]{1,0:T(8,128)(2,1)S(1)} %collective-permute-done), channel_id=1, source_target_pairs={{4,8},{5,9},{6,10},{7,11},{8,4},{9,5},{10,6},{11,7},{20,24},{21,25... | collective-permute-start | bytes 1474568 | tf_op jit(solution)/shard_map/ppermute | solution.py:437
  22.5 11.6 %collective-permute-start.5 = (bf16[48,5120]{1,0:T(8,128)(2,1)S(1)}, bf16[48,5120]{1,0:T(8,128)(2,1)S(1)}, u32[]{:S(2)}, u32[]{:S(2)}) collective-permute-start(bf16[48,5120]{1,0:T(8,128)(2,1)S(1)} %collective-permute-done), channel_id=1, source_target_pairs={{0,2},{1,3},{2,0},{3,1},{4,6},{5,7},{6,4},{7,5},{8,10},{9,11},{10,... | collective-permute-start | bytes 1474568 | tf_op jit(solution)/shard_map/ppermute | solution.py:437
  24.1 11.2 %collective-permute-start.4 = (bf16[48,5120]{1,0:T(8,128)(2,1)S(1)}, bf16[48,5120]{1,0:T(8,128)(2,1)S(1)}, u32[]{:S(2)}, u32[]{:S(2)}) collective-permute-start(bf16[48,5120]{1,0:T(8,128)(2,1)S(1)} %collective-permute-done.1), channel_id=1, source_target_pairs={{0,4},{1,5},{2,6},{3,7},{4,0},{5,1},{6,2},{7,3},{8,12},{9,13},{10,... | collective-permute-start | bytes 1474568 | tf_op jit(solution)/shard_map/ppermute | solution.py:437
  35.5 11.2 %collective-permute-start.7 = (bf16[48,5120]{1,0:T(8,128)(2,1)S(1)}, bf16[48,5120]{1,0:T(8,128)(2,1)S(1)}, u32[]{:S(2)}, u32[]{:S(2)}) collective-permute-start(bf16[48,5120]{1,0:T(8,128)(2,1)S(1)} %add.67), channel_id=1, source_target_pairs={{0,2},{1,3},{2,0},{3,1},{4,6},{5,7},{6,4},{7,5},{8,10},{9,11},{10,... | collective-permute-start | bytes 1474568 | tf_op jit(solution)/shard_map/ppermute | solution.py:437
  36.0 10.6 %collective-permute-start.6 = (bf16[48,5120]{1,0:T(8,128)(2,1)S(1)}, bf16[48,5120]{1,0:T(8,128)(2,1)S(1)}, u32[]{:S(2)}, u32[]{:S(2)}) collective-permute-start(bf16[48,5120]{1,0:T(8,128)(2,1)S(1)} %collective-permute-done.3), channel_id=1, source_target_pairs={{0,4},{1,5},{2,6},{3,7},{4,0},{5,1},{6,2},{7,3},{8,12},{9,13},{10,... | collective-permute-start | bytes 1474568 | tf_op jit(solution)/shard_map/ppermute | solution.py:437
  37.1 19.7 %collective-permute-start.9 = (bf16[96,5120]{1,0:T(8,128)(2,1)S(1)}, bf16[96,5120]{1,0:T(8,128)(2,1)}, u32[]{:S(2)}, u32[]{:S(2)}) collective-permute-start(bf16[96,5120]{1,0:T(8,128)(2,1)S(1)} %pad_maximum_fusion.refs_0_), channel_id=1, source_target_pairs={{0,1},{1,0},{2,3},{3,2},{4,5},{5,4},{6,7},{7,6},{8,9},{9,8},{10,11... | collective-permute-start | bytes 2949128 | tf_op jit(solution)/shard_map/ppermute | solution.py:437
  46.7 9.8 %copy-start.17 = (f32[1,24]{1,0:T(1,128)S(1)}, f32[1,24]{1,0:T(1,128)}, u32[]{:S(2)}) copy-start(f32[1,24]{1,0:T(1,128)} %param.23) | copy-start | bytes 292
  46.7 10.0 %copy-start.16 = (s32[2,128]{1,0:T(2,128)S(1)}, s32[2,128]{1,0:T(2,128)}, u32[]{:S(2)}) copy-start(s32[2,128]{1,0:T(2,128)} %param.14) | copy-start | bytes 3076
  46.8 10.1 %copy-start.18 = (f32[1,24]{1,0:T(1,128)S(1)}, f32[1,24]{1,0:T(1,128)}, u32[]{:S(2)}) copy-start(f32[1,24]{1,0:T(1,128)} %param.22) | copy-start | bytes 292
  46.8 10.0 %copy-start.19 = (f32[1,24]{1,0:T(1,128)S(1)}, f32[1,24]{1,0:T(1,128)}, u32[]{:S(2)}) copy-start(f32[1,24]{1,0:T(1,128)} %param.21) | copy-start | bytes 292
  46.8 9.6 %collective-permute-start.8 = (bf16[48,5120]{1,0:T(8,128)(2,1)S(1)}, bf16[48,5120]{1,0:T(8,128)(2,1)S(1)}, u32[]{:S(2)}, u32[]{:S(2)}) collective-permute-start(bf16[48,5120]{1,0:T(8,128)(2,1)S(1)} %add.68), channel_id=1, source_target_pairs={{0,2},{1,3},{2,0},{3,1},{4,6},{5,7},{6,4},{7,5},{8,10},{9,11},{10,... | collective-permute-start | bytes 1474568 | tf_op jit(solution)/shard_map/ppermute | solution.py:437
  47.8 9.1 %collective-permute-start.10 = (bf16[96,5120]{1,0:T(8,128)(2,1)}, bf16[96,5120]{1,0:T(8,128)(2,1)}, u32[]{:S(2)}, u32[]{:S(2)}) collective-permute-start(bf16[96,5120]{1,0:T(8,128)(2,1)} %constant_dynamic-update-slice_fusion.refs_1_), channel_id=1, source_target_pairs={{0,1},{1,0},{2,3},{3,2},{4,5},{5,4},{6,7},{7,6},{8,9},{9,8},{10,11... | collective-permute-start | bytes 2949128 | tf_op jit(solution)/shard_map/ppermute | solution.py:437
  47.9 9.0 %collective-permute-start.11 = (bf16[96,5120]{1,0:T(8,128)(2,1)S(1)}, bf16[96,5120]{1,0:T(8,128)(2,1)}, u32[]{:S(2)}, u32[]{:S(2)}) collective-permute-start(bf16[96,5120]{1,0:T(8,128)(2,1)S(1)} %pad_maximum_fusion.1.refs_2_), channel_id=1, source_target_pairs={{0,1},{1,0},{2,3},{3,2},{4,5},{5,4},{6,7},{7,6},{8,9},{9,8},{10,11... | collective-permute-start | bytes 2949128 | tf_op jit(solution)/shard_map/ppermute | solution.py:437
  56.4 2.8 %collective-permute-start.12 = (bf16[96,5120]{1,0:T(8,128)(2,1)S(1)}, bf16[96,5120]{1,0:T(8,128)(2,1)}, u32[]{:S(2)}, u32[]{:S(2)}) collective-permute-start(bf16[96,5120]{1,0:T(8,128)(2,1)S(1)} %pad_maximum_fusion.2.refs_3_), channel_id=1, source_target_pairs={{0,1},{1,0},{2,3},{3,2},{4,5},{5,4},{6,7},{7,6},{8,9},{9,8},{10,11... | collective-permute-start | bytes 2949128 | tf_op jit(solution)/shard_map/ppermute | solution.py:437
  56.8 5.9 %copy-start = (bf16[2,128,768]{2,1,0:T(8,128)(2,1)S(1)}, bf16[2,128,768]{2,1,0:T(8,128)(2,1)}, u32[]{:S(2)}) copy-start(bf16[2,128,768]{2,1,0:T(8,128)(2,1)} %refs_1_.5) | copy-start | bytes 1179652
  67.2 11.5 %copy-start.10 = (bf16[128,768]{1,0:T(8,128)(2,1)}, bf16[128,768]{1,0:T(8,128)(2,1)S(1)}, u32[]{:S(2)}) copy-start(bf16[128,768]{1,0:T(8,128)(2,1)S(1)} %get-tuple-element.218) | copy-start | bytes 589828
  67.2 13.1 %copy-start.1 = (bf16[2,128,768]{2,1,0:T(8,128)(2,1)S(1)}, bf16[2,128,768]{2,1,0:T(8,128)(2,1)}, u32[]{:S(2)}) copy-start(bf16[2,128,768]{2,1,0:T(8,128)(2,1)} %refs_8_.3) | copy-start | bytes 1179652
  67.2 7.0 %collective-permute-start.13 = (bf16[128,768]{1,0:T(8,128)(2,1)S(1)}, bf16[128,768]{1,0:T(8,128)(2,1)S(1)}, u32[]{:S(2)}, u32[]{:S(2)}) collective-permute-start(bf16[128,768]{1,0:T(8,128)(2,1)S(1)} %get-tuple-element.218), channel_id=1, source_target_pairs={{0,16},{16,0},{1,17},{17,1},{2,18},{18,2},{3,19},{19,3},{4,20},{20... | collective-permute-start | bytes 589832 | tf_op jit(solution)/shard_map/ppermute | solution.py:803
  78.7 10.5 %copy-start.12 = (bf16[128,768]{1,0:T(8,128)(2,1)}, bf16[128,768]{1,0:T(8,128)(2,1)S(1)}, u32[]{:S(2)}) copy-start(bf16[128,768]{1,0:T(8,128)(2,1)S(1)} %get-tuple-element.219) | copy-start | bytes 589828
  78.7 11.1 %collective-permute-start.14 = (bf16[128,768]{1,0:T(8,128)(2,1)S(1)}, bf16[128,768]{1,0:T(8,128)(2,1)S(1)}, u32[]{:S(2)}, u32[]{:S(2)}) collective-permute-start(bf16[128,768]{1,0:T(8,128)(2,1)S(1)} %get-tuple-element.219), channel_id=1, source_target_pairs={{0,16},{16,0},{1,17},{17,1},{2,18},{18,2},{3,19},{19,3},{4,20},{20... | collective-permute-start | bytes 589832 | tf_op jit(solution)/shard_map/ppermute | solution.py:805
  89.2 5.1 %copy-start.2 = (f32[128,768]{1,0:T(8,128)}, f32[128,768]{1,0:T(8,128)S(1)}, u32[]{:S(2)}) copy-start(f32[128,768]{1,0:T(8,128)S(1)} %get-tuple-element.222) | copy-start | bytes 1179652
  89.2 5.9 %collective-permute-start.15 = (bf16[128,768]{1,0:T(8,128)(2,1)S(1)}, bf16[128,768]{1,0:T(8,128)(2,1)S(1)}, u32[]{:S(2)}, u32[]{:S(2)}) collective-permute-start(bf16[128,768]{1,0:T(8,128)(2,1)S(1)} %get-tuple-element.151), channel_id=1, source_target_pairs={{0,16},{16,0},{1,17},{17,1},{2,18},{18,2},{3,19},{19,3},{4,20},{20... | collective-permute-start | bytes 589832 | tf_op jit(solution)/shard_map/ppermute | solution.py:814
  94.3 9.3 %copy-start.14 = (bf16[128,768]{1,0:T(8,128)(2,1)}, bf16[128,768]{1,0:T(8,128)(2,1)S(1)}, u32[]{:S(2)}) copy-start(bf16[128,768]{1,0:T(8,128)(2,1)S(1)} %get-tuple-element.220) | copy-start | bytes 589828
  103.6 14.9 %copy-start.4 = (f32[128,768]{1,0:T(8,128)}, f32[128,768]{1,0:T(8,128)S(1)}, u32[]{:S(2)}) copy-start(f32[128,768]{1,0:T(8,128)S(1)} %get-tuple-element.221) | copy-start | bytes 1179652
  103.6 5.7 %collective-permute-start.16 = (bf16[128,768]{1,0:T(8,128)(2,1)S(1)}, bf16[128,768]{1,0:T(8,128)(2,1)S(1)}, u32[]{:S(2)}, u32[]{:S(2)}) collective-permute-start(bf16[128,768]{1,0:T(8,128)(2,1)S(1)} %get-tuple-element.165), channel_id=1, source_target_pairs={{0,16},{16,0},{1,17},{17,1},{2,18},{18,2},{3,19},{19,3},{4,20},{20... | collective-permute-start | bytes 589832 | tf_op jit(solution)/shard_map/ppermute | solution.py:820
  118.5 3.5 %copy-start.6 = (f32[128,768]{1,0:T(8,128)}, f32[128,768]{1,0:T(8,128)S(1)}, u32[]{:S(2)}) copy-start(f32[128,768]{1,0:T(8,128)S(1)} %get-tuple-element.223) | copy-start | bytes 1179652
  122.0 2.8 %copy-start.8 = (bf16[256,768]{1,0:T(8,128)(2,1)}, bf16[256,768]{1,0:T(8,128)(2,1)S(1)}, u32[]{:S(2)}) copy-start(bf16[256,768]{1,0:T(8,128)(2,1)S(1)} %get-tuple-element.198.gb_ref) | copy-start | bytes 1179652
  122.0 1.9 %collective-permute-start.17 = (bf16[48,5120]{1,0:T(8,128)(2,1)S(1)}, bf16[48,5120]{1,0:T(8,128)(2,1)S(1)}, u32[]{:S(2)}, u32[]{:S(2)}) collective-permute-start(bf16[48,5120]{1,0:T(8,128)(2,1)S(1)} %get-tuple-element.196), channel_id=1, source_target_pairs={{0,1},{1,0},{2,3},{3,2},{4,5},{5,4},{6,7},{7,6},{8,9},{9,8},{10,11... | collective-permute-start | bytes 1474568 | tf_op jit(solution)/shard_map/ppermute | solution.py:437
  124.8 13.6 %collective-permute-start.20 = (bf16[48,5120]{1,0:T(8,128)(2,1)}, bf16[48,5120]{1,0:T(8,128)(2,1)}, u32[]{:S(2)}, u32[]{:S(2)}) collective-permute-start(bf16[48,5120]{1,0:T(8,128)(2,1)} %add_convert_fusion.2), channel_id=1, source_target_pairs={{0,2},{1,3},{2,0},{3,1},{4,6},{5,7},{6,4},{7,5},{8,10},{9,11},{10,... | collective-permute-start | bytes 1474568 | tf_op jit(solution)/shard_map/ppermute | solution.py:437
  125.4 13.6 %collective-permute-start.23 = (bf16[48,5120]{1,0:T(8,128)(2,1)}, bf16[48,5120]{1,0:T(8,128)(2,1)}, u32[]{:S(2)}, u32[]{:S(2)}) collective-permute-start(bf16[48,5120]{1,0:T(8,128)(2,1)} %get-tuple-element.211), channel_id=1, source_target_pairs={{0,1},{1,0},{2,3},{3,2},{4,5},{5,4},{6,7},{7,6},{8,9},{9,8},{10,11... | collective-permute-start | bytes 1474568 | tf_op jit(solution)/shard_map/ppermute | solution.py:437
  125.4 5.5 %collective-permute-start.21 = (f32[8,128]{1,0:T(8,128)S(1)}, f32[8,128]{1,0:T(8,128)S(1)}, u32[]{:S(2)}, u32[]{:S(2)}) collective-permute-start(f32[8,128]{1,0:T(8,128)S(1)} %get-tuple-element.206), channel_id=1, source_target_pairs={{0,1},{1,0},{2,3},{3,2},{4,5},{5,4},{6,7},{7,6},{8,9},{9,8},{10,11... | collective-permute-start | bytes 12296 | tf_op jit(solution)/shard_map/ppermute | solution.py:494
  125.9 1.0 copy-start.9
  130.3 11.7 %collective-permute-start.19 = (bf16[96,5120]{1,0:T(8,128)(2,1)S(1)}, bf16[96,5120]{1,0:T(8,128)(2,1)S(1)}, u32[]{:S(2)}, u32[]{:S(2)}) collective-permute-start(bf16[96,5120]{1,0:T(8,128)(2,1)S(1)} %get-tuple-element.204), channel_id=1, source_target_pairs={{0,1},{1,0},{2,3},{3,2},{4,5},{5,4},{6,7},{7,6},{8,9},{9,8},{10,11... | collective-permute-start | bytes 2949128 | tf_op jit(solution)/shard_map/ppermute | solution.py:437
  130.4 12.5 %collective-permute-start.18 = (bf16[96,5120]{1,0:T(8,128)(2,1)S(1)}, bf16[96,5120]{1,0:T(8,128)(2,1)S(1)}, u32[]{:S(2)}, u32[]{:S(2)}) collective-permute-start(bf16[96,5120]{1,0:T(8,128)(2,1)S(1)} %get-tuple-element.202), channel_id=1, source_target_pairs={{0,1},{1,0},{2,3},{3,2},{4,5},{5,4},{6,7},{7,6},{8,9},{9,8},{10,11... | collective-permute-start | bytes 2949128 | tf_op jit(solution)/shard_map/ppermute | solution.py:437
  130.9 30.5 %collective-permute-start.30 = (bf16[96,5120]{1,0:T(8,128)(2,1)S(1)}, bf16[96,5120]{1,0:T(8,128)(2,1)S(1)}, u32[]{:S(2)}, u32[]{:S(2)}) collective-permute-start(bf16[96,5120]{1,0:T(8,128)(2,1)S(1)} %get-tuple-element.225), channel_id=1, source_target_pairs={{0,1},{1,0},{2,3},{3,2},{4,5},{5,4},{6,7},{7,6},{8,9},{9,8},{10,11... | collective-permute-start | bytes 2949128 | tf_op jit(solution)/shard_map/ppermute | solution.py:437
  138.4 3.6 %collective-permute-start.25 = (f32[8,128]{1,0:T(8,128)S(1)}, f32[8,128]{1,0:T(8,128)S(1)}, u32[]{:S(2)}, u32[]{:S(2)}) collective-permute-start(f32[8,128]{1,0:T(8,128)S(1)} %add.72), channel_id=1, source_target_pairs={{0,2},{1,3},{2,0},{3,1},{4,6},{5,7},{6,4},{7,5},{8,10},{9,11},{10,... | collective-permute-start | bytes 12296 | tf_op jit(solution)/shard_map/ppermute | solution.py:494
  140.3 12.2 %collective-permute-start.24 = (bf16[48,5120]{1,0:T(8,128)(2,1)S(1)}, bf16[48,5120]{1,0:T(8,128)(2,1)S(1)}, u32[]{:S(2)}, u32[]{:S(2)}) collective-permute-start(bf16[48,5120]{1,0:T(8,128)(2,1)S(1)} %fusion.2), channel_id=1, source_target_pairs={{0,4},{1,5},{2,6},{3,7},{4,0},{5,1},{6,2},{7,3},{8,12},{9,13},{10,... | collective-permute-start | bytes 1474568 | tf_op jit(solution)/shard_map/ppermute | solution.py:437
  142.3 11.4 %collective-permute-start.22 = (bf16[48,5120]{1,0:T(8,128)(2,1)S(1)}, bf16[48,5120]{1,0:T(8,128)(2,1)S(1)}, u32[]{:S(2)}, u32[]{:S(2)}) collective-permute-start(bf16[48,5120]{1,0:T(8,128)(2,1)S(1)} %slice.74), channel_id=1, source_target_pairs={{0,2},{1,3},{2,0},{3,1},{4,6},{5,7},{6,4},{7,5},{8,10},{9,11},{10,... | collective-permute-start | bytes 1474568 | tf_op jit(solution)/shard_map/ppermute | solution.py:437
  153.6 8.0 %collective-permute-start.29 = (f32[8,128]{1,0:T(8,128)S(1)}, f32[8,128]{1,0:T(8,128)S(1)}, u32[]{:S(2)}, u32[]{:S(2)}) collective-permute-start(f32[8,128]{1,0:T(8,128)S(1)} %add.75), channel_id=1, source_target_pairs={{0,4},{1,5},{2,6},{3,7},{4,0},{5,1},{6,2},{7,3},{8,12},{9,13},{10,... | collective-permute-start | bytes 12296 | tf_op jit(solution)/shard_map/ppermute | solution.py:494
  154.7 10.6 %collective-permute-start.28 = (bf16[48,5120]{1,0:T(8,128)(2,1)S(1)}, bf16[48,5120]{1,0:T(8,128)(2,1)S(1)}, u32[]{:S(2)}, u32[]{:S(2)}) collective-permute-start(bf16[48,5120]{1,0:T(8,128)(2,1)S(1)} %fusion.3), channel_id=1, source_target_pairs={{0,4},{1,5},{2,6},{3,7},{4,0},{5,1},{6,2},{7,3},{8,12},{9,13},{10,... | collective-permute-start | bytes 1474568 | tf_op jit(solution)/shard_map/ppermute | solution.py:437
  157.2 11.7 %collective-permute-start.27 = (bf16[48,5120]{1,0:T(8,128)(2,1)S(1)}, bf16[48,5120]{1,0:T(8,128)(2,1)S(1)}, u32[]{:S(2)}, u32[]{:S(2)}) collective-permute-start(bf16[48,5120]{1,0:T(8,128)(2,1)S(1)} %add_convert_fusion.1), channel_id=1, source_target_pairs={{4,8},{5,9},{6,10},{7,11},{8,4},{9,5},{10,6},{11,7},{20,24},{21,25... | collective-permute-start | bytes 1474568 | tf_op jit(solution)/shard_map/ppermute | solution.py:437
  160.3 9.6 %collective-permute-start.26 = (bf16[48,5120]{1,0:T(8,128)(2,1)S(1)}, bf16[48,5120]{1,0:T(8,128)(2,1)S(1)}, u32[]{:S(2)}, u32[]{:S(2)}) collective-permute-start(bf16[48,5120]{1,0:T(8,128)(2,1)S(1)} %slice.75), channel_id=1, source_target_pairs={{0,2},{1,3},{2,0},{3,1},{4,6},{5,7},{6,4},{7,5},{8,10},{9,11},{10,... | collective-permute-start | bytes 1474568 | tf_op jit(solution)/shard_map/ppermute | solution.py:437
  161.7 15.5 %copy-start.3 = (f32[128,768]{1,0:T(8,128)S(1)}, f32[128,768]{1,0:T(8,128)}, u32[]{:S(2)}) copy-start(f32[128,768]{1,0:T(8,128)} %copy-done.2) | copy-start | bytes 1179652
  161.7 15.5 %copy-start.5 = (f32[128,768]{1,0:T(8,128)S(1)}, f32[128,768]{1,0:T(8,128)}, u32[]{:S(2)}) copy-start(f32[128,768]{1,0:T(8,128)} %copy-done.4) | copy-start | bytes 1179652
  161.7 15.5 %copy-start.7 = (f32[128,768]{1,0:T(8,128)S(1)}, f32[128,768]{1,0:T(8,128)}, u32[]{:S(2)}) copy-start(f32[128,768]{1,0:T(8,128)} %copy-done.6) | copy-start | bytes 1179652
  170.1 7.2 %copy-start.11 = (bf16[128,768]{1,0:T(8,128)(2,1)S(1)}, bf16[128,768]{1,0:T(8,128)(2,1)}, u32[]{:S(2)}) copy-start(bf16[128,768]{1,0:T(8,128)(2,1)} %copy-done.10) | copy-start | bytes 589828
  170.1 7.2 %copy-start.13 = (bf16[128,768]{1,0:T(8,128)(2,1)S(1)}, bf16[128,768]{1,0:T(8,128)(2,1)}, u32[]{:S(2)}) copy-start(bf16[128,768]{1,0:T(8,128)(2,1)} %copy-done.12) | copy-start | bytes 589828
  170.1 7.2 %copy-start.15 = (bf16[128,768]{1,0:T(8,128)(2,1)S(1)}, bf16[128,768]{1,0:T(8,128)(2,1)}, u32[]{:S(2)}) copy-start(bf16[128,768]{1,0:T(8,128)(2,1)} %copy-done.14) | copy-start | bytes 589828
  170.1 14.6 %collective-permute-start.33 = (bf16[48,5120]{1,0:T(8,128)(2,1)S(1)}, bf16[48,5120]{1,0:T(8,128)(2,1)S(1)}, u32[]{:S(2)}, u32[]{:S(2)}) collective-permute-start(bf16[48,5120]{1,0:T(8,128)(2,1)S(1)} %fusion.1), channel_id=1, source_target_pairs={{0,4},{1,5},{2,6},{3,7},{4,0},{5,1},{6,2},{7,3},{8,12},{9,13},{10,... | collective-permute-start | bytes 1474568 | tf_op jit(solution)/shard_map/ppermute | solution.py:437
  170.2 9.3 %collective-permute-start.34 = (f32[8,128]{1,0:T(8,128)S(1)}, f32[8,128]{1,0:T(8,128)S(1)}, u32[]{:S(2)}, u32[]{:S(2)}) collective-permute-start(f32[8,128]{1,0:T(8,128)S(1)} %add.78), channel_id=1, source_target_pairs={{0,8},{1,9},{2,10},{3,11},{4,12},{5,13},{6,14},{7,15},{8,0},{9,1},... | collective-permute-start | bytes 12296 | tf_op jit(solution)/shard_map/ppermute | solution.py:494
  172.7 12.0 %collective-permute-start.32 = (bf16[48,5120]{1,0:T(8,128)(2,1)S(1)}, bf16[48,5120]{1,0:T(8,128)(2,1)S(1)}, u32[]{:S(2)}, u32[]{:S(2)}) collective-permute-start(bf16[48,5120]{1,0:T(8,128)(2,1)S(1)} %add_convert_fusion), channel_id=1, source_target_pairs={{4,8},{5,9},{6,10},{7,11},{8,4},{9,5},{10,6},{11,7},{20,24},{21,25... | collective-permute-start | bytes 1474568 | tf_op jit(solution)/shard_map/ppermute | solution.py:437
  175.7 8.9 %collective-permute-start.31 = (bf16[48,5120]{1,0:T(8,128)(2,1)S(1)}, bf16[48,5120]{1,0:T(8,128)(2,1)S(1)}, u32[]{:S(2)}, u32[]{:S(2)}) collective-permute-start(bf16[48,5120]{1,0:T(8,128)(2,1)S(1)} %slice.73), channel_id=1, source_target_pairs={{0,2},{1,3},{2,0},{3,1},{4,6},{5,7},{6,4},{7,5},{8,10},{9,11},{10,... | collective-permute-start | bytes 1474568 | tf_op jit(solution)/shard_map/ppermute | solution.py:437
